TPU v7x, 32 devices: a whole 2x2x4 slice. The times are simulated.
32 devices in a mesh: gz: 4 (over x, core), row: 4 (over z), col: 2 (over y).
Axes of the slice: x: 2, y: 2, z: 4, core: 2. Of those that a mesh axis runs over, the one named last changes fastest.
Arguments:
- leaf_rhs: float32 [64, 256, 512], P(('gz', 'col')), may hold values from -6 to 6
- leaf_inv: bfloat16 [64, 512, 512], P(('gz', 'col'), 'row'), as said below
- leaf_lower_mid: bfloat16 [64, 512, 512], P(('gz', 'col'), None, 'row'), may hold values from -0.09375 to 0.09375
- leaf_lower_coupling: bfloat16 [64, 3, 512, 512], P(('gz', 'col'), None, None, 'row'), may hold values from -0.046875 to 0.046875
- leaf_parent: int32 [64], P(('gz', 'col')), may hold values from 0 to 1
- leaf_pattern: int32 [64, 3], P(('gz', 'col')), may hold values 0 or 1
- mid_rhs: float32 [8, 256, 512], P(('gz', 'col')), may hold values from -6 to 6
- parent_diagonal_inverse: bfloat16 [8, 512, 512], P(('gz', 'col'), 'row'), as said below
- mid_lower: bfloat16 [8, 3, 512, 512], P(('gz', 'col'), None, None, 'row'), may hold values from -0.125 to 0.125
- mid_pattern: int32 [8, 2], P(('gz', 'col')), may hold values 0 or 1
- top_rhs: float32 [4, 256, 512], P('gz'), may hold values from -6 to 6
- top_inv: bfloat16 [4, 512, 512], P('gz', 'row'), as said below
- top_lower: bfloat16 [4, 2, 512, 512], P('gz', None, None, 'row'), may hold values from -0.1875 to 0.1875
- apex_rhs: float32 [3, 256, 512], replicated, may hold values from -6 to 6
- apex_inv: bfloat16 [3, 512, 512], P(None, 'row'), as said below
- apex_lower: bfloat16 [2, 512, 512], P(None, None, 'row'), may hold values from -0.25 to 0.25
Outputs:
- leaf_solution: float32 [64, 256, 512], P(('gz', 'col'), None, 'row')
- mid_solution: float32 [8, 256, 512], P(('gz', 'col'), None, 'row')
- top_solution: float32 [4, 256, 512], P('gz', None, 'row')
- apex_solution: float32 [3, 256, 512], P(None, 'gz', 'row')
Inputs may be any that keep to these rules, and one draw needn't show every extreme that they name: `leaf_inv`: each diagonal-block inverse is lower triangular with a unit diagonal. `parent_diagonal_inverse`: lower triangular with a unit diagonal. `top_inv`: lower triangular with a unit diagonal. `apex_inv`: lower triangular with a unit diagonal.
All inputs are finite; a program needn't handle non-finite values. No bound on the sum of `leaf_pattern` or of `mid_pattern` on one device may be relied on, other than what follows from the above.
Results may differ from a plain program's by a relative error of at most 0.015.
Values may be sent and summed in bfloat16 or wider, within the bound.
No kernel may reach another device: no remote copies, remote signals or barrier semaphores. Data moves between devices by JAX's collectives and lax.ppermute only.
A program may use at most 128 MiB of HBM per device.

v0:
```python
import jax
import jax.numpy as jnp
from jax import lax
from jax.sharding import PartitionSpec as P


def from_partner(block, axis, apart):
    count = lax.axis_size(axis)
    route = []
    for low in range(count):
        high = low | 1 << apart
        if high != low and high < count:
            route += [(low, high), (high, low)]
    return lax.ppermute(block, axis, route)


def per_device(
    leaf_rhs,
    leaf_inv,
    leaf_lower_mid,
    leaf_lower_coupling,
    leaf_parent,
    leaf_pattern,
    mid_rhs,
    parent_diagonal_inverse,
    mid_lower,
    mid_pattern,
    top_rhs,
    top_inv,
    top_lower,
    apex_rhs,
    apex_inv,
    apex_lower,
):
    col_count = lax.axis_size("col")
    leaf_solved = jnp.einsum(
        "lrb,lcb->lrc", leaf_rhs.astype(jnp.bfloat16), leaf_inv, preferred_element_type=jnp.float32
    )
    leaf_round = leaf_solved.astype(jnp.bfloat16)
    toward_parent = jnp.einsum(
        "lrc,lac->lra", leaf_round, leaf_lower_mid, preferred_element_type=jnp.float32
    )
    to_up = jnp.einsum(
        "lrc,lkac->lkra", leaf_round, leaf_lower_coupling, preferred_element_type=jnp.float32
    )
    up_weight = leaf_pattern.astype(jnp.float32)
    layer_up = jnp.einsum("lk,lkra->kra", up_weight, to_up, precision=lax.Precision.HIGHEST)
    parent_ids = lax.broadcasted_iota(jnp.int32, (leaf_parent.shape[0], col_count), 1)
    onehot = (leaf_parent[:, None] == parent_ids).astype(jnp.float32)
    mid_terms = jnp.einsum("lm,lra->mra", onehot, toward_parent, precision=lax.Precision.HIGHEST)
    summed = lax.psum_scatter(mid_terms, "col", scatter_dimension=0, tiled=True)
    summed = lax.psum(summed, "row")
    parent_prepared = (mid_rhs - summed).astype(jnp.bfloat16)
    parent_unknowns = jnp.einsum(
        "atg,adg->atd", parent_prepared, parent_diagonal_inverse, preferred_element_type=jnp.float32
    )
    mid_round = parent_unknowns.astype(jnp.bfloat16)
    mid_up = jnp.einsum(
        "rc,kac->kra", mid_round[0], mid_lower[0], preferred_element_type=jnp.float32
    )
    mid_weight = jnp.concatenate([jnp.ones((1,), jnp.float32), mid_pattern[0].astype(jnp.float32)])
    layer_part = layer_up + mid_weight[:, None, None] * mid_up
    layer_full = lax.psum(layer_part, ("row", "col"))
    top_ready = (top_rhs[0] - layer_full[0]).astype(jnp.bfloat16)
    top_solved = jnp.einsum("rb,cb->rc", top_ready, top_inv[0], preferred_element_type=jnp.float32)
    top_round = top_solved.astype(jnp.bfloat16)
    top_up = jnp.einsum("rc,kac->kra", top_round, top_lower[0], preferred_element_type=jnp.float32)
    first_row = (lax.axis_index("row") == 0).astype(jnp.float32)
    carried = top_up + first_row * layer_full[1:]
    pair_index = lax.axis_index("gz") // 2
    paired = carried + from_partner(carried.astype(jnp.bfloat16), "gz", 0).astype(carried.dtype)
    paired = lax.psum(paired, "row")
    front_rhs = lax.dynamic_index_in_dim(apex_rhs, pair_index, 0, keepdims=False)
    front_inv = lax.dynamic_index_in_dim(apex_inv, pair_index, 0, keepdims=False)
    front_lower = lax.dynamic_index_in_dim(apex_lower, pair_index, 0, keepdims=False)
    local_unknowns = jnp.einsum(
        "rb,cb->rc",
        (front_rhs - paired[0]).astype(jnp.bfloat16),
        front_inv,
        preferred_element_type=jnp.float32,
    )
    own_up = jnp.einsum(
        "rc,ac->ra",
        local_unknowns.astype(jnp.bfloat16),
        front_lower,
        preferred_element_type=jnp.float32,
    )
    pair_last = paired[1] + lax.psum(own_up.astype(jnp.bfloat16), "row").astype(jnp.float32)
    other_last, other_solved = (
        from_partner(pair_last.astype(jnp.bfloat16), "gz", 1).astype(pair_last.dtype),
        from_partner(local_unknowns.astype(jnp.bfloat16), "gz", 1).astype(local_unknowns.dtype),
    )
    last_sum = pair_last + other_last
    leading = pair_index == 0
    front_solved = jnp.stack(
        [
            jnp.where(leading, local_unknowns, other_solved),
            jnp.where(leading, other_solved, local_unknowns),
        ]
    )
    last_solved = jnp.einsum(
        "rb,cb->rc",
        (apex_rhs[2] - last_sum).astype(jnp.bfloat16),
        apex_inv[2],
        preferred_element_type=jnp.float32,
    )
    apex_unknowns = jnp.concatenate([front_solved, last_solved[None]], axis=0)
    quarter = apex_unknowns.shape[1] // lax.axis_size("gz")
    apex_part = lax.dynamic_slice_in_dim(apex_unknowns, lax.axis_index("gz") * quarter, quarter, 1)
    return (leaf_solved, parent_unknowns, top_solved[None], apex_part)


def solution(mesh):
    placed = (
        P(("gz", "col"), None, None),
        P(("gz", "col"), "row", None),
        P(("gz", "col"), None, "row"),
        P(("gz", "col"), None, None, "row"),
        P(("gz", "col")),
        P(("gz", "col"), None),
        P(("gz", "col"), None, None),
        P(("gz", "col"), "row", None),
        P(("gz", "col"), None, None, "row"),
        P(("gz", "col"), None),
        P("gz", None, None),
        P("gz", "row", None),
        P("gz", None, None, "row"),
        P(),
        P(None, "row", None),
        P(None, None, "row"),
    )
    return jax.shard_map(
        per_device,
        mesh=mesh,
        in_specs=placed,
        out_specs=(
            P(("gz", "col"), None, "row"),
            P(("gz", "col"), None, "row"),
            P("gz", None, "row"),
            P(None, "gz", "row"),
        ),
        check_vma=False,
    )
```

profile of v0, /device:TPU:0, one launch (start us, length us, event | category | flops | bytes accessed | tf_op | source)
XLA Modules:
  0.0 288.6 jit_solution(6090779050180414616)
XLA Ops:
  7.2 3.3 %fusion.4 = f32[8,256,128]{2,1,0:T(8,128)S(1)} fusion(bf16[8,128,512]{2,1,0:T(8,128)(2,1)} %param.17, f32[8,256,512]{2,1,0:T(8,128)} %param.16), kind=kOutput, calls=%fused_computation.5 | convolution fusion | flops 269484032 | bytes 6291456 | tf_op jit(solution)/shard_map/lrb,lcb->lrc/dot_general | solution.py:36
  11.6 4.3 %fusion.2 = f32[2,256,512]{2,0,1:T(2,128)S(1)} fusion(f32[8,256,512]{2,1,0:T(8,128)S(1)} %fusion.26, s32[8]{0:T(128)S(1)} %copy-done.9), kind=kOutput, calls=%fused_computation.3 | convolution fusion | flops 25165840 | bytes 5242912 | tf_op jit(solution)/shard_map/lm,lra->mra/dot_general | solution.py:50
  15.9 1.2 copy.23
  17.3 7.5 %convolution_bitcast_fusion = f32[8,3,256,512]{3,2,1,0:T(8,128)} fusion(bf16[8,3,512,128]{3,2,1,0:T(8,128)(2,1)S(1)} %copy-done, f32[8,256,128]{2,1,0:T(8,128)} %copy-done.1), kind=kOutput, calls=%fused_computation.2 | convolution fusion | flops 805568512 | bytes 16777216 | tf_op jit(solution)/shard_map/lrc,lkac->lkra/dot_general | solution.py:43
  24.9 15.5 %reduce-scatter.2.cloned.1.call-done = f32[1,256,512]{2,1,0:T(8,128)} async-done(((f32[2,256,512]{2,1,0:T(8,128)}), f32[1,256,512]{2,1,0:T(8,128)}) %reduce-scatter.2.cloned.1.call-update) | async-done | bytes 524304 | tf_op jit(solution)/shard_map/reduce_scatter | solution.py:51
  40.6 22.7 %fusion = f32[3,1,256,512]{3,1,2,0:T(1,128)} fusion(f32[8,3,256,512]{3,2,1,0:T(8,128)} %convolution_bitcast_fusion, f32[8,3,1,1]{0,1,2,3:T(4,128)S(1)} %convert_bitcast_fusion), kind=kOutput, calls=%fused_computation | convolution fusion | flops 37748736 | bytes 14155872 | tf_op jit(solution)/shard_map/lk,lkra->kra/dot_general | solution.py:47
  63.3 17.8 %all-reduce.5.cloned.1.call-done = f32[1,256,512]{2,1,0:T(8,128)} async-done(((f32[1,256,512]{2,1,0:T(8,128)}), f32[1,256,512]{2,1,0:T(8,128)}) %all-reduce.5.cloned.1.call-update) | async-done | bytes 524304 | tf_op jit(solution)/shard_map/psum | solution.py:52
  81.1 1.4 fusion.15
  82.6 3.1 %bitcast_add_fusion = f32[3,256,512]{2,1,0:T(8,128)} fusion(f32[3,1,256,512]{3,1,2,0:T(1,128)} %fusion, f32[3]{0:T(128)S(1)} %pad_maximum_fusion, bf16[1,3,512,128]{3,2,1,0:T(8,128)(2,1)} %param.24, f32[256,128]{1,0:T(8,128)S(1)} %fusion.15), kind=kOutput, calls=%fused_computation.7 | convolution fusion | flops 101482496 | bytes 3670028 | tf_op jit(solution)/shard_map/rc,kac->kra/dot_general | solution.py:58
  85.8 88.9 %all-reduce.7.cloned.1.call-done = f32[3,256,512]{2,1,0:T(8,128)} async-done(((f32[3,256,512]{2,1,0:T(8,128)}), f32[3,256,512]{2,1,0:T(8,128)}) %all-reduce.7.cloned.1.call-update) | async-done | bytes 1572880 | tf_op jit(solution)/shard_map/psum | solution.py:63
  174.7 1.4 fusion.19
  176.2 1.6 fusion.51
  177.9 1.9 collective-permute-done
  179.7 1.2 convert_add_fusion
  181.0 51.3 %all-reduce.9.cloned.1.call-done = f32[2,256,512]{2,1,0:T(8,128)} async-done(((f32[2,256,512]{2,1,0:T(8,128)}), f32[2,256,512]{2,1,0:T(8,128)}) %all-reduce.9.cloned.1.call-update) | async-done | bytes 1048592 | tf_op jit(solution)/shard_map/psum | solution.py:72
  232.3 2.1 fusion.52
  234.4 1.8 convolution_convert_fusion
  236.2 1.5 collective-permute-start.1
  237.7 33.3 %all-reduce.11.cloned.1.call-done = bf16[256,512]{1,0:T(8,128)(2,1)} async-done(((bf16[256,512]{1,0:T(8,128)(2,1)}), bf16[256,512]{1,0:T(8,128)(2,1)}) %all-reduce.11.cloned.1.call-update) | async-done | bytes 262160 | tf_op jit(solution)/shard_map/psum | solution.py:88
  271.1 1.9 fusion.13
  273.0 1.5 collective-permute-start.2
  274.4 0.9 fusion.29
  275.3 4.5 %collective-permute-done.2 = bf16[256,512]{1,0:T(8,128)(2,1)S(1)} collective-permute-done((bf16[256,512]{1,0:T(8,128)(2,1)}, bf16[256,512]{1,0:T(8,128)(2,1)S(1)}, u32[]{:S(2)}, u32[]{:S(2)}) %collective-permute-start.2) | collective-permute-done | bytes 262176 | tf_op jit(solution)/shard_map/ppermute | solution.py:14
  279.8 1.5 convolution_bitcast_fusion.2
  (39 shorter events, 2.3 us)
Async XLA Ops:
  7.2 10.2 %copy-start = (bf16[8,3,512,128]{3,2,1,0:T(8,128)(2,1)S(1)}, bf16[8,3,512,128]{3,2,1,0:T(8,128)(2,1)}, u32[]{:S(2)}) copy-start(bf16[8,3,512,128]{3,2,1,0:T(8,128)(2,1)} %param.19) | copy-start | bytes 9437188
  7.2 33.2 %reduce-scatter.2.cloned.1.call-start = ((), (), s32[]{:S(2)}) async-start(), calls=%async_computation.1 | async-start | bytes 1572864 | tf_op jit(solution)/shard_map/reduce_scatter | solution.py:51
  7.2 3.4 %copy-start.2 = (bf16[8,512,128]{2,1,0:T(8,128)(2,1)S(1)}, bf16[8,512,128]{2,1,0:T(8,128)(2,1)}, u32[]{:S(2)}) copy-start(bf16[8,512,128]{2,1,0:T(8,128)(2,1)} %param.18) | copy-start | bytes 3145732
  10.6 1.0 copy-start.1
  10.6 1.0 copy-start.9
  15.9 1.3 copy-start.10
  15.9 1.4 copy-start.8
  17.2 63.9 %all-reduce.5.cloned.1.call-start = ((), (), s32[]{:S(2)}) async-start(), calls=%async_computation.2 | async-start | bytes 1048576 | tf_op jit(solution)/shard_map/psum | solution.py:52
  40.4 40.7 %copy-start.6 = (bf16[1,128,512]{2,1,0:T(8,128)(2,1)S(1)}, bf16[1,128,512]{2,1,0:T(8,128)(2,1)}, u32[]{:S(2)}) copy-start(bf16[1,128,512]{2,1,0:T(8,128)(2,1)} %param.23) | copy-start | bytes 393220
  40.4 134.3 %all-reduce.7.cloned.1.call-start = ((), (), s32[]{:S(2)}) async-start(), calls=%async_computation.3 | async-start | bytes 3145728 | tf_op jit(solution)/shard_map/psum | solution.py:63
  82.5 3.2 %copy-start.3 = (f32[256,128]{1,0:T(8,128)}, f32[256,128]{1,0:T(8,128)S(1)}, u32[]{:S(2)}) copy-start(f32[256,128]{1,0:T(8,128)S(1)} %fusion.15) | copy-start | bytes 393220
  85.7 90.5 %copy-start.5 = (bf16[1,2,512,128]{3,2,1,0:T(8,128)(2,1)S(1)}, bf16[1,2,512,128]{3,2,1,0:T(8,128)(2,1)}, u32[]{:S(2)}) copy-start(bf16[1,2,512,128]{3,2,1,0:T(8,128)(2,1)} %param.28) | copy-start | bytes 786436
  85.7 146.6 %all-reduce.9.cloned.1.call-start = ((), (), s32[]{:S(2)}) async-start(), calls=%async_computation.4 | async-start | bytes 2097152 | tf_op jit(solution)/shard_map/psum | solution.py:72
  176.2 4.8 %copy-start.4 = (f32[256,128]{1,0:T(8,128)}, f32[256,128]{1,0:T(8,128)S(1)}, u32[]{:S(2)}) copy-start(f32[256,128]{1,0:T(8,128)S(1)} %fusion.19) | copy-start | bytes 393220
  177.8 2.0 collective-permute-start
  179.7 54.7 %copy-start.7 = (bf16[2,512,128]{2,1,0:T(8,128)(2,1)S(1)}, bf16[2,512,128]{2,1,0:T(8,128)(2,1)}, u32[]{:S(2)}) copy-start(bf16[2,512,128]{2,1,0:T(8,128)(2,1)} %param.31) | copy-start | bytes 786436
  180.9 90.1 %all-reduce.11.cloned.1.call-start = ((), (), s32[]{:S(2)}) async-start(), calls=%async_computation.5 | async-start | bytes 524288 | tf_op jit(solution)/shard_map/psum | solution.py:88
  236.2 38.2 %collective-permute-start.1 = (bf16[256,128]{1,0:T(8,128)(2,1)}, bf16[256,128]{1,0:T(8,128)(2,1)}, u32[]{:S(2)}, u32[]{:S(2)}) collective-permute-start(bf16[256,128]{1,0:T(8,128)(2,1)} %get-tuple-element.8), channel_id=1, source_target_pairs={{0,16},{16,0},{8,24},{24,8},{1,17},{17,1},{9,25},{25,9},{2,18},{18... | collective-permute-start | bytes 196616 | tf_op jit(solution)/shard_map/ppermute | solution.py:14
  273.0 6.9 %collective-permute-start.2 = (bf16[256,512]{1,0:T(8,128)(2,1)}, bf16[256,512]{1,0:T(8,128)(2,1)S(1)}, u32[]{:S(2)}, u32[]{:S(2)}) collective-permute-start(bf16[256,512]{1,0:T(8,128)(2,1)} %fusion.13), channel_id=1, source_target_pairs={{0,16},{16,0},{8,24},{24,8},{1,17},{17,1},{9,25},{25,9},{2,18},{18... | collective-permute-start | bytes 786440 | tf_op jit(solution)/shard_map/ppermute | solution.py:14
Sparse Core Ops, SparseCore 0:
  17.3 22.9 reduce-scatter.1
  42.8 38.2 all-reduce.4
  85.8 88.8 all-reduce.6
  181.1 51.1 all-reduce.8
  236.3 34.7 all-reduce.10
where the time goes:
time: 289 us
  waiting for transfers between devices  213 us (74%)
  matrix products  51.6 us (18%)
  between operations  14 us (5%)
  other arithmetic  4.67 us (2%)
  starting transfers between devices  3.49 us (1%)
    psum x1, waiting for transfers between devices, per_device(): layer_full = lax.psum(layer_part, ('row', 'col'))  88.9 us
    psum x1, waiting for transfers between devices, per_device(): paired = lax.psum(paired, 'row')  51.3 us
    psum x1, waiting for transfers between devices, per_device(): lax.psum(own_up.astype(jnp.bfloat16), 'row').astype(jnp.float32)  33.3 us
    dot_general x1, matrix products, per_device(): jnp.einsum('lk,lkra->kra', up_weight, to_up, precision=lax.Precision.HIGH...  22.7 us
    psum x1, waiting for transfers between devices, per_device(): summed = lax.psum(summed, 'row')  17.8 us
    reduce_scatter x1, waiting for transfers between devices, per_device(): summed = lax.psum_scatter(mid_terms, 'col', scatter_dimension=0, tiled=True)  15.5 us
    dot_general x1, matrix products, per_device(): jnp.einsum('lrc,lkac->lkra', leaf_round, leaf_lower_coupling, preferred_e...  7.54 us
    ppermute x3, waiting for transfers between devices, from_partner(): return lax.ppermute(block, axis, route)  6.41 us
  transfers between devices with their start and end apart: 8, of which 7 were waited for; matrix products, arithmetic and copies ran while one was open for 11% of the time, Pallas kernels for 0%

commit v1 on v0

v1 whole, which is shorter than its diff:
```python
import functools

import jax
import jax.numpy as jnp
from jax import lax
from jax.experimental import pallas as pl
from jax.experimental.pallas import tpu as pltpu
from jax.sharding import PartitionSpec as P

BF16 = jnp.bfloat16
F32 = jnp.float32
VMEM_BYTES = 48 * 1024 * 1024


def times_transposed(left, right):
    return lax.dot_general(left, right, (((1,), (1,)), ((), ())), preferred_element_type=F32)


def leaf_kernel(per_step, slots, slot_ref, rhs_ref, inv_ref, mid_ref, solved_ref, round_ref, terms_ref, total):
    step = pl.program_id(0)

    @pl.when(step == 0)
    def _():
        total[...] = jnp.zeros_like(total)

    for i in range(per_step):
        solved = times_transposed(rhs_ref[i].astype(BF16), inv_ref[i])
        solved_ref[i] = solved
        rounded = solved.astype(BF16)
        round_ref[i] = rounded
        slot = slot_ref[step * per_step + i]
        total[slot] += times_transposed(rounded, mid_ref[i])

    @pl.when(step == pl.num_programs(0) - 1)
    def _():
        for s in range(slots):
            terms_ref[s] = total[s].astype(BF16)


def leaf_solve(slot, rhs, inv, lower_mid, slots):
    leaves, rows, size = rhs.shape
    width = inv.shape[1]
    per_step = 2 if leaves % 2 == 0 else 1
    return pl.pallas_call(
        functools.partial(leaf_kernel, per_step, slots),
        grid=(leaves // per_step,),
        in_specs=[
            pl.BlockSpec(memory_space=pltpu.SMEM),
            pl.BlockSpec((per_step, rows, size), lambda i: (i, 0, 0)),
            pl.BlockSpec((per_step, width, size), lambda i: (i, 0, 0)),
            pl.BlockSpec((per_step, size, width), lambda i: (i, 0, 0)),
        ],
        out_specs=[
            pl.BlockSpec((per_step, rows, width), lambda i: (i, 0, 0)),
            pl.BlockSpec((per_step, rows, width), lambda i: (i, 0, 0)),
            pl.BlockSpec((slots, rows, size), lambda i: (0, 0, 0)),
        ],
        out_shape=[
            jax.ShapeDtypeStruct((leaves, rows, width), F32),
            jax.ShapeDtypeStruct((leaves, rows, width), BF16),
            jax.ShapeDtypeStruct((slots, rows, size), BF16),
        ],
        scratch_shapes=[pltpu.VMEM((slots, rows, size), F32)],
        compiler_params=pltpu.CompilerParams(
            dimension_semantics=("arbitrary",), vmem_limit_bytes=VMEM_BYTES
        ),
        cost_estimate=pl.CostEstimate(
            flops=4 * leaves * rows * size * width,
            bytes_accessed=leaves * (rows * size * 4 + 4 * width * size + rows * width * 6),
            transcendentals=0,
        ),
        name="leaf_solve",
    )(slot, rhs, inv, lower_mid)


def coupling_kernel(per_step, pattern_ref, round_ref, lower_ref, up_ref):
    step = pl.program_id(0)

    @pl.when(step == 0)
    def _():
        up_ref[...] = jnp.zeros_like(up_ref)

    for k in range(up_ref.shape[0]):
        left, right = [], []
        for i in range(per_step):
            weight = pattern_ref[step * per_step + i, k].astype(F32).astype(BF16)
            left.append(round_ref[i] * weight)
            right.append(lower_ref[i, k])
        left = left[0] if per_step == 1 else jnp.concatenate(left, axis=1)
        right = right[0] if per_step == 1 else jnp.concatenate(right, axis=1)
        up_ref[k] += times_transposed(left, right)


def leaf_coupling(pattern, rounded, lower):
    leaves, rows, width = rounded.shape
    kinds, size = lower.shape[1:3]
    per_step = 2 if leaves % 2 == 0 else 1
    return pl.pallas_call(
        functools.partial(coupling_kernel, per_step),
        grid=(leaves // per_step,),
        in_specs=[
            pl.BlockSpec(memory_space=pltpu.SMEM),
            pl.BlockSpec((per_step, rows, width), lambda i: (i, 0, 0)),
            pl.BlockSpec((per_step, kinds, size, width), lambda i: (i, 0, 0, 0)),
        ],
        out_specs=pl.BlockSpec((kinds, rows, size), lambda i: (0, 0, 0)),
        out_shape=jax.ShapeDtypeStruct((kinds, rows, size), F32),
        compiler_params=pltpu.CompilerParams(
            dimension_semantics=("arbitrary",), vmem_limit_bytes=VMEM_BYTES
        ),
        cost_estimate=pl.CostEstimate(
            flops=2 * leaves * kinds * rows * size * width,
            bytes_accessed=leaves * (rows * width * 2 + kinds * size * width * 2) + kinds * rows * size * 4,
            transcendentals=0,
        ),
        name="leaf_coupling",
    )(pattern, rounded, lower)


def swap(block, axis, bit):
    count = lax.axis_size(axis)
    return lax.ppermute(block, axis, [(i, i ^ 1 << bit) for i in range(count)])


def swap_sum(halves, axis, bit):
    here = lax.axis_index(axis) >> bit & 1
    kept = lax.dynamic_index_in_dim(halves, here, 0, keepdims=False)
    given = lax.dynamic_index_in_dim(halves, 1 - here, 0, keepdims=False)
    return kept.astype(F32) + swap(given.astype(BF16), axis, bit).astype(F32)


def exchange(pieces, axis):
    return lax.all_to_all(pieces, axis, split_axis=0, concat_axis=0, tiled=True)


def scatter_sum(pieces, axis):
    return jnp.sum(exchange(pieces.astype(BF16), axis).astype(F32), axis=0)


def col_sum(pieces):
    if pieces.shape[0] == 2:
        return swap_sum(pieces, "col", 0)
    return scatter_sum(pieces, "col")


def spread(piece, axis):
    count = lax.axis_size(axis)
    return exchange(jnp.broadcast_to(piece[None], (count,) + piece.shape), axis)


def col_spread(piece):
    if lax.axis_size("col") == 2:
        other = swap(piece, "col", 0)
        first = lax.axis_index("col") == 0
        return jnp.stack([jnp.where(first, piece, other), jnp.where(first, other, piece)])
    return spread(piece, "col")


def per_device(
    leaf_rhs,
    leaf_inv,
    leaf_lower_mid,
    leaf_lower_coupling,
    leaf_parent,
    leaf_pattern,
    mid_rhs,
    parent_diagonal_inverse,
    mid_lower,
    mid_pattern,
    top_rhs,
    top_inv,
    top_lower,
    apex_rhs,
    apex_inv,
    apex_lower,
):
    cols = lax.axis_size("col")
    rows = lax.axis_size("row")
    col = lax.axis_index("col")
    row = lax.axis_index("row")
    gz = lax.axis_index("gz")
    pair, core = gz // 2, gz % 2
    rhs_count, size = leaf_rhs.shape[1:]
    part = rhs_count // (4 * cols)

    first = col if cols == 2 else 0
    slot = lax.rem(leaf_parent - first + cols, cols)
    leaf_solved, leaf_round, terms = leaf_solve(slot, leaf_rhs, leaf_inv, leaf_lower_mid, cols)
    if cols == 2:
        mid_part = terms[0].astype(F32) + swap(terms[1], "col", 0).astype(F32)
    else:
        mid_part = scatter_sum(terms, "col")
    layer_up = leaf_coupling(leaf_pattern, leaf_round, leaf_lower_coupling)
    quarter = rhs_count // rows
    mid_sum = scatter_sum(mid_part.reshape(rows, quarter, size), "row")
    mid_total = lax.dynamic_slice_in_dim(mid_rhs[0], row * quarter, quarter, 0) - mid_sum
    mid_ready = spread(mid_total.astype(BF16), "row").reshape(rhs_count, size)
    mid_solved = times_transposed(mid_ready, parent_diagonal_inverse[0])
    mid_round = mid_solved.astype(BF16)
    mid_weight = mid_pattern[0].astype(F32)

    top_part = layer_up[0] + times_transposed(mid_round, mid_lower[0, 0])
    top_part = top_part.astype(BF16).reshape(rows, cols, part, size).swapaxes(0, 1)
    top_sum = scatter_sum(top_part.reshape(rows * cols, part, size), ("col", "row"))
    top_start = (row * cols + col) * part
    top_total = lax.dynamic_slice_in_dim(top_rhs[0], top_start, part, 0) - top_sum
    top_ready = spread(top_total.astype(BF16), "row").reshape(rows * part, size)
    top_solved = times_transposed(top_ready, top_inv[0])
    top_round = top_solved.astype(BF16)

    late = jnp.stack([layer_up[k] + mid_weight[k - 1] * times_transposed(mid_round, mid_lower[0, k]) for k in (1, 2)])
    late = late.reshape(2, 2, 2, cols, part, size)
    late = swap_sum(late.transpose(2, 0, 1, 3, 4, 5), "gz", 0)
    late = col_sum(late.transpose(2, 0, 1, 3, 4))

    up = jnp.stack([times_transposed(top_round, top_lower[0, k]) for k in (0, 1)])
    up = swap_sum(up.reshape(2, 2, 2, part, size).transpose(2, 0, 1, 3, 4), "gz", 0) + late
    half = part // 2
    front_sum = scatter_sum(up[0].reshape(rows, half, size), "row")
    front_start = row // 2 * (rhs_count // 2) + (core * cols + col) * part + row % 2 * half
    front_rhs = lax.dynamic_slice(apex_rhs, (pair, front_start, 0), (1, half, size))[0]
    front_ready = spread((front_rhs - front_sum).astype(BF16), "row").reshape(2 * part, size)
    front_inv = lax.dynamic_index_in_dim(apex_inv, pair, 0, keepdims=False)
    front_lower = lax.dynamic_index_in_dim(apex_lower, pair, 0, keepdims=False)
    front_solved = times_transposed(front_ready, front_inv)

    own_up = times_transposed(front_solved.astype(BF16), front_lower)
    last_part = swap_sum(up[1] + own_up.reshape(2, part, size), "gz", 1)
    last_sum = jnp.sum(spread(last_part.astype(BF16), "row").astype(F32), axis=0)
    last_start = (pair * 2 * cols + core * cols + col) * part
    last_rhs = lax.dynamic_slice_in_dim(apex_rhs[2], last_start, part, 0)
    last_solved = times_transposed((last_rhs - last_sum).astype(BF16), apex_inv[2])

    width = last_solved.shape[1]
    front_solved = front_solved.reshape(2, part, width)
    own_front = lax.dynamic_index_in_dim(front_solved, pair, 0, keepdims=False)
    other_front = swap(lax.dynamic_index_in_dim(front_solved, 1 - pair, 0, keepdims=False), "gz", 1)
    leading = pair == 0
    fronts = jnp.stack([jnp.where(leading, own_front, other_front), jnp.where(leading, other_front, own_front)])
    fronts = col_spread(fronts).swapaxes(0, 1).reshape(2, cols * part, width)
    last = col_spread(last_solved).reshape(1, cols * part, width)
    top_all = col_spread(top_solved.reshape(rows, part, width)).swapaxes(0, 1).reshape(1, rhs_count, width)
    return (leaf_solved, mid_solved[None], top_all, jnp.concatenate([fronts, last], axis=0))


def solution(mesh):
    placed = (
        P(("gz", "col"), None, None),
        P(("gz", "col"), "row", None),
        P(("gz", "col"), None, "row"),
        P(("gz", "col"), None, None, "row"),
        P(("gz", "col")),
        P(("gz", "col"), None),
        P(("gz", "col"), None, None),
        P(("gz", "col"), "row", None),
        P(("gz", "col"), None, None, "row"),
        P(("gz", "col"), None),
        P("gz", None, None),
        P("gz", "row", None),
        P("gz", None, None, "row"),
        P(),
        P(None, "row", None),
        P(None, None, "row"),
    )
    return jax.shard_map(
        per_device,
        mesh=mesh,
        in_specs=placed,
        out_specs=(
            P(("gz", "col"), None, "row"),
            P(("gz", "col"), None, "row"),
            P("gz", None, "row"),
            P(None, "gz", "row"),
        ),
        check_vma=False,
    )
```

time: 289 us -> 115 us (0.40)
  waiting for transfers between devices: 213 us -> 48.2 us
  matrix products: 51.6 us -> 7.79 us
  starting transfers between devices: 3.49 us -> 34.6 us
  between operations: 14 us -> 1.08 us
  local copies, waits for them, and re-layouts: 1.53 us -> 10.5 us
  Pallas kernels: 0 us -> 7.77 us
    psum x4 -> x0, waiting for transfers between devices: 191 us -> none  [the longest x1 88.9 us: per_device(): layer_full = lax.psum(layer_part, ('row', 'col'))]
    dot_general x12 -> x10, matrix products: 51.6 us -> 7.79 us  [times_transposed(): lax.dot_general(left, right, (((1,), (1,)), ((), ())), preferred_element_...]
    all_to_all x0 -> x7, waiting for transfers between devices: none -> 35.9 us  [exchange(): return lax.all_to_all(pieces, axis, split_axis=0, concat_axis=0, tiled=True)]
    all_to_all x0 -> x7, starting transfers between devices: none -> 26.2 us  [exchange(): return lax.all_to_all(pieces, axis, split_axis=0, concat_axis=0, tiled=True)]
    reduce_scatter x1 -> x0, waiting for transfers between devices: 15.5 us -> none  [per_device(): summed = lax.psum_scatter(mid_terms, 'col', scatter_dimension=0, tiled=True)]
    pallas_call x0 -> x2, Pallas kernels: none -> 7.77 us  [the longest x1 5.36 us: leaf_solve(): pl.pallas_call(functools.partial(leaf_kernel, per_step, slots), grid=(lea...]
    ppermute x3 -> x9, waiting for transfers between devices: 6.41 us -> 12.3 us  [swap(): return lax.ppermute(block, axis, [(i, i ^ 1 << bit) for i in range(count)])]
    ppermute x3 -> x9, starting transfers between devices: 3.11 us -> 8.32 us  [swap(): return lax.ppermute(block, axis, [(i, i ^ 1 << bit) for i in range(count)])]
  transfers between devices with their start and end apart: 8 -> 16, of which waited for: 7 -> 12; matrix products, arithmetic and copies ran while one was open for 11% -> 8% of each run, Pallas kernels for 0% -> 2%
where the time goes in v1:
time: 115 us; the launch traced here: 114 us
  waiting for transfers between devices  48.2 us (42%)
  starting transfers between devices  34.6 us (30%)
  local copies, waits for them, and re-layouts  10.5 us (9%)
  matrix products  7.79 us (7%)
  Pallas kernels  7.77 us (7%)
  other arithmetic  4.35 us (4%)
    all_to_all x7, waiting for transfers between devices, exchange(): return lax.all_to_all(pieces, axis, split_axis=0, concat_axis=0, tiled=True)  35.9 us
    all_to_all x7, starting transfers between devices, exchange(): return lax.all_to_all(pieces, axis, split_axis=0, concat_axis=0, tiled=True)  26.2 us
    ppermute x9, waiting for transfers between devices, swap(): return lax.ppermute(block, axis, [(i, i ^ 1 << bit) for i in range(count)])  12.3 us
    ppermute x9, starting transfers between devices, swap(): return lax.ppermute(block, axis, [(i, i ^ 1 << bit) for i in range(count)])  8.32 us
    dot_general x10, matrix products, times_transposed(): lax.dot_general(left, right, (((1,), (1,)), ((), ())), preferred_element_...  7.79 us
    pallas_call x1, Pallas kernels, leaf_solve(): pl.pallas_call(functools.partial(leaf_kernel, per_step, slots), grid=(lea...  5.36 us
    unnamed x23, local copies, waits for them, and re-layouts  4.47 us
    broadcast_in_dim x4, local copies, waits for them, and re-layouts, spread(): return exchange(jnp.broadcast_to(piece[None], (count,) + piece.shape), axis)  2.68 us
  transfers between devices with their start and end apart: 16, of which 12 were waited for; matrix products, arithmetic and copies ran while one was open for 8% of the time, Pallas kernels for 2%

profile of v1, /device:TPU:0, one launch (start us, length us, event | category | flops | bytes accessed | tf_op | source)
XLA Modules:
  0.0 114.2 jit_solution(5086784905500434880)
XLA Ops:
  3.8 5.4 %leaf_solve.1 = (f32[8,256,128]{2,1,0:T(8,128)}, bf16[8,256,128]{2,1,0:T(8,128)(2,1)S(1)}, bf16[2,256,512]{2,1,0:T(8,128)(2,1)S(1)}) custom-call(s32[8]{0:T(128)S(1)} %compare_select_fusion.slot_ref, f32[8,256,512]{2,1,0:T(8,128)} %rhs_ref.1, bf16[8,128,512]{2,1,0:T(8,128)(2,1)S(1)} %copy-done.2, bf16[8,512,128]{2,1,0:T(8,128)(2,1)S(1)} %copy-done.3), custom_call_target="tpu_custom_call" | custom-call | flops 536870912 | bytes 7864320 | tf_op jit(solution)/shard_map/leaf_solve/pallas_call | solution.py:44
  9.2 3.0 %collective-permute-start = (bf16[256,512]{1,0:T(8,128)(2,1)S(1)}, bf16[256,512]{1,0:T(8,128)(2,1)S(1)}, u32[]{:S(2)}, u32[]{:S(2)}) collective-permute-start(bf16[256,512]{1,0:T(8,128)(2,1)S(1)} %slice_bitcast_fusion.3), channel_id=1, source_target_pairs={{0,1},{1,0},{2,3},{3,2},{4,5},{5,4},{6,7},{7,6},{8,9},{9,8},{10,11... | collective-permute-start | bytes 786440 | tf_op jit(solution)/shard_map/ppermute | solution.py:122
  12.3 6.3 %collective-permute-done = bf16[256,512]{1,0:T(8,128)(2,1)S(1)} collective-permute-done((bf16[256,512]{1,0:T(8,128)(2,1)S(1)}, bf16[256,512]{1,0:T(8,128)(2,1)S(1)}, u32[]{:S(2)}, u32[]{:S(2)}) %collective-permute-start) | collective-permute-done | bytes 262176 | tf_op jit(solution)/shard_map/ppermute | solution.py:122
  19.3 5.1 %all-to-all-start = ((bf16[4,64,512]{2,1,0:T(8,128)(2,1)}), bf16[4,64,512]{2,1,0:T(8,128)(2,1)S(1)}, u32[]{:S(2)}, u32[]{:S(2)}) async-start(bf16[4,64,512]{2,1,0:T(8,128)(2,1)} %bitcast.2), calls=%async_computation | async-start | bytes 524288 | tf_op jit(solution)/shard_map/all_to_all | solution.py:133
  24.4 8.2 %all-to-all-done = bf16[4,64,512]{2,1,0:T(8,128)(2,1)S(1)} async-done(((bf16[4,64,512]{2,1,0:T(8,128)(2,1)}), bf16[4,64,512]{2,1,0:T(8,128)(2,1)S(1)}, u32[]{:S(2)}, u32[]{:S(2)}) %all-to-all-start) | async-done | bytes 262176 | tf_op jit(solution)/shard_map/all_to_all | solution.py:133
  34.3 3.4 %all-to-all-start.1 = ((bf16[4,64,512]{2,1,0:T(8,128)(2,1)}), bf16[4,64,512]{2,1,0:T(8,128)(2,1)S(1)}, u32[]{:S(2)}, u32[]{:S(2)}) async-start(bf16[4,64,512]{2,1,0:T(8,128)(2,1)} %broadcast_in_dim.34), calls=%async_computation.1 | async-start | bytes 524288 | tf_op jit(solution)/shard_map/all_to_all | solution.py:133
  37.8 1.9 %copy-done.1 = bf16[8,3,512,128]{3,2,1,0:T(8,128)(2,1)S(1)} copy-done((bf16[8,3,512,128]{3,2,1,0:T(8,128)(2,1)S(1)}, bf16[8,3,512,128]{3,2,1,0:T(8,128)(2,1)}, u32[]{:S(2)}) %copy-start.1) | copy-done | bytes 3145752
  39.7 2.4 %leaf_coupling.1 = f32[3,256,512]{2,1,0:T(8,128)S(1)} custom-call(s32[8,3]{1,0:T(8,128)S(1)} %copy.31.pattern_ref, bf16[8,256,128]{2,1,0:T(8,128)(2,1)S(1)} %get-tuple-element.9.round_ref, bf16[8,3,512,128]{3,2,1,0:T(8,128)(2,1)S(1)} %copy-done.1), custom_call_target="tpu_custom_call" | custom-call | flops 805306368 | bytes 5242880 | tf_op jit(solution)/shard_map/leaf_coupling/pallas_call | solution.py:98
  42.7 1.7 %all-to-all-done.1 = bf16[4,64,512]{2,1,0:T(8,128)(2,1)S(1)} async-done(((bf16[4,64,512]{2,1,0:T(8,128)(2,1)}), bf16[4,64,512]{2,1,0:T(8,128)(2,1)S(1)}, u32[]{:S(2)}, u32[]{:S(2)}) %all-to-all-start.1) | async-done | bytes 262176 | tf_op jit(solution)/shard_map/all_to_all | solution.py:133
  46.6 4.4 %all-to-all-start.2 = ((bf16[8,32,512]{2,1,0:T(8,128)(2,1)}), bf16[8,32,512]{2,1,0:T(8,128)(2,1)S(1)}, u32[]{:S(2)}, u32[]{:S(2)}) async-start(bf16[8,32,512]{2,1,0:T(8,128)(2,1)} %bitcast.12), calls=%async_computation.2 | async-start | bytes 524288 | tf_op jit(solution)/shard_map/all_to_all | solution.py:133
  51.0 1.8 %fusion = f32[256,512]{1,0:T(8,128)S(1)} fusion(f32[3,256,512]{2,1,0:T(8,128)S(1)} %leaf_coupling.1, f32[]{:T(128)} %bitcast.34, bf16[1,3,512,128]{3,2,1,0:T(8,128)(2,1)} %param.24, f32[256,128]{1,0:T(8,128)S(1)} %fusion.32), kind=kOutput, calls=%fused_computation.7 | convolution fusion | flops 33849344 | bytes 1311232 | tf_op jit(solution)/shard_map/dot_general | solution.py:16
  52.8 1.8 %fusion.1 = f32[256,512]{1,0:T(8,128)S(1)} fusion(f32[3,256,512]{2,1,0:T(8,128)S(1)} %leaf_coupling.1, f32[]{:T(128)} %bitcast.38, bf16[1,3,512,128]{3,2,1,0:T(8,128)(2,1)} %param.24, f32[256,128]{1,0:T(8,128)S(1)} %fusion.32), kind=kOutput, calls=%fused_computation.8 | convolution fusion | flops 33849344 | bytes 1311232 | tf_op jit(solution)/shard_map/dot_general | solution.py:16
  54.7 4.9 %all-to-all-done.2 = bf16[8,32,512]{2,1,0:T(8,128)(2,1)S(1)} async-done(((bf16[8,32,512]{2,1,0:T(8,128)(2,1)}), bf16[8,32,512]{2,1,0:T(8,128)(2,1)S(1)}, u32[]{:S(2)}, u32[]{:S(2)}) %all-to-all-start.2) | async-done | bytes 262176 | tf_op jit(solution)/shard_map/all_to_all | solution.py:133
  61.2 3.3 %all-to-all-start.3 = ((bf16[4,32,512]{2,1,0:T(8,128)(2,1)}), bf16[4,32,512]{2,1,0:T(8,128)(2,1)S(1)}, u32[]{:S(2)}, u32[]{:S(2)}) async-start(bf16[4,32,512]{2,1,0:T(8,128)(2,1)} %broadcast_in_dim.37), calls=%async_computation.3 | async-start | bytes 262144 | tf_op jit(solution)/shard_map/all_to_all | solution.py:133
  65.8 4.5 %all-to-all-done.3 = bf16[4,32,512]{2,1,0:T(8,128)(2,1)S(1)} async-done(((bf16[4,32,512]{2,1,0:T(8,128)(2,1)}), bf16[4,32,512]{2,1,0:T(8,128)(2,1)S(1)}, u32[]{:S(2)}, u32[]{:S(2)}) %all-to-all-start.3) | async-done | bytes 131104 | tf_op jit(solution)/shard_map/all_to_all | solution.py:133
  73.1 3.4 %all-to-all-start.4 = ((bf16[4,16,512]{2,1,0:T(8,128)(2,1)}), bf16[4,16,512]{2,1,0:T(8,128)(2,1)S(1)}, u32[]{:S(2)}, u32[]{:S(2)}) async-start(bf16[4,16,512]{2,1,0:T(8,128)(2,1)} %bitcast.45), calls=%async_computation.4 | async-start | bytes 131072 | tf_op jit(solution)/shard_map/all_to_all | solution.py:133
  76.6 5.7 %all-to-all-done.4 = bf16[4,16,512]{2,1,0:T(8,128)(2,1)S(1)} async-done(((bf16[4,16,512]{2,1,0:T(8,128)(2,1)}), bf16[4,16,512]{2,1,0:T(8,128)(2,1)S(1)}, u32[]{:S(2)}, u32[]{:S(2)}) %all-to-all-start.4) | async-done | bytes 65568 | tf_op jit(solution)/shard_map/all_to_all | solution.py:133
  83.0 3.3 %all-to-all-start.5 = ((bf16[4,16,512]{2,1,0:T(8,128)(2,1)}), bf16[4,16,512]{2,1,0:T(8,128)(2,1)S(1)}, u32[]{:S(2)}, u32[]{:S(2)}) async-start(bf16[4,16,512]{2,1,0:T(8,128)(2,1)} %broadcast_in_dim.39), calls=%async_computation.5 | async-start | bytes 131072 | tf_op jit(solution)/shard_map/all_to_all | solution.py:133
  86.9 5.0 %all-to-all-done.5 = bf16[4,16,512]{2,1,0:T(8,128)(2,1)S(1)} async-done(((bf16[4,16,512]{2,1,0:T(8,128)(2,1)}), bf16[4,16,512]{2,1,0:T(8,128)(2,1)S(1)}, u32[]{:S(2)}, u32[]{:S(2)}) %all-to-all-start.5) | async-done | bytes 65568 | tf_op jit(solution)/shard_map/all_to_all | solution.py:133
  93.1 1.6 %collective-permute-start.5 = (f32[32,128]{1,0:T(8,128)S(1)}, f32[32,128]{1,0:T(8,128)S(1)}, u32[]{:S(2)}, u32[]{:S(2)}) collective-permute-start(f32[32,128]{1,0:T(8,128)S(1)} %dynamic-slice_bitcast_fusion), channel_id=1, source_target_pairs={{0,16},{8,24},{16,0},{24,8},{1,17},{9,25},{17,1},{25,9},{2,18},{10... | collective-permute-start | bytes 49160 | tf_op jit(solution)/shard_map/ppermute | solution.py:122
  95.4 1.4 %collective-permute-done.5 = f32[32,128]{1,0:T(8,128)S(1)} collective-permute-done((f32[32,128]{1,0:T(8,128)S(1)}, f32[32,128]{1,0:T(8,128)S(1)}, u32[]{:S(2)}, u32[]{:S(2)}) %collective-permute-start.5) | collective-permute-done | bytes 16416 | tf_op jit(solution)/shard_map/ppermute | solution.py:122
  99.5 3.3 %all-to-all-start.6 = ((bf16[4,32,512]{2,1,0:T(8,128)(2,1)}), bf16[4,32,512]{2,1,0:T(8,128)(2,1)S(1)}, u32[]{:S(2)}, u32[]{:S(2)}) async-start(bf16[4,32,512]{2,1,0:T(8,128)(2,1)} %broadcast_in_dim.40), calls=%async_computation.6 | async-start | bytes 262144 | tf_op jit(solution)/shard_map/all_to_all | solution.py:133
  102.8 5.9 %all-to-all-done.6 = bf16[4,32,512]{2,1,0:T(8,128)(2,1)S(1)} async-done(((bf16[4,32,512]{2,1,0:T(8,128)(2,1)}), bf16[4,32,512]{2,1,0:T(8,128)(2,1)S(1)}, u32[]{:S(2)}, u32[]{:S(2)}) %all-to-all-start.6) | async-done | bytes 131104 | tf_op jit(solution)/shard_map/all_to_all | solution.py:133
  110.6 2.9 %collective-permute-done.8 = f32[32,128]{1,0:T(8,128)S(1)} collective-permute-done((f32[32,128]{1,0:T(8,128)S(1)}, f32[32,128]{1,0:T(8,128)S(1)}, u32[]{:S(2)}, u32[]{:S(2)}) %collective-permute-start.8) | collective-permute-done | bytes 16416 | tf_op jit(solution)/shard_map/ppermute | solution.py:122
  (81 shorter events, 22.5 us)
Async XLA Ops:
  0.6 94.0 %copy-start = (bf16[2,512,128]{2,1,0:T(8,128)(2,1)S(1)}, bf16[2,512,128]{2,1,0:T(8,128)(2,1)}, u32[]{:S(2)}) copy-start(bf16[2,512,128]{2,1,0:T(8,128)(2,1)} %param.31) | copy-start | bytes 786436
  9.2 28.5 %copy-start.9 = (s32[8,3]{0,1:T(4,128)S(1)}, s32[8,3]{0,1:T(4,128)}, u32[]{:S(2)}) copy-start(s32[8,3]{0,1:T(4,128)} %param.21) | copy-start | bytes 292
  9.2 28.6 %copy-start.10 = (s32[1,2]{1,0:T(1,128)S(1)}, s32[1,2]{1,0:T(1,128)}, u32[]{:S(2)}) copy-start(s32[1,2]{1,0:T(1,128)} %param.25) | copy-start | bytes 28
  9.2 9.3 %collective-permute-start = (bf16[256,512]{1,0:T(8,128)(2,1)S(1)}, bf16[256,512]{1,0:T(8,128)(2,1)S(1)}, u32[]{:S(2)}, u32[]{:S(2)}) collective-permute-start(bf16[256,512]{1,0:T(8,128)(2,1)S(1)} %slice_bitcast_fusion.3), channel_id=1, source_target_pairs={{0,1},{1,0},{2,3},{3,2},{4,5},{5,4},{6,7},{7,6},{8,9},{9,8},{10,11... | collective-permute-start | bytes 786440 | tf_op jit(solution)/shard_map/ppermute | solution.py:122
  19.3 13.3 %all-to-all-start = ((bf16[4,64,512]{2,1,0:T(8,128)(2,1)}), bf16[4,64,512]{2,1,0:T(8,128)(2,1)S(1)}, u32[]{:S(2)}, u32[]{:S(2)}) async-start(bf16[4,64,512]{2,1,0:T(8,128)(2,1)} %bitcast.2), calls=%async_computation | async-start | bytes 524288 | tf_op jit(solution)/shard_map/all_to_all | solution.py:133
  34.3 10.2 %all-to-all-start.1 = ((bf16[4,64,512]{2,1,0:T(8,128)(2,1)}), bf16[4,64,512]{2,1,0:T(8,128)(2,1)S(1)}, u32[]{:S(2)}, u32[]{:S(2)}) async-start(bf16[4,64,512]{2,1,0:T(8,128)(2,1)} %broadcast_in_dim.34), calls=%async_computation.1 | async-start | bytes 524288 | tf_op jit(solution)/shard_map/all_to_all | solution.py:133
  44.7 8.1 %copy-start.4 = (f32[256,128]{1,0:T(8,128)}, f32[256,128]{1,0:T(8,128)S(1)}, u32[]{:S(2)}) copy-start(f32[256,128]{1,0:T(8,128)S(1)} %fusion.32) | copy-start | bytes 393220
  46.6 13.0 %all-to-all-start.2 = ((bf16[8,32,512]{2,1,0:T(8,128)(2,1)}), bf16[8,32,512]{2,1,0:T(8,128)(2,1)S(1)}, u32[]{:S(2)}, u32[]{:S(2)}) async-start(bf16[8,32,512]{2,1,0:T(8,128)(2,1)} %bitcast.12), calls=%async_computation.2 | async-start | bytes 524288 | tf_op jit(solution)/shard_map/all_to_all | solution.py:133
  54.6 15.8 %copy-start.8 = (bf16[1,128,512]{2,1,0:T(8,128)(2,1)S(1)}, bf16[1,128,512]{2,1,0:T(8,128)(2,1)}, u32[]{:S(2)}) copy-start(bf16[1,128,512]{2,1,0:T(8,128)(2,1)} %param.27) | copy-start | bytes 393220
  54.6 9.9 %collective-permute-start.3 = (bf16[2,2,2,32,512]{4,3,1,0,2:T(8,128)(2,1)S(1)}, bf16[2,2,2,32,512]{4,3,1,0,2:T(8,128)(2,1)S(1)}, u32[]{:S(2)}, u32[]{:S(2)}) collective-permute-start(bf16[2,2,2,32,512]{4,3,1,0,2:T(8,128)(2,1)S(1)} %fusion.7), channel_id=1, source_target_pairs={{0,8},{8,0},{16,24},{24,16},{1,9},{9,1},{17,25},{25,17},{2,10},{10... | collective-permute-start | bytes 786440 | tf_op jit(solution)/shard_map/ppermute | solution.py:122
  59.6 11.0 %copy-start.6 = (bf16[1,2,512,128]{3,2,1,0:T(8,128)(2,1)S(1)}, bf16[1,2,512,128]{3,2,1,0:T(8,128)(2,1)}, u32[]{:S(2)}) copy-start(bf16[1,2,512,128]{3,2,1,0:T(8,128)(2,1)} %param.28) | copy-start | bytes 786436
  61.2 9.2 %all-to-all-start.3 = ((bf16[4,32,512]{2,1,0:T(8,128)(2,1)}), bf16[4,32,512]{2,1,0:T(8,128)(2,1)S(1)}, u32[]{:S(2)}, u32[]{:S(2)}) async-start(bf16[4,32,512]{2,1,0:T(8,128)(2,1)} %broadcast_in_dim.37), calls=%async_computation.3 | async-start | bytes 262144 | tf_op jit(solution)/shard_map/all_to_all | solution.py:133
  65.3 6.5 %collective-permute-start.4 = (bf16[2,2,32,512]{3,2,1,0:T(8,128)(2,1)}, bf16[2,2,32,512]{3,2,1,0:T(8,128)(2,1)S(1)}, u32[]{:S(2)}, u32[]{:S(2)}) collective-permute-start(bf16[2,2,32,512]{3,2,1,0:T(8,128)(2,1)} %fusion.14), channel_id=1, source_target_pairs={{0,1},{1,0},{2,3},{3,2},{4,5},{5,4},{6,7},{7,6},{8,9},{9,8},{10,11... | collective-permute-start | bytes 393224 | tf_op jit(solution)/shard_map/ppermute | solution.py:122
  71.0 11.3 %copy-start.5 = (f32[3,256,512]{2,1,0:T(8,128)S(1)}, f32[3,256,512]{2,1,0:T(8,128)}, u32[]{:S(2)}) copy-start(f32[3,256,512]{2,1,0:T(8,128)} %param.29) | copy-start | bytes 4718596
  71.0 1.4 %collective-permute-start.2 = (bf16[2,2,32,512]{3,2,1,0:T(8,128)(2,1)S(1)}, bf16[2,2,32,512]{3,2,1,0:T(8,128)(2,1)S(1)}, u32[]{:S(2)}, u32[]{:S(2)}) collective-permute-start(bf16[2,2,32,512]{3,2,1,0:T(8,128)(2,1)S(1)} %fusion.15), channel_id=1, source_target_pairs={{0,8},{8,0},{16,24},{24,16},{1,9},{9,1},{17,25},{25,17},{2,10},{10... | collective-permute-start | bytes 393224 | tf_op jit(solution)/shard_map/ppermute | solution.py:122
  71.2 5.4 %collective-permute-start.1 = (f32[4,32,128]{2,1,0:T(8,128)S(1)}, f32[4,32,128]{2,1,0:T(8,128)S(1)}, u32[]{:S(2)}, u32[]{:S(2)}) collective-permute-start(f32[4,32,128]{2,1,0:T(8,128)S(1)} %bitcast.200), channel_id=1, source_target_pairs={{0,1},{1,0},{2,3},{3,2},{4,5},{5,4},{6,7},{7,6},{8,9},{9,8},{10,11... | collective-permute-start | bytes 196616 | tf_op jit(solution)/shard_map/ppermute | solution.py:122
  73.1 35.6 %slice-start = ((f32[3,256,512]{2,1,0:T(8,128)}), f32[1,256,512]{2,1,0:T(8,128)S(1)}, s32[]{:S(2)}) async-start(f32[3,256,512]{2,1,0:T(8,128)} %param.29), calls=%async_computation.7 | async-start | bytes 1048576 | tf_op jit(solution)/shard_map/slice | solution.py:231
  73.1 9.1 %all-to-all-start.4 = ((bf16[4,16,512]{2,1,0:T(8,128)(2,1)}), bf16[4,16,512]{2,1,0:T(8,128)(2,1)S(1)}, u32[]{:S(2)}, u32[]{:S(2)}) async-start(bf16[4,16,512]{2,1,0:T(8,128)(2,1)} %bitcast.45), calls=%async_computation.4 | async-start | bytes 131072 | tf_op jit(solution)/shard_map/all_to_all | solution.py:133
  83.0 9.0 %all-to-all-start.5 = ((bf16[4,16,512]{2,1,0:T(8,128)(2,1)}), bf16[4,16,512]{2,1,0:T(8,128)(2,1)S(1)}, u32[]{:S(2)}, u32[]{:S(2)}) async-start(bf16[4,16,512]{2,1,0:T(8,128)(2,1)} %broadcast_in_dim.39), calls=%async_computation.5 | async-start | bytes 131072 | tf_op jit(solution)/shard_map/all_to_all | solution.py:133
  93.1 3.8 %collective-permute-start.5 = (f32[32,128]{1,0:T(8,128)S(1)}, f32[32,128]{1,0:T(8,128)S(1)}, u32[]{:S(2)}, u32[]{:S(2)}) collective-permute-start(f32[32,128]{1,0:T(8,128)S(1)} %dynamic-slice_bitcast_fusion), channel_id=1, source_target_pairs={{0,16},{8,24},{16,0},{24,8},{1,17},{9,25},{17,1},{25,9},{2,18},{10... | collective-permute-start | bytes 49160 | tf_op jit(solution)/shard_map/ppermute | solution.py:122
  94.8 4.0 %collective-permute-start.7 = (bf16[32,512]{1,0:T(8,128)(2,1)S(1)}, bf16[32,512]{1,0:T(8,128)(2,1)S(1)}, u32[]{:S(2)}, u32[]{:S(2)}) collective-permute-start(bf16[32,512]{1,0:T(8,128)(2,1)S(1)} %fusion.47), channel_id=1, source_target_pairs={{0,16},{8,24},{16,0},{24,8},{1,17},{9,25},{17,1},{25,9},{2,18},{10... | collective-permute-start | bytes 98312 | tf_op jit(solution)/shard_map/ppermute | solution.py:122
  96.9 5.9 %collective-permute-start.6 = (f32[2,32,128]{2,1,0:T(8,128)S(1)}, f32[2,32,128]{2,1,0:T(8,128)S(1)}, u32[]{:S(2)}, u32[]{:S(2)}) collective-permute-start(f32[2,32,128]{2,1,0:T(8,128)S(1)} %pad_maximum_fusion.2), channel_id=1, source_target_pairs={{0,1},{1,0},{2,3},{3,2},{4,5},{5,4},{6,7},{7,6},{8,9},{9,8},{10,11... | collective-permute-start | bytes 98312 | tf_op jit(solution)/shard_map/ppermute | solution.py:122
  99.5 9.2 %all-to-all-start.6 = ((bf16[4,32,512]{2,1,0:T(8,128)(2,1)}), bf16[4,32,512]{2,1,0:T(8,128)(2,1)S(1)}, u32[]{:S(2)}, u32[]{:S(2)}) async-start(bf16[4,32,512]{2,1,0:T(8,128)(2,1)} %broadcast_in_dim.40), calls=%async_computation.6 | async-start | bytes 262144 | tf_op jit(solution)/shard_map/all_to_all | solution.py:133
  109.8 3.8 %collective-permute-start.8 = (f32[32,128]{1,0:T(8,128)S(1)}, f32[32,128]{1,0:T(8,128)S(1)}, u32[]{:S(2)}, u32[]{:S(2)}) collective-permute-start(f32[32,128]{1,0:T(8,128)S(1)} %fusion.19), channel_id=1, source_target_pairs={{0,1},{1,0},{2,3},{3,2},{4,5},{5,4},{6,7},{7,6},{8,9},{9,8},{10,11... | collective-permute-start | bytes 49160 | tf_op jit(solution)/shard_map/ppermute | solution.py:122
  (4 other events, 9.1 us)

commit v2 on v1

--- a/solution.py
+++ b/solution.py
@@ -1,4 +1,5 @@
 import functools
+import math
 
 import jax
 import jax.numpy as jnp
@@ -9,15 +10,18 @@
 
 BF16 = jnp.bfloat16
 F32 = jnp.float32
-VMEM_BYTES = 48 * 1024 * 1024
+VMEM_BYTES = 60 * 1024 * 1024
+STEP_VMEM_BYTES = 32 * 1024 * 1024
 
 
 def times_transposed(left, right):
     return lax.dot_general(left, right, (((1,), (1,)), ((), ())), preferred_element_type=F32)
 
 
-def leaf_kernel(per_step, slots, slot_ref, rhs_ref, inv_ref, mid_ref, solved_ref, round_ref, terms_ref, total):
+def leaf_kernel(per_step, slots, parent_ref, rhs_ref, inv_ref, mid_ref, solved_ref, round_ref, *rest):
+    terms_refs, total = rest[:-1], rest[-1]
     step = pl.program_id(0)
+    first = lax.axis_index("col") if slots == 2 else 0
 
     @pl.when(step == 0)
     def _():
@@ -27,17 +31,17 @@
         solved = times_transposed(rhs_ref[i].astype(BF16), inv_ref[i])
         solved_ref[i] = solved
         rounded = solved.astype(BF16)
-        round_ref[i] = rounded
-        slot = slot_ref[step * per_step + i]
+        round_ref[step * per_step + i] = rounded
+        slot = parent_ref[step * per_step + i] ^ first
         total[slot] += times_transposed(rounded, mid_ref[i])
 
     @pl.when(step == pl.num_programs(0) - 1)
     def _():
-        for s in range(slots):
-            terms_ref[s] = total[s].astype(BF16)
-
-
-def leaf_solve(slot, rhs, inv, lower_mid, slots):
+        for s, ref in enumerate(terms_refs):
+            ref[...] = total[s].astype(ref.dtype)
+
+
+def leaf_solve(parent, rhs, inv, lower_mid, slots):
     leaves, rows, size = rhs.shape
     width = inv.shape[1]
     per_step = 2 if leaves % 2 == 0 else 1
@@ -52,14 +56,13 @@
         ],
         out_specs=[
             pl.BlockSpec((per_step, rows, width), lambda i: (i, 0, 0)),
-            pl.BlockSpec((per_step, rows, width), lambda i: (i, 0, 0)),
-            pl.BlockSpec((slots, rows, size), lambda i: (0, 0, 0)),
-        ],
+        ]
+        + [pl.BlockSpec(memory_space=pltpu.VMEM)] * (1 + slots),
         out_shape=[
             jax.ShapeDtypeStruct((leaves, rows, width), F32),
             jax.ShapeDtypeStruct((leaves, rows, width), BF16),
-            jax.ShapeDtypeStruct((slots, rows, size), BF16),
-        ],
+        ]
+        + [jax.ShapeDtypeStruct((rows, size), BF16)] * slots,
         scratch_shapes=[pltpu.VMEM((slots, rows, size), F32)],
         compiler_params=pltpu.CompilerParams(
             dimension_semantics=("arbitrary",), vmem_limit_bytes=VMEM_BYTES
@@ -70,7 +73,7 @@
             transcendentals=0,
         ),
         name="leaf_solve",
-    )(slot, rhs, inv, lower_mid)
+    )(parent, rhs, inv, lower_mid)
 
 
 def coupling_kernel(per_step, pattern_ref, round_ref, lower_ref, up_ref):
@@ -84,7 +87,7 @@
         left, right = [], []
         for i in range(per_step):
             weight = pattern_ref[step * per_step + i, k].astype(F32).astype(BF16)
-            left.append(round_ref[i] * weight)
+            left.append(round_ref[step * per_step + i] * weight)
             right.append(lower_ref[i, k])
         left = left[0] if per_step == 1 else jnp.concatenate(left, axis=1)
         right = right[0] if per_step == 1 else jnp.concatenate(right, axis=1)
@@ -100,10 +103,10 @@
         grid=(leaves // per_step,),
         in_specs=[
             pl.BlockSpec(memory_space=pltpu.SMEM),
-            pl.BlockSpec((per_step, rows, width), lambda i: (i, 0, 0)),
+            pl.BlockSpec(memory_space=pltpu.VMEM),
             pl.BlockSpec((per_step, kinds, size, width), lambda i: (i, 0, 0, 0)),
         ],
-        out_specs=pl.BlockSpec((kinds, rows, size), lambda i: (0, 0, 0)),
+        out_specs=pl.BlockSpec(memory_space=pltpu.VMEM),
         out_shape=jax.ShapeDtypeStruct((kinds, rows, size), F32),
         compiler_params=pltpu.CompilerParams(
             dimension_semantics=("arbitrary",), vmem_limit_bytes=VMEM_BYTES
@@ -156,7 +159,7 @@
     return spread(piece, "col")
 
 
-def per_device(
+def any_cols(
     leaf_rhs,
     leaf_inv,
     leaf_lower_mid,
@@ -183,13 +186,11 @@
     rhs_count, size = leaf_rhs.shape[1:]
     part = rhs_count // (4 * cols)
 
-    first = col if cols == 2 else 0
-    slot = lax.rem(leaf_parent - first + cols, cols)
-    leaf_solved, leaf_round, terms = leaf_solve(slot, leaf_rhs, leaf_inv, leaf_lower_mid, cols)
+    leaf_solved, leaf_round, *terms = leaf_solve(leaf_parent, leaf_rhs, leaf_inv, leaf_lower_mid, cols)
     if cols == 2:
         mid_part = terms[0].astype(F32) + swap(terms[1], "col", 0).astype(F32)
     else:
-        mid_part = scatter_sum(terms, "col")
+        mid_part = scatter_sum(jnp.stack(terms), "col")
     layer_up = leaf_coupling(leaf_pattern, leaf_round, leaf_lower_coupling)
     quarter = rhs_count // rows
     mid_sum = scatter_sum(mid_part.reshape(rows, quarter, size), "row")
@@ -241,6 +242,325 @@
     last = col_spread(last_solved).reshape(1, cols * part, width)
     top_all = col_spread(top_solved.reshape(rows, part, width)).swapaxes(0, 1).reshape(1, rhs_count, width)
     return (leaf_solved, mid_solved[None], top_all, jnp.concatenate([fronts, last], axis=0))
+
+
+def partners(block, moves):
+    blocks = block if isinstance(block, (list, tuple)) else [block] * len(moves)
+    arrived = []
+    for item, move in zip(blocks, moves):
+        axes = tuple(move)
+        sizes = [lax.axis_size(axis) for axis in axes]
+        route = []
+        for source in range(math.prod(sizes)):
+            place, rest = [], source
+            for count in reversed(sizes):
+                place.insert(0, rest % count)
+                rest //= count
+            target = 0
+            for at, count, axis in zip(place, sizes, axes):
+                target = target * count + (at ^ move[axis])
+            route.append((source, target))
+        arrived.append(lax.ppermute(item, axes, route))
+    return arrived
+
+
+def whole_call(kernel, name, operands, results, flops=0, scratch=(), scalars=0, after=()):
+    moved = sum(math.prod(a.shape) * a.dtype.itemsize for a in operands)
+    moved += sum(math.prod(shape) * jnp.dtype(kind).itemsize for shape, kind in results)
+    smem, vmem = pl.BlockSpec(memory_space=pltpu.SMEM), pl.BlockSpec(memory_space=pltpu.VMEM)
+
+    def body(*refs):
+        kernel(*refs[len(after) :])
+
+    return pl.pallas_call(
+        body,
+        in_specs=[pl.BlockSpec(memory_space=pl.ANY)] * len(after)
+        + [smem] * scalars
+        + [vmem] * (len(operands) - scalars),
+        out_specs=[vmem] * len(results),
+        out_shape=[jax.ShapeDtypeStruct(shape, kind) for shape, kind in results],
+        scratch_shapes=list(scratch),
+        compiler_params=pltpu.CompilerParams(vmem_limit_bytes=STEP_VMEM_BYTES),
+        cost_estimate=pl.CostEstimate(flops=flops, bytes_accessed=moved, transcendentals=0),
+        name=name,
+    )(*after, *operands)
+
+
+def piece(index, length):
+    return pl.ds(pl.multiple_of(index * length, length), length)
+
+
+def widened(*refs):
+    total = refs[0][...].astype(F32)
+    for ref in refs[1:]:
+        total = total + ref[...].astype(F32)
+    return total
+
+
+ROW_MOVES = [{"row": d} for d in (3, 2, 1)]
+
+
+def mid_pieces_kernel(terms_ref, other_ref, kept_ref, *given_refs):
+    row, length = lax.axis_index("row"), kept_ref.shape[0]
+    for d, ref in zip((0, 3, 2, 1), (kept_ref,) + given_refs):
+        at = piece(row ^ d, length)
+        ref[...] = (terms_ref[at].astype(F32) + other_ref[at].astype(F32)).astype(ref.dtype)
+
+
+def mid_total_kernel(rhs_ref, kept_ref, r1, r2, r3, ready_ref):
+    at = piece(lax.axis_index("row"), ready_ref.shape[0])
+    ready_ref[...] = (rhs_ref[0, at] - widened(kept_ref, r1, r2, r3)).astype(BF16)
+
+
+def mid_solve_kernel(
+    pattern_ref, p0, p3, p2, p1, inv_ref, lower_ref, up_ref,
+    solved_ref, top_ref, top_given_ref, late_ref, late_given_ref, rounded, total,
+):
+    row, col, core = lax.axis_index("row"), lax.axis_index("col"), lax.axis_index("gz") & 1
+    length, part = p0.shape[0], top_ref.shape[1]
+    for d, ref in zip((0, 3, 2, 1), (p0, p3, p2, p1)):
+        at = piece(row ^ d, length)
+        solved = times_transposed(ref[...], inv_ref[0])
+        solved_ref[at] = solved
+        rounded[at] = solved.astype(BF16)
+    total[...] = up_ref[0] + times_transposed(rounded[...], lower_ref[0, 0])
+    for i in range(4):
+        top_ref[i] = total[piece(i * 2 + col, part)]
+        top_given_ref[i] = total[piece(i * 2 + 1 - col, part)].astype(BF16)
+    for k in (1, 2):
+        weight = pattern_ref[0, k - 1].astype(F32)
+        total[...] = up_ref[k] + weight * times_transposed(rounded[...], lower_ref[0, k])
+        for half in (0, 1):
+            late_ref[k - 1, half] = total[piece(half * 2 + core, length)]
+            late_given_ref[k - 1, half] = total[piece(half * 2 + 1 - core, length)].astype(BF16)
+
+
+def repeat_top_kernel(inv_ref, share_ref):
+    half = lax.axis_index("col")
+    block = share_ref.shape[3]
+    for i in (0, 1):
+        share = inv_ref[0, :, piece(half * 2 + i, block)]
+        for r in range(share_ref.shape[0]):
+            share_ref[r, i] = share
+
+
+def whole_top_kernel(own_ref, other_ref, whole_ref):
+    half = lax.axis_index("col")
+    block = own_ref.shape[3]
+    for r in range(own_ref.shape[0]):
+        for i in (0, 1):
+            whole_ref[pl.ds(r * block, block), piece(half * 2 + i, block)] = own_ref[r, i]
+            whole_ref[pl.ds(r * block, block), piece((1 - half) * 2 + i, block)] = other_ref[r, i]
+
+
+def repeat_apex_kernel(inv_ref, lower_ref, share_ref):
+    gz, col = lax.axis_index("gz"), lax.axis_index("col")
+    pair, block = gz >> 1, share_ref.shape[3]
+    quarter = piece((gz & 1) * 2 + col, block)
+    shares = (inv_ref[pair, :, quarter], inv_ref[2, :, quarter], lower_ref[pair, quarter, :])
+    for i, share in enumerate(shares):
+        for r in range(share_ref.shape[0]):
+            share_ref[r, i] = share
+
+
+def whole_apex_kernel(own_ref, col_ref, core_ref, both_ref, front_ref, last_ref, lower_ref):
+    core, col = lax.axis_index("gz") & 1, lax.axis_index("col")
+    block = own_ref.shape[3]
+    for d, ref in enumerate((own_ref, col_ref, core_ref, both_ref)):
+        quarter = piece((core ^ d >> 1) * 2 + (col ^ d & 1), block)
+        for r in range(own_ref.shape[0]):
+            at = pl.ds(r * block, block)
+            front_ref[at, quarter] = ref[r, 0]
+            last_ref[at, quarter] = ref[r, 1]
+            lower_ref[quarter, at] = ref[r, 2]
+
+
+def on_first_row(rhs):
+    return jnp.where(lax.axis_index("row") == 0, rhs, 0.0)
+
+
+def top_blocks_kernel(rhs_ref, top_ref, other_ref, inv_ref, late_ref, late_other_ref, blocks_ref, out_ref, given_ref, ready):
+    col, part = lax.axis_index("col"), top_ref.shape[1]
+    block = blocks_ref.shape[2]
+    for i in range(4):
+        total = top_ref[i] + other_ref[i].astype(F32)
+        ready[pl.ds(i * part, part)] = (on_first_row(rhs_ref[0, piece(i * 2 + col, part)]) - total).astype(BF16)
+    solved = times_transposed(ready[...], inv_ref[...])
+    for r in range(blocks_ref.shape[0]):
+        blocks_ref[r] = solved[:, r * block : (r + 1) * block].astype(BF16)
+    for k in (0, 1):
+        for half in (0, 1):
+            for ref, side in ((out_ref, col), (given_ref, 1 - col)):
+                at = piece(side, part)
+                total = late_ref[k, half, at] + late_other_ref[k, half, at].astype(F32)
+                ref[k, half] = total.astype(ref.dtype)
+
+
+def top_up_kernel(blocks_ref, lower_ref, late_ref, late_other_ref, solved_ref, send_ref, kept_ref, given_ref, total):
+    core = lax.axis_index("gz") & 1
+    part = solved_ref.shape[1]
+    solved = sum(blocks_ref[r].astype(F32) for r in range(blocks_ref.shape[0]))
+    rounded = solved.astype(BF16)
+    for i in range(4):
+        solved_ref[i] = solved[i * part : (i + 1) * part]
+        send_ref[i] = rounded[i * part : (i + 1) * part]
+    for k in (0, 1):
+        total[...] = times_transposed(rounded, lower_ref[0, k])
+        for half in (0, 1):
+            late = late_ref[k, half] + late_other_ref[k, half].astype(F32)
+            kept_ref[k, half] = total[piece(half * 2 + core, part)] + late
+            given_ref[k, half] = total[piece(half * 2 + 1 - core, part)].astype(BF16)
+
+
+def apex_rows(rhs_ref, which, half, part):
+    core, col = lax.axis_index("gz") & 1, lax.axis_index("col")
+    return on_first_row(rhs_ref[which, piece(half * 4 + core * 2 + col, part)])
+
+
+def front_kernel(rhs_ref, kept_ref, other_ref, inv_ref, lower_ref, front_ref, last_ref, given_ref, ready, fronts, ups):
+    pair, part = lax.axis_index("gz") >> 1, last_ref.shape[0]
+    for half in (0, 1):
+        total = kept_ref[0, half] + other_ref[0, half].astype(F32)
+        ready[pl.ds(half * part, part)] = (apex_rows(rhs_ref, pair, half, part) - total).astype(BF16)
+    fronts[...] = times_transposed(ready[...], inv_ref[...])
+    front_ref[...] = fronts[piece(pair, part)].astype(BF16)
+    given_ref[0] = fronts[piece(1 - pair, part)].astype(BF16)
+    ups[...] = times_transposed(fronts[...].astype(BF16), lower_ref[...])
+    for half in (0, 1):
+        ups[pl.ds(half * part, part)] += kept_ref[1, half] + other_ref[1, half].astype(F32)
+    last_ref[...] = ups[piece(pair, part)]
+    given_ref[1] = ups[piece(1 - pair, part)].astype(BF16)
+
+
+def last_kernel(rhs_ref, inv_ref, front_ref, last_ref, other_ref, top_ref, other_top_ref, blocks_ref, top_all_ref):
+    pair, col, part = lax.axis_index("gz") >> 1, lax.axis_index("col"), last_ref.shape[0]
+    block = blocks_ref.shape[3]
+    ready = (apex_rows(rhs_ref, 2, pair, part) - (last_ref[...] + other_ref[1].astype(F32))).astype(BF16)
+    solved = times_transposed(ready, inv_ref[...])
+    for r in range(blocks_ref.shape[0]):
+        at = slice(r * block, (r + 1) * block)
+        blocks_ref[r, 2] = solved[:, at].astype(BF16)
+        blocks_ref[r, pair] = front_ref[:, at]
+        blocks_ref[r, 1 - pair] = other_ref[0, :, at]
+    for i in range(top_ref.shape[0]):
+        top_all_ref[0, piece(i * 2 + col, part)] = top_ref[i]
+        top_all_ref[0, piece(i * 2 + 1 - col, part)] = other_top_ref[i].astype(F32)
+
+
+def apex_sum_kernel(blocks_ref, solved_ref, send_ref):
+    solved = sum(blocks_ref[r].astype(F32) for r in range(blocks_ref.shape[0]))
+    solved_ref[...] = solved
+    send_ref[...] = solved.astype(BF16)
+
+
+def place_apex_kernel(solved_ref, other_ref, apex_ref):
+    col, part = lax.axis_index("col"), solved_ref.shape[1]
+    for k in range(3):
+        apex_ref[k, piece(col, part)] = solved_ref[k]
+        apex_ref[k, piece(1 - col, part)] = other_ref[k].astype(F32)
+
+
+def two_cols(
+    leaf_rhs,
+    leaf_inv,
+    leaf_lower_mid,
+    leaf_lower_coupling,
+    leaf_parent,
+    leaf_pattern,
+    mid_rhs,
+    parent_diagonal_inverse,
+    mid_lower,
+    mid_pattern,
+    top_rhs,
+    top_inv,
+    top_lower,
+    apex_rhs,
+    apex_inv,
+    apex_lower,
+):
+    count, size = leaf_rhs.shape[1:]
+    width = leaf_inv.shape[1]
+    quarter, part = count // 4, count // 8
+
+    rows = lax.axis_size("row")
+    leaf_solved, leaf_round, terms, other_terms = leaf_solve(leaf_parent, leaf_rhs, leaf_inv, leaf_lower_mid, 2)
+    (other_terms,) = partners(other_terms, [{"col": 1}])
+    layer_up = leaf_coupling(leaf_pattern, leaf_round, leaf_lower_coupling)
+
+    (share,) = whole_call(
+        repeat_top_kernel, "repeat_top", [top_inv], [((rows, 2, width, width), BF16)], after=[leaf_round]
+    )
+    top_share = exchange(share, "row")
+
+    kept, *given = whole_call(
+        mid_pieces_kernel, "mid_pieces", [terms, other_terms],
+        [((quarter, size), F32)] + [((quarter, size), BF16)] * 3,
+        after=[top_share],
+    )
+    arrived = partners(given, ROW_MOVES)
+    (top_other,) = partners(top_share, [{"col": 1}])
+    (ready,) = whole_call(mid_total_kernel, "mid_total", [mid_rhs, kept, *arrived], [((quarter, size), BF16)])
+    arrived = partners(ready, ROW_MOVES)
+    (top_whole,) = whole_call(whole_top_kernel, "whole_top", [top_share, top_other], [((size, size), BF16)])
+    mid_solved, kept, given, late_kept, late_given = whole_call(
+        mid_solve_kernel, "mid_solve", [mid_pattern, ready, *arrived, parent_diagonal_inverse, mid_lower, layer_up],
+        [((count, width), F32), ((4, part, size), F32), ((4, part, size), BF16)]
+        + [((2, 2, quarter, size), F32), ((2, 2, quarter, size), BF16)],
+        flops=8 * count * size * width,
+        scratch=[pltpu.VMEM((count, width), BF16), pltpu.VMEM((count, size), F32)],
+        scalars=1,
+        after=[top_whole],
+    )
+
+    (other,) = partners(given, [{"col": 1}])
+    (late_other,) = partners(late_given, [{"gz": 1}])
+    (share,) = whole_call(
+        repeat_apex_kernel, "repeat_apex", [apex_inv, apex_lower], [((rows, 3, width, width), BF16)], after=[given]
+    )
+    apex_share = exchange(share, "row")
+    blocks, late_kept, late_given = whole_call(
+        top_blocks_kernel, "top_blocks", [top_rhs, kept, other, top_whole, late_kept, late_other],
+        [((rows, count // 2, width), BF16), ((2, 2, part, size), F32), ((2, 2, part, size), BF16)],
+        flops=count * size * size,
+        scratch=[pltpu.VMEM((count // 2, size), BF16)],
+    )
+    blocks = exchange(blocks, "row")
+    (late_other,) = partners(late_given, [{"col": 1}])
+    apex_share, _ = lax.optimization_barrier((apex_share, other))
+    (apex_col,) = partners(apex_share, [{"col": 1}])
+    apex_share, apex_col, blocks = lax.optimization_barrier((apex_share, apex_col, blocks))
+    top_solved, top_send, kept, given = whole_call(
+        top_up_kernel, "top_up", [blocks, top_lower, late_kept, late_other],
+        [((4, part, width), F32), ((4, part, width), BF16), ((2, 2, part, size), F32), ((2, 2, part, size), BF16)],
+        flops=2 * count * size * width,
+        scratch=[pltpu.VMEM((4 * part, size), F32)],
+    )
+    (other,) = partners(given, [{"gz": 1}])
+    (other_top,) = partners(top_send, [{"col": 1}])
+
+    (apex_core,) = partners(apex_share, [{"gz": 1}])
+    (apex_both,) = partners(apex_col, [{"gz": 1}])
+    front_whole, last_whole, lower_whole = whole_call(
+        whole_apex_kernel, "whole_apex", [apex_share, apex_col, apex_core, apex_both], [((size, size), BF16)] * 3
+    )
+    front, last, given = whole_call(
+        front_kernel, "front", [apex_rhs, kept, other, front_whole, lower_whole],
+        [((part, size), BF16), ((part, size), F32), ((2, part, size), BF16)],
+        flops=count * size * size,
+        scratch=[pltpu.VMEM((2 * part, size), BF16)] + [pltpu.VMEM((2 * part, size), F32)] * 2,
+    )
+    (other,) = partners(given, [{"gz": 2}])
+    blocks, top_all = whole_call(
+        last_kernel, "last", [apex_rhs, last_whole, front, last, other, top_solved, other_top],
+        [((rows, 3, part, width), BF16), ((1, count, width), F32)],
+        flops=count * size * size // 4,
+    )
+    solved, send = whole_call(
+        apex_sum_kernel, "apex_sum", [exchange(blocks, "row")], [((3, part, width), F32), ((3, part, width), BF16)]
+    )
+    (other,) = partners(send, [{"col": 1}])
+    (apex,) = whole_call(place_apex_kernel, "place_apex", [solved, other], [((3, 2 * part, width), F32)])
+    return (leaf_solved, mid_solved[None], top_all, apex)
 
 
 def solution(mesh):
@@ -263,7 +583,7 @@
         P(None, None, "row"),
     )
     return jax.shard_map(
-        per_device,
+        two_cols if mesh.shape["col"] == 2 else any_cols,
         mesh=mesh,
         in_specs=placed,
         out_specs=(

time: 115 us -> 109 us (0.948)
  waiting for transfers between devices: 48.2 us -> 28.3 us
  blocking collectives: 0 us -> 16.7 us
  Pallas kernels: 7.77 us -> 18.6 us
  matrix products: 7.79 us -> 0 us
  starting transfers between devices: 34.6 us -> 29.8 us
  other arithmetic: 4.35 us -> 0 us
  local copies, waits for them, and re-layouts: 10.5 us -> 13.4 us
    all_to_all x7 -> x2, waiting for transfers between devices: 35.9 us -> 11.3 us  [exchange(): return lax.all_to_all(pieces, axis, split_axis=0, concat_axis=0, tiled=True)]
    all_to_all x0 -> x2, blocking collectives: none -> 16.7 us  [exchange(): return lax.all_to_all(pieces, axis, split_axis=0, concat_axis=0, tiled=True)]
    all_to_all x7 -> x2, starting transfers between devices: 26.2 us -> 9.88 us  [exchange(): return lax.all_to_all(pieces, axis, split_axis=0, concat_axis=0, tiled=True)]
    ppermute x9 -> x18, starting transfers between devices: 8.32 us -> 19.9 us  [partners(): arrived.append(lax.ppermute(item, axes, route))]
    unnamed x23 -> x53, local copies, waits for them, and re-layouts: 4.47 us -> 13.4 us
    dot_general x10 -> x0, matrix products: 7.79 us -> none  [times_transposed(): lax.dot_general(left, right, (((1,), (1,)), ((), ())), preferred_element_...]
    pallas_call x0 -> x13, Pallas kernels: none -> 7.4 us  [whole_call(): pl.pallas_call(body, in_specs=[pl.BlockSpec(memory_space=pl.ANY)] * len(a...]
    ppermute x9 -> x18, waiting for transfers between devices: 12.3 us -> 17.1 us  [partners(): arrived.append(lax.ppermute(item, axes, route))]
  transfers between devices with their start and end apart: 16 -> 20, of which waited for: 12 -> 9; matrix products, arithmetic and copies ran while one was open for 8% -> 1% of each run, Pallas kernels for 2% -> 7%
where the time goes in v2:
time: 109 us; the launch traced here: 108 us
  starting transfers between devices  29.8 us (27%)
  waiting for transfers between devices  28.3 us (26%)
  Pallas kernels  18.6 us (17%)
  blocking collectives  16.7 us (15%)
  local copies, waits for them, and re-layouts  13.4 us (12%)
    ppermute x18, starting transfers between devices, partners(): arrived.append(lax.ppermute(item, axes, route))  19.9 us
    ppermute x18, waiting for transfers between devices, partners(): arrived.append(lax.ppermute(item, axes, route))  17.1 us
    all_to_all x2, blocking collectives, exchange(): return lax.all_to_all(pieces, axis, split_axis=0, concat_axis=0, tiled=True)  16.7 us
    unnamed x53, local copies, waits for them, and re-layouts  13.4 us
    all_to_all x2, waiting for transfers between devices, exchange(): return lax.all_to_all(pieces, axis, split_axis=0, concat_axis=0, tiled=True)  11.3 us
    all_to_all x2, starting transfers between devices, exchange(): return lax.all_to_all(pieces, axis, split_axis=0, concat_axis=0, tiled=True)  9.88 us
    pallas_call x13, Pallas kernels, whole_call(): pl.pallas_call(body, in_specs=[pl.BlockSpec(memory_space=pl.ANY)] * len(a...  7.4 us
    pallas_call x1, Pallas kernels, leaf_solve(): pl.pallas_call(functools.partial(leaf_kernel, per_step, slots), grid=(lea...  6.14 us
  transfers between devices with their start and end apart: 20, of which 9 were waited for; matrix products, arithmetic and copies ran while one was open for 1% of the time, Pallas kernels for 7%

profile of v2, /device:TPU:0, one launch (start us, length us, event | category | flops | bytes accessed | tf_op | source)
XLA Modules:
  0.0 107.7 jit_solution(2627188661418646641)
XLA Ops:
  0.7 6.1 %leaf_solve.1 = (f32[8,256,128]{2,1,0:T(8,128)}, bf16[8,256,128]{2,1,0:T(8,128)(2,1)}, bf16[256,512]{1,0:T(8,128)(2,1)}, bf16[256,512]{1,0:T(8,128)(2,1)}) custom-call(s32[8]{0:T(128)} %parent_ref.1, f32[8,256,512]{2,1,0:T(8,128)} %rhs_ref.1, bf16[8,128,512]{2,1,0:T(8,128)(2,1)} %inv_ref.1, bf16[8,512,128]{2,1,0:T(8,128)(2,1)} %mid_ref.1), custom_call_target="tpu_custom_call" | custom-call | flops 536870912 | bytes 7864320 | tf_op jit(solution)/shard_map/leaf_solve/pallas_call | solution.py:48
  8.6 6.3 %all-to-all-start = ((bf16[4,2,128,128]{3,2,1,0:T(8,128)(2,1)}), bf16[4,2,128,128]{3,2,1,0:T(8,128)(2,1)S(1)}, u32[]{:S(2)}, u32[]{:S(2)}) async-start(bf16[4,2,128,128]{3,2,1,0:T(8,128)(2,1)} %repeat_top.1), calls=%async_computation | async-start | bytes 524288 | tf_op jit(solution)/shard_map/all_to_all | solution.py:136
  14.9 1.5 %collective-permute-start.1 = (bf16[256,512]{1,0:T(8,128)(2,1)}, bf16[256,512]{1,0:T(8,128)(2,1)S(1)}, u32[]{:S(2)}, u32[]{:S(2)}) collective-permute-start(bf16[256,512]{1,0:T(8,128)(2,1)} %get-tuple-element.41), channel_id=1, source_target_pairs={{0,1},{1,0},{2,3},{3,2},{4,5},{5,4},{6,7},{7,6},{8,9},{9,8},{10,11... | collective-permute-start | bytes 786440 | tf_op jit(solution)/shard_map/ppermute | solution.py:263
  16.4 7.4 %all-to-all-done.refs_0_ = bf16[4,2,128,128]{3,2,1,0:T(8,128)(2,1)S(1)} async-done(((bf16[4,2,128,128]{3,2,1,0:T(8,128)(2,1)}), bf16[4,2,128,128]{3,2,1,0:T(8,128)(2,1)S(1)}, u32[]{:S(2)}, u32[]{:S(2)}) %all-to-all-start) | async-done | bytes 262176 | tf_op jit(solution)/shard_map/all_to_all | solution.py:136
  23.8 1.5 %collective-permute-start = (bf16[4,2,128,128]{3,2,1,0:T(8,128)(2,1)S(1)}, bf16[4,2,128,128]{3,2,1,0:T(8,128)(2,1)S(1)}, u32[]{:S(2)}, u32[]{:S(2)}) collective-permute-start(bf16[4,2,128,128]{3,2,1,0:T(8,128)(2,1)S(1)} %all-to-all-done.refs_0_), channel_id=1, source_target_pairs={{0,1},{1,0},{2,3},{3,2},{4,5},{5,4},{6,7},{7,6},{8,9},{9,8},{10,11... | collective-permute-start | bytes 786440 | tf_op jit(solution)/shard_map/ppermute | solution.py:263
  26.4 1.5 %collective-permute-start.2 = (bf16[64,512]{1,0:T(8,128)(2,1)S(1)}, bf16[64,512]{1,0:T(8,128)(2,1)S(1)}, u32[]{:S(2)}, u32[]{:S(2)}) collective-permute-start(bf16[64,512]{1,0:T(8,128)(2,1)S(1)} %get-tuple-element.43), channel_id=1, source_target_pairs={{0,6},{2,4},{4,2},{6,0},{1,7},{3,5},{5,3},{7,1},{8,14},{10,12},{12... | collective-permute-start | bytes 196616 | tf_op jit(solution)/shard_map/ppermute | solution.py:263
  28.2 2.6 %collective-permute-start.4 = (bf16[64,512]{1,0:T(8,128)(2,1)S(1)}, bf16[64,512]{1,0:T(8,128)(2,1)S(1)}, u32[]{:S(2)}, u32[]{:S(2)}) collective-permute-start(bf16[64,512]{1,0:T(8,128)(2,1)S(1)} %get-tuple-element.45), channel_id=1, source_target_pairs={{0,2},{2,0},{4,6},{6,4},{1,3},{3,1},{5,7},{7,5},{8,10},{10,8},{12,... | collective-permute-start | bytes 196616 | tf_op jit(solution)/shard_map/ppermute | solution.py:263
  32.5 1.4 %collective-permute-done.3.refs_3_ = bf16[64,512]{1,0:T(8,128)(2,1)S(1)} collective-permute-done((bf16[64,512]{1,0:T(8,128)(2,1)S(1)}, bf16[64,512]{1,0:T(8,128)(2,1)S(1)}, u32[]{:S(2)}, u32[]{:S(2)}) %collective-permute-start.3) | collective-permute-done | bytes 65568 | tf_op jit(solution)/shard_map/ppermute | solution.py:263
  34.0 1.9 %collective-permute-start.7 = (bf16[64,512]{1,0:T(8,128)(2,1)S(1)}, bf16[64,512]{1,0:T(8,128)(2,1)S(1)}, u32[]{:S(2)}, u32[]{:S(2)}) collective-permute-start(bf16[64,512]{1,0:T(8,128)(2,1)S(1)} %mid_total.1.refs_2_), channel_id=1, source_target_pairs={{0,2},{2,0},{4,6},{6,4},{1,3},{3,1},{5,7},{7,5},{8,10},{10,8},{12,... | collective-permute-start | bytes 196616 | tf_op jit(solution)/shard_map/ppermute | solution.py:263
  36.9 1.5 %collective-permute-start.5 = (bf16[64,512]{1,0:T(8,128)(2,1)S(1)}, bf16[64,512]{1,0:T(8,128)(2,1)S(1)}, u32[]{:S(2)}, u32[]{:S(2)}) collective-permute-start(bf16[64,512]{1,0:T(8,128)(2,1)S(1)} %mid_total.1.refs_2_), channel_id=1, source_target_pairs={{0,6},{2,4},{4,2},{6,0},{1,7},{3,5},{5,3},{7,1},{8,14},{10,12},{12... | collective-permute-start | bytes 196616 | tf_op jit(solution)/shard_map/ppermute | solution.py:263
  38.4 5.1 %leaf_coupling.1.refs_8_ = f32[3,256,512]{2,1,0:T(8,128)} custom-call(s32[8,3]{1,0:T(8,128)} %copy.20.pattern_ref, bf16[8,256,128]{2,1,0:T(8,128)(2,1)} %get-tuple-element.39.refs_0_.round_ref, bf16[8,3,512,128]{3,2,1,0:T(8,128)(2,1)} %lower_ref.1), custom_call_target="tpu_custom_call" | custom-call | flops 805306368 | bytes 5242880 | tf_op jit(solution)/shard_map/leaf_coupling/pallas_call | solution.py:101
  45.6 1.4 %copy-done.1 = f32[3,256,512]{2,1,0:T(8,128)S(1)} copy-done((f32[3,256,512]{2,1,0:T(8,128)S(1)}, f32[3,256,512]{2,1,0:T(8,128)}, u32[]{:S(2)}) %copy-start.1) | copy-done | bytes 1572888
  49.5 1.9 %mid_solve.1 = (f32[256,128]{1,0:T(8,128)}, f32[4,32,512]{2,1,0:T(8,128)S(1)}, bf16[4,32,512]{2,1,0:T(8,128)(2,1)S(1)}, f32[2,2,64,512]{3,2,1,0:T(8,128)S(1)}, bf16[2,2,64,512]{3,2,1,0:T(8,128)(2,1)S(1)}) custom-call(bf16[512,512]{1,0:T(8,128)(2,1)S(1)} %whole_top.1.refs_0_.refs_3_, s32[1,2]{1,0:T(1,128)S(1)} %copy-done.23, ...), custom_call_target="tpu_custom_call" | custom-call | flops 134217728 | bytes 3670024 | tf_op jit(solution)/shard_map/mid_solve/pallas_call | solution.py:275
  53.7 3.6 %all-to-all-start.1 = ((bf16[4,3,128,128]{3,2,1,0:T(8,128)(2,1)}), bf16[4,3,128,128]{3,2,1,0:T(8,128)(2,1)S(1)}, u32[]{:S(2)}, u32[]{:S(2)}) async-start(bf16[4,3,128,128]{3,2,1,0:T(8,128)(2,1)} %repeat_apex.1), calls=%async_computation.1 | async-start | bytes 786432 | tf_op jit(solution)/shard_map/all_to_all | solution.py:136
  57.2 1.9 %collective-permute-start.8 = (bf16[4,32,512]{2,1,0:T(8,128)(2,1)}, bf16[4,32,512]{2,1,0:T(8,128)(2,1)S(1)}, u32[]{:S(2)}, u32[]{:S(2)}) collective-permute-start(bf16[4,32,512]{2,1,0:T(8,128)(2,1)} %copy-done.16), channel_id=1, source_target_pairs={{0,1},{1,0},{2,3},{3,2},{4,5},{5,4},{6,7},{7,6},{8,9},{9,8},{10,11... | collective-permute-start | bytes 393224 | tf_op jit(solution)/shard_map/ppermute | solution.py:263
  59.1 3.3 %collective-permute-done.8.refs_2_ = bf16[4,32,512]{2,1,0:T(8,128)(2,1)S(1)} collective-permute-done((bf16[4,32,512]{2,1,0:T(8,128)(2,1)}, bf16[4,32,512]{2,1,0:T(8,128)(2,1)S(1)}, u32[]{:S(2)}, u32[]{:S(2)}) %collective-permute-start.8) | collective-permute-done | bytes 131104 | tf_op jit(solution)/shard_map/ppermute | solution.py:263
  63.1 3.9 %all-to-all-done.1.refs_0_ = bf16[4,3,128,128]{3,2,1,0:T(8,128)(2,1)S(1)} async-done(((bf16[4,3,128,128]{3,2,1,0:T(8,128)(2,1)}), bf16[4,3,128,128]{3,2,1,0:T(8,128)(2,1)S(1)}, u32[]{:S(2)}, u32[]{:S(2)}) %all-to-all-start.1) | async-done | bytes 393248 | tf_op jit(solution)/shard_map/all_to_all | solution.py:136
  69.9 1.3 %top_blocks.1 = (bf16[4,128,128]{2,1,0:T(8,128)(2,1)S(1)}, f32[2,2,32,512]{3,2,1,0:T(8,128)S(1)}, bf16[2,2,32,512]{3,2,1,0:T(8,128)(2,1)S(1)}) custom-call(f32[1,256,512]{2,1,0:T(8,128)S(1)} %copy-done.3, f32[4,32,512]{2,1,0:T(8,128)S(1)} %copy-done.9, bf16[4,32,512]{2,1,0:T(8,128)(2,1)S(1)} %copy-done.15, bf16[512,512]{1,0:T(8,128)(2,1)S(1)} %whole_top.1.refs_0_.refs_3_, ...), custom_call_target="tpu_custom_call" | custom-call | flops 67108864 | bytes 2752512 | tf_op jit(solution)/shard_map/top_blocks/pallas_call | solution.py:275
  71.1 8.5 %all_to_all.20.refs_0_ = bf16[4,128,128]{2,1,0:T(8,128)(2,1)S(1)} all-to-all(bf16[4,128,128]{2,1,0:T(8,128)(2,1)S(1)} %get-tuple-element.52), channel_id=1, replica_groups=mesh['gz'=4,'row'=4,'col'=2] {'row'}, dimensions={0} | all-to-all | bytes 262144 | tf_op jit(solution)/shard_map/all_to_all | solution.py:136
  81.1 4.5 %collective-permute-done.13.refs_3_ = bf16[2,2,32,512]{3,2,1,0:T(8,128)(2,1)S(1)} collective-permute-done((bf16[2,2,32,512]{3,2,1,0:T(8,128)(2,1)S(1)}, bf16[2,2,32,512]{3,2,1,0:T(8,128)(2,1)S(1)}, u32[]{:S(2)}, u32[]{:S(2)}) %collective-permute-start.13) | collective-permute-done | bytes 131104 | tf_op jit(solution)/shard_map/ppermute | solution.py:263
  88.7 1.6 %collective-permute-start.15 = (bf16[2,32,512]{2,1,0:T(8,128)(2,1)S(1)}, bf16[2,32,512]{2,1,0:T(8,128)(2,1)S(1)}, u32[]{:S(2)}, u32[]{:S(2)}) collective-permute-start(bf16[2,32,512]{2,1,0:T(8,128)(2,1)S(1)} %get-tuple-element.65), channel_id=1, source_target_pairs={{0,16},{8,24},{16,0},{24,8},{1,17},{9,25},{17,1},{25,9},{2,18},{10... | collective-permute-start | bytes 196616 | tf_op jit(solution)/shard_map/ppermute | solution.py:263
  91.2 3.0 %collective-permute-done.16.refs_6_ = bf16[4,32,128]{2,1,0:T(8,128)(2,1)S(1)} collective-permute-done((bf16[4,32,128]{2,1,0:T(8,128)(2,1)S(1)}, bf16[4,32,128]{2,1,0:T(8,128)(2,1)S(1)}, u32[]{:S(2)}, u32[]{:S(2)}) %collective-permute-start.16) | collective-permute-done | bytes 32800 | tf_op jit(solution)/shard_map/ppermute | solution.py:263
  94.9 8.3 %all_to_all.21.refs_0_ = bf16[4,3,32,128]{3,2,1,0:T(8,128)(2,1)S(1)} all-to-all(bf16[4,3,32,128]{3,2,1,0:T(8,128)(2,1)S(1)} %get-tuple-element.69), channel_id=1, replica_groups=mesh['gz'=4,'row'=4,'col'=2] {'row'}, dimensions={0} | all-to-all | bytes 196608 | tf_op jit(solution)/shard_map/all_to_all | solution.py:136
  104.2 2.9 %collective-permute-done.17.refs_1_ = bf16[3,32,128]{2,1,0:T(8,128)(2,1)S(1)} collective-permute-done((bf16[3,32,128]{2,1,0:T(8,128)(2,1)S(1)}, bf16[3,32,128]{2,1,0:T(8,128)(2,1)S(1)}, u32[]{:S(2)}, u32[]{:S(2)}) %collective-permute-start.17) | collective-permute-done | bytes 24608 | tf_op jit(solution)/shard_map/ppermute | solution.py:263
  (86 shorter events, 24.4 us)
Async XLA Ops:
  0.6 30.2 %copy-start.25 = (s32[8,3]{0,1:T(4,128)S(1)}, s32[8,3]{0,1:T(4,128)}, u32[]{:S(2)}) copy-start(s32[8,3]{0,1:T(4,128)} %param.21) | copy-start | bytes 292
  0.7 33.3 %copy-start.4 = (f32[1,256,512]{2,1,0:T(8,128)S(1)}, f32[1,256,512]{2,1,0:T(8,128)}, u32[]{:S(2)}) copy-start(f32[1,256,512]{2,1,0:T(8,128)} %refs_0_.4) | copy-start | bytes 1572868
  8.6 15.2 %all-to-all-start = ((bf16[4,2,128,128]{3,2,1,0:T(8,128)(2,1)}), bf16[4,2,128,128]{3,2,1,0:T(8,128)(2,1)S(1)}, u32[]{:S(2)}, u32[]{:S(2)}) async-start(bf16[4,2,128,128]{3,2,1,0:T(8,128)(2,1)} %repeat_top.1), calls=%async_computation | async-start | bytes 524288 | tf_op jit(solution)/shard_map/all_to_all | solution.py:136
  14.9 10.4 %collective-permute-start.1 = (bf16[256,512]{1,0:T(8,128)(2,1)}, bf16[256,512]{1,0:T(8,128)(2,1)S(1)}, u32[]{:S(2)}, u32[]{:S(2)}) collective-permute-start(bf16[256,512]{1,0:T(8,128)(2,1)} %get-tuple-element.41), channel_id=1, source_target_pairs={{0,1},{1,0},{2,3},{3,2},{4,5},{5,4},{6,7},{7,6},{8,9},{9,8},{10,11... | collective-permute-start | bytes 786440 | tf_op jit(solution)/shard_map/ppermute | solution.py:263
  23.8 19.7 %collective-permute-start = (bf16[4,2,128,128]{3,2,1,0:T(8,128)(2,1)S(1)}, bf16[4,2,128,128]{3,2,1,0:T(8,128)(2,1)S(1)}, u32[]{:S(2)}, u32[]{:S(2)}) collective-permute-start(bf16[4,2,128,128]{3,2,1,0:T(8,128)(2,1)S(1)} %all-to-all-done.refs_0_), channel_id=1, source_target_pairs={{0,1},{1,0},{2,3},{3,2},{4,5},{5,4},{6,7},{7,6},{8,9},{9,8},{10,11... | collective-permute-start | bytes 786440 | tf_op jit(solution)/shard_map/ppermute | solution.py:263
  26.4 6.2 %collective-permute-start.2 = (bf16[64,512]{1,0:T(8,128)(2,1)S(1)}, bf16[64,512]{1,0:T(8,128)(2,1)S(1)}, u32[]{:S(2)}, u32[]{:S(2)}) collective-permute-start(bf16[64,512]{1,0:T(8,128)(2,1)S(1)} %get-tuple-element.43), channel_id=1, source_target_pairs={{0,6},{2,4},{4,2},{6,0},{1,7},{3,5},{5,3},{7,1},{8,14},{10,12},{12... | collective-permute-start | bytes 196616 | tf_op jit(solution)/shard_map/ppermute | solution.py:263
  27.8 6.1 %collective-permute-start.3 = (bf16[64,512]{1,0:T(8,128)(2,1)S(1)}, bf16[64,512]{1,0:T(8,128)(2,1)S(1)}, u32[]{:S(2)}, u32[]{:S(2)}) collective-permute-start(bf16[64,512]{1,0:T(8,128)(2,1)S(1)} %get-tuple-element.44), channel_id=1, source_target_pairs={{0,4},{2,6},{4,0},{6,2},{1,5},{3,7},{5,1},{7,3},{8,12},{10,14},{12... | collective-permute-start | bytes 196616 | tf_op jit(solution)/shard_map/ppermute | solution.py:263
  28.2 5.7 %collective-permute-start.4 = (bf16[64,512]{1,0:T(8,128)(2,1)S(1)}, bf16[64,512]{1,0:T(8,128)(2,1)S(1)}, u32[]{:S(2)}, u32[]{:S(2)}) collective-permute-start(bf16[64,512]{1,0:T(8,128)(2,1)S(1)} %get-tuple-element.45), channel_id=1, source_target_pairs={{0,2},{2,0},{4,6},{6,4},{1,3},{3,1},{5,7},{7,5},{8,10},{10,8},{12,... | collective-permute-start | bytes 196616 | tf_op jit(solution)/shard_map/ppermute | solution.py:263
  34.0 9.7 %collective-permute-start.7 = (bf16[64,512]{1,0:T(8,128)(2,1)S(1)}, bf16[64,512]{1,0:T(8,128)(2,1)S(1)}, u32[]{:S(2)}, u32[]{:S(2)}) collective-permute-start(bf16[64,512]{1,0:T(8,128)(2,1)S(1)} %mid_total.1.refs_2_), channel_id=1, source_target_pairs={{0,2},{2,0},{4,6},{6,4},{1,3},{3,1},{5,7},{7,5},{8,10},{10,8},{12,... | collective-permute-start | bytes 196616 | tf_op jit(solution)/shard_map/ppermute | solution.py:263
  35.9 8.5 %collective-permute-start.6 = (bf16[64,512]{1,0:T(8,128)(2,1)S(1)}, bf16[64,512]{1,0:T(8,128)(2,1)S(1)}, u32[]{:S(2)}, u32[]{:S(2)}) collective-permute-start(bf16[64,512]{1,0:T(8,128)(2,1)S(1)} %mid_total.1.refs_2_), channel_id=1, source_target_pairs={{0,4},{2,6},{4,0},{6,2},{1,5},{3,7},{5,1},{7,3},{8,12},{10,14},{12... | collective-permute-start | bytes 196616 | tf_op jit(solution)/shard_map/ppermute | solution.py:263
  36.9 8.0 %collective-permute-start.5 = (bf16[64,512]{1,0:T(8,128)(2,1)S(1)}, bf16[64,512]{1,0:T(8,128)(2,1)S(1)}, u32[]{:S(2)}, u32[]{:S(2)}) collective-permute-start(bf16[64,512]{1,0:T(8,128)(2,1)S(1)} %mid_total.1.refs_2_), channel_id=1, source_target_pairs={{0,6},{2,4},{4,2},{6,0},{1,7},{3,5},{5,3},{7,1},{8,14},{10,12},{12... | collective-permute-start | bytes 196616 | tf_op jit(solution)/shard_map/ppermute | solution.py:263
  43.5 24.5 %copy-start.3 = (f32[1,256,512]{2,1,0:T(8,128)S(1)}, f32[1,256,512]{2,1,0:T(8,128)}, u32[]{:S(2)}) copy-start(f32[1,256,512]{2,1,0:T(8,128)} %refs_0_.5) | copy-start | bytes 1572868
  52.8 35.4 %copy-start = (f32[3,256,512]{2,1,0:T(8,128)S(1)}, f32[3,256,512]{2,1,0:T(8,128)}, u32[]{:S(2)}) copy-start(f32[3,256,512]{2,1,0:T(8,128)} %refs_0_.7) | copy-start | bytes 4718596
  53.7 13.3 %all-to-all-start.1 = ((bf16[4,3,128,128]{3,2,1,0:T(8,128)(2,1)}), bf16[4,3,128,128]{3,2,1,0:T(8,128)(2,1)S(1)}, u32[]{:S(2)}, u32[]{:S(2)}) async-start(bf16[4,3,128,128]{3,2,1,0:T(8,128)(2,1)} %repeat_apex.1), calls=%async_computation.1 | async-start | bytes 786432 | tf_op jit(solution)/shard_map/all_to_all | solution.py:136
  57.2 5.2 %collective-permute-start.8 = (bf16[4,32,512]{2,1,0:T(8,128)(2,1)}, bf16[4,32,512]{2,1,0:T(8,128)(2,1)S(1)}, u32[]{:S(2)}, u32[]{:S(2)}) collective-permute-start(bf16[4,32,512]{2,1,0:T(8,128)(2,1)} %copy-done.16), channel_id=1, source_target_pairs={{0,1},{1,0},{2,3},{3,2},{4,5},{5,4},{6,7},{7,6},{8,9},{9,8},{10,11... | collective-permute-start | bytes 393224 | tf_op jit(solution)/shard_map/ppermute | solution.py:263
  59.1 8.9 %collective-permute-start.10 = (bf16[2,2,64,512]{3,2,1,0:T(8,128)(2,1)}, bf16[2,2,64,512]{3,2,1,0:T(8,128)(2,1)}, u32[]{:S(2)}, u32[]{:S(2)}) collective-permute-start(bf16[2,2,64,512]{3,2,1,0:T(8,128)(2,1)} %copy-done.24), channel_id=1, source_target_pairs={{0,8},{8,0},{16,24},{24,16},{1,9},{9,1},{17,25},{25,17},{2,10},{10... | collective-permute-start | bytes 786440 | tf_op jit(solution)/shard_map/ppermute | solution.py:263
  66.9 12.7 %collective-permute-start.9 = (bf16[4,3,128,128]{3,2,1,0:T(8,128)(2,1)S(1)}, bf16[4,3,128,128]{3,2,1,0:T(8,128)(2,1)S(1)}, u32[]{:S(2)}, u32[]{:S(2)}) collective-permute-start(bf16[4,3,128,128]{3,2,1,0:T(8,128)(2,1)S(1)} %all-to-all-done.1.refs_0_), channel_id=1, source_target_pairs={{0,1},{1,0},{2,3},{3,2},{4,5},{5,4},{6,7},{7,6},{8,9},{9,8},{10,11... | collective-permute-start | bytes 1179656 | tf_op jit(solution)/shard_map/ppermute | solution.py:263
  79.6 7.2 %collective-permute-start.11 = (bf16[4,3,128,128]{3,2,1,0:T(8,128)(2,1)S(1)}, bf16[4,3,128,128]{3,2,1,0:T(8,128)(2,1)S(1)}, u32[]{:S(2)}, u32[]{:S(2)}) collective-permute-start(bf16[4,3,128,128]{3,2,1,0:T(8,128)(2,1)S(1)} %all-to-all-done.1.refs_0_), channel_id=1, source_target_pairs={{0,8},{8,0},{16,24},{24,16},{1,9},{9,1},{17,25},{25,17},{2,10},{10... | collective-permute-start | bytes 1179656 | tf_op jit(solution)/shard_map/ppermute | solution.py:263
  79.6 7.3 %collective-permute-start.12 = (bf16[4,3,128,128]{3,2,1,0:T(8,128)(2,1)S(1)}, bf16[4,3,128,128]{3,2,1,0:T(8,128)(2,1)S(1)}, u32[]{:S(2)}, u32[]{:S(2)}) collective-permute-start(bf16[4,3,128,128]{3,2,1,0:T(8,128)(2,1)S(1)} %collective-permute-done.9.refs_1_), channel_id=1, source_target_pairs={{0,8},{8,0},{16,24},{24,16},{1,9},{9,1},{17,25},{25,17},{2,10},{10... | collective-permute-start | bytes 1179656 | tf_op jit(solution)/shard_map/ppermute | solution.py:263
  80.1 5.4 %collective-permute-start.13 = (bf16[2,2,32,512]{3,2,1,0:T(8,128)(2,1)S(1)}, bf16[2,2,32,512]{3,2,1,0:T(8,128)(2,1)S(1)}, u32[]{:S(2)}, u32[]{:S(2)}) collective-permute-start(bf16[2,2,32,512]{3,2,1,0:T(8,128)(2,1)S(1)} %get-tuple-element.58), channel_id=1, source_target_pairs={{0,1},{1,0},{2,3},{3,2},{4,5},{5,4},{6,7},{7,6},{8,9},{9,8},{10,11... | collective-permute-start | bytes 393224 | tf_op jit(solution)/shard_map/ppermute | solution.py:263
  86.8 1.4 %collective-permute-start.14 = (bf16[2,2,32,512]{3,2,1,0:T(8,128)(2,1)S(1)}, bf16[2,2,32,512]{3,2,1,0:T(8,128)(2,1)S(1)}, u32[]{:S(2)}, u32[]{:S(2)}) collective-permute-start(bf16[2,2,32,512]{3,2,1,0:T(8,128)(2,1)S(1)} %get-tuple-element.60), channel_id=1, source_target_pairs={{0,8},{8,0},{16,24},{24,16},{1,9},{9,1},{17,25},{25,17},{2,10},{10... | collective-permute-start | bytes 393224 | tf_op jit(solution)/shard_map/ppermute | solution.py:263
  88.7 5.5 %collective-permute-start.15 = (bf16[2,32,512]{2,1,0:T(8,128)(2,1)S(1)}, bf16[2,32,512]{2,1,0:T(8,128)(2,1)S(1)}, u32[]{:S(2)}, u32[]{:S(2)}) collective-permute-start(bf16[2,32,512]{2,1,0:T(8,128)(2,1)S(1)} %get-tuple-element.65), channel_id=1, source_target_pairs={{0,16},{8,24},{16,0},{24,8},{1,17},{9,25},{17,1},{25,9},{2,18},{10... | collective-permute-start | bytes 196616 | tf_op jit(solution)/shard_map/ppermute | solution.py:263
  90.2 3.9 %collective-permute-start.16 = (bf16[4,32,128]{2,1,0:T(8,128)(2,1)S(1)}, bf16[4,32,128]{2,1,0:T(8,128)(2,1)S(1)}, u32[]{:S(2)}, u32[]{:S(2)}) collective-permute-start(bf16[4,32,128]{2,1,0:T(8,128)(2,1)S(1)} %get-tuple-element.67), channel_id=1, source_target_pairs={{0,1},{1,0},{2,3},{3,2},{4,5},{5,4},{6,7},{7,6},{8,9},{9,8},{10,11... | collective-permute-start | bytes 98312 | tf_op jit(solution)/shard_map/ppermute | solution.py:263
  103.2 3.9 %collective-permute-start.17 = (bf16[3,32,128]{2,1,0:T(8,128)(2,1)S(1)}, bf16[3,32,128]{2,1,0:T(8,128)(2,1)S(1)}, u32[]{:S(2)}, u32[]{:S(2)}) collective-permute-start(bf16[3,32,128]{2,1,0:T(8,128)(2,1)S(1)} %get-tuple-element.71), channel_id=1, source_target_pairs={{0,1},{1,0},{2,3},{3,2},{4,5},{5,4},{6,7},{7,6},{8,9},{9,8},{10,11... | collective-permute-start | bytes 73736 | tf_op jit(solution)/shard_map/ppermute | solution.py:263
  (22 other events, 78.3 us)

commit v3 on v2

--- a/solution.py
+++ b/solution.py
@@ -10,63 +10,77 @@
 
 BF16 = jnp.bfloat16
 F32 = jnp.float32
-VMEM_BYTES = 60 * 1024 * 1024
-STEP_VMEM_BYTES = 32 * 1024 * 1024
+VMEM_BYTES = 56 * 1024 * 1024
+STEP_VMEM_BYTES = 16 * 1024 * 1024
 
 
 def times_transposed(left, right):
     return lax.dot_general(left, right, (((1,), (1,)), ((), ())), preferred_element_type=F32)
 
 
-def leaf_kernel(per_step, slots, parent_ref, rhs_ref, inv_ref, mid_ref, solved_ref, round_ref, *rest):
-    terms_refs, total = rest[:-1], rest[-1]
-    step = pl.program_id(0)
+def leaf_kernel(
+    slots, parent_ref, rhs_ref, inv_ref, mid_ref, solved_ref, round_ref, *rest
+):
+    terms_refs, (rhs, inv, mid, solved, total, rhs_sems, inv_sems, mid_sem, out_sems) = rest[:slots], rest[slots:]
+    leaves = rhs.shape[0]
     first = lax.axis_index("col") if slots == 2 else 0
-
-    @pl.when(step == 0)
-    def _():
+    rhs_copies = [pltpu.make_async_copy(rhs_ref.at[i], rhs.at[i], rhs_sems.at[i]) for i in range(leaves)]
+    inv_copies = [pltpu.make_async_copy(inv_ref.at[i], inv.at[i], inv_sems.at[i]) for i in range(leaves)]
+    mid_copy = pltpu.make_async_copy(mid_ref, mid, mid_sem)
+    for i in range(leaves):
+        inv_copies[i].start()
+        rhs_copies[i].start()
+    mid_copy.start()
+    out_copies = []
+    for i in range(leaves):
+        inv_copies[i].wait()
+        rhs_copies[i].wait()
+        solved[i] = times_transposed(rhs[i].astype(BF16), inv[i])
+        out_copies.append(pltpu.make_async_copy(solved.at[i], solved_ref.at[i], out_sems.at[i]))
+        out_copies[i].start()
+        round_ref[i] = solved[i].astype(BF16)
+    mid_copy.wait()
+    if slots == 2:
+        right = jnp.concatenate([mid[i] for i in range(leaves)], axis=1)
+        for s, ref in enumerate(terms_refs):
+            weights = [jnp.where(parent_ref[i] ^ first == s, 1.0, 0.0).astype(BF16) for i in range(leaves)]
+            left = jnp.concatenate([round_ref[i] * weights[i] for i in range(leaves)], axis=1)
+            ref[...] = times_transposed(left, right).astype(ref.dtype)
+    else:
         total[...] = jnp.zeros_like(total)
-
-    for i in range(per_step):
-        solved = times_transposed(rhs_ref[i].astype(BF16), inv_ref[i])
-        solved_ref[i] = solved
-        rounded = solved.astype(BF16)
-        round_ref[step * per_step + i] = rounded
-        slot = parent_ref[step * per_step + i] ^ first
-        total[slot] += times_transposed(rounded, mid_ref[i])
-
-    @pl.when(step == pl.num_programs(0) - 1)
-    def _():
+        for i in range(leaves):
+            total[parent_ref[i]] += times_transposed(round_ref[i], mid[i])
         for s, ref in enumerate(terms_refs):
             ref[...] = total[s].astype(ref.dtype)
+    for copy in out_copies:
+        copy.wait()
 
 
 def leaf_solve(parent, rhs, inv, lower_mid, slots):
     leaves, rows, size = rhs.shape
     width = inv.shape[1]
-    per_step = 2 if leaves % 2 == 0 else 1
+    hbm, vmem = pl.BlockSpec(memory_space=pltpu.HBM), pl.BlockSpec(memory_space=pltpu.VMEM)
     return pl.pallas_call(
-        functools.partial(leaf_kernel, per_step, slots),
-        grid=(leaves // per_step,),
-        in_specs=[
-            pl.BlockSpec(memory_space=pltpu.SMEM),
-            pl.BlockSpec((per_step, rows, size), lambda i: (i, 0, 0)),
-            pl.BlockSpec((per_step, width, size), lambda i: (i, 0, 0)),
-            pl.BlockSpec((per_step, size, width), lambda i: (i, 0, 0)),
-        ],
-        out_specs=[
-            pl.BlockSpec((per_step, rows, width), lambda i: (i, 0, 0)),
-        ]
-        + [pl.BlockSpec(memory_space=pltpu.VMEM)] * (1 + slots),
+        functools.partial(leaf_kernel, slots),
+        in_specs=[pl.BlockSpec(memory_space=pltpu.SMEM), hbm, hbm, hbm],
+        out_specs=[hbm] + [vmem] * (1 + slots),
         out_shape=[
             jax.ShapeDtypeStruct((leaves, rows, width), F32),
             jax.ShapeDtypeStruct((leaves, rows, width), BF16),
         ]
         + [jax.ShapeDtypeStruct((rows, size), BF16)] * slots,
-        scratch_shapes=[pltpu.VMEM((slots, rows, size), F32)],
-        compiler_params=pltpu.CompilerParams(
-            dimension_semantics=("arbitrary",), vmem_limit_bytes=VMEM_BYTES
-        ),
+        scratch_shapes=[
+            pltpu.VMEM(rhs.shape, F32),
+            pltpu.VMEM(inv.shape, BF16),
+            pltpu.VMEM(lower_mid.shape, BF16),
+            pltpu.VMEM((leaves, rows, width), F32),
+            pltpu.VMEM((8, 128) if slots == 2 else (slots, rows, size), F32),
+            pltpu.SemaphoreType.DMA((leaves,)),
+            pltpu.SemaphoreType.DMA((leaves,)),
+            pltpu.SemaphoreType.DMA,
+            pltpu.SemaphoreType.DMA((leaves,)),
+        ],
+        compiler_params=pltpu.CompilerParams(vmem_limit_bytes=VMEM_BYTES),
         cost_estimate=pl.CostEstimate(
             flops=4 * leaves * rows * size * width,
             bytes_accessed=leaves * (rows * size * 4 + 4 * width * size + rows * width * 6),
@@ -76,41 +90,37 @@
     )(parent, rhs, inv, lower_mid)
 
 
-def coupling_kernel(per_step, pattern_ref, round_ref, lower_ref, up_ref):
-    step = pl.program_id(0)
-
-    @pl.when(step == 0)
-    def _():
-        up_ref[...] = jnp.zeros_like(up_ref)
-
-    for k in range(up_ref.shape[0]):
-        left, right = [], []
-        for i in range(per_step):
-            weight = pattern_ref[step * per_step + i, k].astype(F32).astype(BF16)
-            left.append(round_ref[step * per_step + i] * weight)
-            right.append(lower_ref[i, k])
-        left = left[0] if per_step == 1 else jnp.concatenate(left, axis=1)
-        right = right[0] if per_step == 1 else jnp.concatenate(right, axis=1)
-        up_ref[k] += times_transposed(left, right)
+def coupling_kernel(pattern_ref, round_ref, lower_ref, up_ref, rounded, lower, round_sem, sems):
+    leaves, kinds = lower.shape[:2]
+    round_copy = pltpu.make_async_copy(round_ref, rounded, round_sem)
+    round_copy.start()
+    copies = [pltpu.make_async_copy(lower_ref.at[:, k], lower.at[:, k], sems.at[k]) for k in range(kinds)]
+    for copy in copies:
+        copy.start()
+    round_copy.wait()
+    for k in range(kinds):
+        copies[k].wait()
+        left = [rounded[i] * pattern_ref[i, k].astype(F32).astype(BF16) for i in range(leaves)]
+        right = [lower[i, k] for i in range(leaves)]
+        up_ref[k] = times_transposed(jnp.concatenate(left, axis=1), jnp.concatenate(right, axis=1))
 
 
 def leaf_coupling(pattern, rounded, lower):
     leaves, rows, width = rounded.shape
     kinds, size = lower.shape[1:3]
-    per_step = 2 if leaves % 2 == 0 else 1
+    hbm = pl.BlockSpec(memory_space=pltpu.HBM)
     return pl.pallas_call(
-        functools.partial(coupling_kernel, per_step),
-        grid=(leaves // per_step,),
-        in_specs=[
-            pl.BlockSpec(memory_space=pltpu.SMEM),
-            pl.BlockSpec(memory_space=pltpu.VMEM),
-            pl.BlockSpec((per_step, kinds, size, width), lambda i: (i, 0, 0, 0)),
-        ],
+        coupling_kernel,
+        in_specs=[pl.BlockSpec(memory_space=pltpu.SMEM), hbm, hbm],
         out_specs=pl.BlockSpec(memory_space=pltpu.VMEM),
         out_shape=jax.ShapeDtypeStruct((kinds, rows, size), F32),
-        compiler_params=pltpu.CompilerParams(
-            dimension_semantics=("arbitrary",), vmem_limit_bytes=VMEM_BYTES
-        ),
+        scratch_shapes=[
+            pltpu.VMEM(rounded.shape, BF16),
+            pltpu.VMEM(lower.shape, BF16),
+            pltpu.SemaphoreType.DMA,
+            pltpu.SemaphoreType.DMA((kinds,)),
+        ],
+        compiler_params=pltpu.CompilerParams(vmem_limit_bytes=STEP_VMEM_BYTES),
         cost_estimate=pl.CostEstimate(
             flops=2 * leaves * kinds * rows * size * width,
             bytes_accessed=leaves * (rows * width * 2 + kinds * size * width * 2) + kinds * rows * size * 4,
@@ -335,71 +345,54 @@
             late_given_ref[k - 1, half] = total[piece(half * 2 + 1 - core, length)].astype(BF16)
 
 
-def repeat_top_kernel(inv_ref, share_ref):
-    half = lax.axis_index("col")
-    block = share_ref.shape[3]
-    for i in (0, 1):
-        share = inv_ref[0, :, piece(half * 2 + i, block)]
-        for r in range(share_ref.shape[0]):
-            share_ref[r, i] = share
+def top_share_kernel(terms_ref, inv_ref, own_ref, share_ref):
+    own_ref[...] = terms_ref[...]
+    length = share_ref.shape[1]
+    share_ref[...] = inv_ref[0, :, piece(lax.axis_index("col"), length)]
+
+
+def half_top_kernel(p0, p3, p2, p1, half_ref):
+    row = lax.axis_index("row")
+    for d, ref in zip((0, 3, 2, 1), (p0, p3, p2, p1)):
+        half_ref[piece(row ^ d, ref.shape[0])] = ref[...]
 
 
 def whole_top_kernel(own_ref, other_ref, whole_ref):
-    half = lax.axis_index("col")
-    block = own_ref.shape[3]
-    for r in range(own_ref.shape[0]):
-        for i in (0, 1):
-            whole_ref[pl.ds(r * block, block), piece(half * 2 + i, block)] = own_ref[r, i]
-            whole_ref[pl.ds(r * block, block), piece((1 - half) * 2 + i, block)] = other_ref[r, i]
-
-
-def repeat_apex_kernel(inv_ref, lower_ref, share_ref):
-    gz, col = lax.axis_index("gz"), lax.axis_index("col")
-    pair, block = gz >> 1, share_ref.shape[3]
-    quarter = piece((gz & 1) * 2 + col, block)
-    shares = (inv_ref[pair, :, quarter], inv_ref[2, :, quarter], lower_ref[pair, quarter, :])
-    for i, share in enumerate(shares):
-        for r in range(share_ref.shape[0]):
-            share_ref[r, i] = share
-
-
-def whole_apex_kernel(own_ref, col_ref, core_ref, both_ref, front_ref, last_ref, lower_ref):
-    core, col = lax.axis_index("gz") & 1, lax.axis_index("col")
-    block = own_ref.shape[3]
-    for d, ref in enumerate((own_ref, col_ref, core_ref, both_ref)):
-        quarter = piece((core ^ d >> 1) * 2 + (col ^ d & 1), block)
-        for r in range(own_ref.shape[0]):
-            at = pl.ds(r * block, block)
-            front_ref[at, quarter] = ref[r, 0]
-            last_ref[at, quarter] = ref[r, 1]
-            lower_ref[quarter, at] = ref[r, 2]
+    col, length = lax.axis_index("col"), own_ref.shape[1]
+    whole_ref[:, piece(col, length)] = own_ref[...]
+    whole_ref[:, piece(1 - col, length)] = other_ref[...]
 
 
 def on_first_row(rhs):
     return jnp.where(lax.axis_index("row") == 0, rhs, 0.0)
 
 
-def top_blocks_kernel(rhs_ref, top_ref, other_ref, inv_ref, late_ref, late_other_ref, blocks_ref, out_ref, given_ref, ready):
-    col, part = lax.axis_index("col"), top_ref.shape[1]
-    block = blocks_ref.shape[2]
-    for i in range(4):
-        total = top_ref[i] + other_ref[i].astype(F32)
-        ready[pl.ds(i * part, part)] = (on_first_row(rhs_ref[0, piece(i * 2 + col, part)]) - total).astype(BF16)
-    solved = times_transposed(ready[...], inv_ref[...])
-    for r in range(blocks_ref.shape[0]):
-        blocks_ref[r] = solved[:, r * block : (r + 1) * block].astype(BF16)
+def late_pieces_kernel(late_ref, other_ref, out_ref, given_ref):
+    col, part = lax.axis_index("col"), out_ref.shape[2]
     for k in (0, 1):
         for half in (0, 1):
             for ref, side in ((out_ref, col), (given_ref, 1 - col)):
                 at = piece(side, part)
-                total = late_ref[k, half, at] + late_other_ref[k, half, at].astype(F32)
+                total = late_ref[k, half, at] + other_ref[k, half, at].astype(F32)
                 ref[k, half] = total.astype(ref.dtype)
 
 
-def top_up_kernel(blocks_ref, lower_ref, late_ref, late_other_ref, solved_ref, send_ref, kept_ref, given_ref, total):
+def top_blocks_kernel(rhs_ref, top_ref, other_ref, inv_ref, kept_ref, g3, g2, g1, ready, solved):
+    row, col, part = lax.axis_index("row"), lax.axis_index("col"), top_ref.shape[1]
+    for i in range(4):
+        total = top_ref[i] + other_ref[i].astype(F32)
+        ready[pl.ds(i * part, part)] = (on_first_row(rhs_ref[0, piece(i * 2 + col, part)]) - total).astype(BF16)
+    solved[...] = times_transposed(ready[...], inv_ref[...])
+    for d, ref in zip((0, 3, 2, 1), (kept_ref, g3, g2, g1)):
+        ref[...] = solved[:, piece(row ^ d, ref.shape[1])].astype(ref.dtype)
+
+
+def top_up_kernel(
+    kept_ref, r3, r2, r1, lower_ref, late_ref, late_other_ref, solved_ref, send_ref, out_ref, given_ref, total
+):
     core = lax.axis_index("gz") & 1
     part = solved_ref.shape[1]
-    solved = sum(blocks_ref[r].astype(F32) for r in range(blocks_ref.shape[0]))
+    solved = widened(kept_ref, r3, r2, r1)
     rounded = solved.astype(BF16)
     for i in range(4):
         solved_ref[i] = solved[i * part : (i + 1) * part]
@@ -408,49 +401,57 @@
         total[...] = times_transposed(rounded, lower_ref[0, k])
         for half in (0, 1):
             late = late_ref[k, half] + late_other_ref[k, half].astype(F32)
-            kept_ref[k, half] = total[piece(half * 2 + core, part)] + late
+            out_ref[k, half] = total[piece(half * 2 + core, part)] + late
             given_ref[k, half] = total[piece(half * 2 + 1 - core, part)].astype(BF16)
+
+
+def front_pieces_kernel(kept_ref, other_ref, own_ref, send_ref, last_ref):
+    part = kept_ref.shape[2]
+    for half in (0, 1):
+        at = pl.ds(half * part, part)
+        total = kept_ref[0, half] + other_ref[0, half].astype(F32)
+        own_ref[at] = total
+        send_ref[at] = total.astype(BF16)
+        last_ref[half] = kept_ref[1, half] + other_ref[1, half].astype(F32)
 
 
 def apex_rows(rhs_ref, which, half, part):
     core, col = lax.axis_index("gz") & 1, lax.axis_index("col")
-    return on_first_row(rhs_ref[which, piece(half * 4 + core * 2 + col, part)])
-
-
-def front_kernel(rhs_ref, kept_ref, other_ref, inv_ref, lower_ref, front_ref, last_ref, given_ref, ready, fronts, ups):
-    pair, part = lax.axis_index("gz") >> 1, last_ref.shape[0]
-    for half in (0, 1):
-        total = kept_ref[0, half] + other_ref[0, half].astype(F32)
-        ready[pl.ds(half * part, part)] = (apex_rows(rhs_ref, pair, half, part) - total).astype(BF16)
-    fronts[...] = times_transposed(ready[...], inv_ref[...])
-    front_ref[...] = fronts[piece(pair, part)].astype(BF16)
-    given_ref[0] = fronts[piece(1 - pair, part)].astype(BF16)
-    ups[...] = times_transposed(fronts[...].astype(BF16), lower_ref[...])
-    for half in (0, 1):
-        ups[pl.ds(half * part, part)] += kept_ref[1, half] + other_ref[1, half].astype(F32)
-    last_ref[...] = ups[piece(pair, part)]
-    given_ref[1] = ups[piece(1 - pair, part)].astype(BF16)
-
-
-def last_kernel(rhs_ref, inv_ref, front_ref, last_ref, other_ref, top_ref, other_top_ref, blocks_ref, top_all_ref):
-    pair, col, part = lax.axis_index("gz") >> 1, lax.axis_index("col"), last_ref.shape[0]
-    block = blocks_ref.shape[3]
-    ready = (apex_rows(rhs_ref, 2, pair, part) - (last_ref[...] + other_ref[1].astype(F32))).astype(BF16)
-    solved = times_transposed(ready, inv_ref[...])
-    for r in range(blocks_ref.shape[0]):
-        at = slice(r * block, (r + 1) * block)
-        blocks_ref[r, 2] = solved[:, at].astype(BF16)
-        blocks_ref[r, pair] = front_ref[:, at]
-        blocks_ref[r, 1 - pair] = other_ref[0, :, at]
+    return rhs_ref[which, piece(half * 4 + core * 2 + col, part)]
+
+
+def front_solve_kernel(rhs_ref, own_ref, r3, r2, r1, inv_ref, lower_ref, last_ref, front_ref, kept_ref, given_ref, total, fronts):
+    pair = lax.axis_index("gz") >> 1
+    part, size = kept_ref.shape
+    rhs = jnp.concatenate([apex_rows(rhs_ref, pair, half, part) for half in (0, 1)])
+    ready = (rhs - widened(own_ref, r3, r2, r1)).astype(BF16)
+    fronts[...] = times_transposed(ready, inv_ref[pair])
+    total[...] = times_transposed(fronts[...].astype(BF16), lower_ref[pair])
+    front_ref[...] = fronts[piece(pair, part)]
+    kept_ref[...] = total[piece(pair, part)] + last_ref[pair]
+    given_ref[:, :size] = (total[piece(1 - pair, part)] + last_ref[1 - pair]).astype(BF16)
+    given_ref[:, size:] = fronts[piece(1 - pair, part)].astype(BF16)
+
+
+def last_pieces_kernel(kept_ref, other_ref, own_ref, send_ref):
+    total = kept_ref[...] + other_ref[:, : own_ref.shape[1]].astype(F32)
+    own_ref[...] = total
+    send_ref[...] = total.astype(BF16)
+
+
+def last_solve_kernel(
+    rhs_ref, inv_ref, own_ref, r3, r2, r1, front_ref, other_ref, top_ref, other_top_ref, solved_ref, send_ref, top_all_ref
+):
+    pair, col = lax.axis_index("gz") >> 1, lax.axis_index("col")
+    part, size = own_ref.shape
+    ready = (apex_rows(rhs_ref, 2, pair, part) - widened(own_ref, r3, r2, r1)).astype(BF16)
+    solved_ref[2] = times_transposed(ready, inv_ref[2])
+    solved_ref[pair] = front_ref[...]
+    solved_ref[1 - pair] = other_ref[:, size:].astype(F32)
+    send_ref[...] = solved_ref[...].astype(BF16)
     for i in range(top_ref.shape[0]):
         top_all_ref[0, piece(i * 2 + col, part)] = top_ref[i]
         top_all_ref[0, piece(i * 2 + 1 - col, part)] = other_top_ref[i].astype(F32)
-
-
-def apex_sum_kernel(blocks_ref, solved_ref, send_ref):
-    solved = sum(blocks_ref[r].astype(F32) for r in range(blocks_ref.shape[0]))
-    solved_ref[...] = solved
-    send_ref[...] = solved.astype(BF16)
 
 
 def place_apex_kernel(solved_ref, other_ref, apex_ref):
@@ -483,25 +484,27 @@
     quarter, part = count // 4, count // 8
 
     rows = lax.axis_size("row")
+
     leaf_solved, leaf_round, terms, other_terms = leaf_solve(leaf_parent, leaf_rhs, leaf_inv, leaf_lower_mid, 2)
     (other_terms,) = partners(other_terms, [{"col": 1}])
     layer_up = leaf_coupling(leaf_pattern, leaf_round, leaf_lower_coupling)
 
-    (share,) = whole_call(
-        repeat_top_kernel, "repeat_top", [top_inv], [((rows, 2, width, width), BF16)], after=[leaf_round]
-    )
-    top_share = exchange(share, "row")
+    terms, share = whole_call(
+        top_share_kernel, "top_share", [terms, top_inv], [((count, size), BF16), ((width, size // 2), BF16)]
+    )
+    shares = partners(share, ROW_MOVES)
 
     kept, *given = whole_call(
         mid_pieces_kernel, "mid_pieces", [terms, other_terms],
         [((quarter, size), F32)] + [((quarter, size), BF16)] * 3,
-        after=[top_share],
+        after=shares,
     )
     arrived = partners(given, ROW_MOVES)
-    (top_other,) = partners(top_share, [{"col": 1}])
+    (top_half,) = whole_call(half_top_kernel, "half_top", [share, *shares], [((size, size // 2), BF16)], after=[kept])
+    (top_other,) = partners(top_half, [{"col": 1}])
     (ready,) = whole_call(mid_total_kernel, "mid_total", [mid_rhs, kept, *arrived], [((quarter, size), BF16)])
     arrived = partners(ready, ROW_MOVES)
-    (top_whole,) = whole_call(whole_top_kernel, "whole_top", [top_share, top_other], [((size, size), BF16)])
+    (top_whole,) = whole_call(whole_top_kernel, "whole_top", [top_half, top_other], [((size, size), BF16)])
     mid_solved, kept, given, late_kept, late_given = whole_call(
         mid_solve_kernel, "mid_solve", [mid_pattern, ready, *arrived, parent_diagonal_inverse, mid_lower, layer_up],
         [((count, width), F32), ((4, part, size), F32), ((4, part, size), BF16)]
@@ -514,23 +517,21 @@
 
     (other,) = partners(given, [{"col": 1}])
     (late_other,) = partners(late_given, [{"gz": 1}])
-    (share,) = whole_call(
-        repeat_apex_kernel, "repeat_apex", [apex_inv, apex_lower], [((rows, 3, width, width), BF16)], after=[given]
-    )
-    apex_share = exchange(share, "row")
-    blocks, late_kept, late_given = whole_call(
-        top_blocks_kernel, "top_blocks", [top_rhs, kept, other, top_whole, late_kept, late_other],
-        [((rows, count // 2, width), BF16), ((2, 2, part, size), F32), ((2, 2, part, size), BF16)],
+    late_kept, late_given = whole_call(
+        late_pieces_kernel, "late_pieces", [late_kept, late_other],
+        [((2, 2, part, size), F32), ((2, 2, part, size), BF16)],
+    )
+    (late_other,) = partners(late_given, [{"col": 1}])
+    kept, *given = whole_call(
+        top_blocks_kernel, "top_blocks", [top_rhs, kept, other, top_whole],
+        [((count // 2, width), F32)] + [((count // 2, width), BF16)] * 3,
         flops=count * size * size,
-        scratch=[pltpu.VMEM((count // 2, size), BF16)],
-    )
-    blocks = exchange(blocks, "row")
-    (late_other,) = partners(late_given, [{"col": 1}])
-    apex_share, _ = lax.optimization_barrier((apex_share, other))
-    (apex_col,) = partners(apex_share, [{"col": 1}])
-    apex_share, apex_col, blocks = lax.optimization_barrier((apex_share, apex_col, blocks))
+        scratch=[pltpu.VMEM((count // 2, size), BF16), pltpu.VMEM((count // 2, size), F32)],
+        after=[late_given],
+    )
+    arrived = partners(given, ROW_MOVES)
     top_solved, top_send, kept, given = whole_call(
-        top_up_kernel, "top_up", [blocks, top_lower, late_kept, late_other],
+        top_up_kernel, "top_up", [kept, *arrived, top_lower, late_kept, late_other],
         [((4, part, width), F32), ((4, part, width), BF16), ((2, 2, part, size), F32), ((2, 2, part, size), BF16)],
         flops=2 * count * size * width,
         scratch=[pltpu.VMEM((4 * part, size), F32)],
@@ -538,25 +539,28 @@
     (other,) = partners(given, [{"gz": 1}])
     (other_top,) = partners(top_send, [{"col": 1}])
 
-    (apex_core,) = partners(apex_share, [{"gz": 1}])
-    (apex_both,) = partners(apex_col, [{"gz": 1}])
-    front_whole, last_whole, lower_whole = whole_call(
-        whole_apex_kernel, "whole_apex", [apex_share, apex_col, apex_core, apex_both], [((size, size), BF16)] * 3
-    )
-    front, last, given = whole_call(
-        front_kernel, "front", [apex_rhs, kept, other, front_whole, lower_whole],
-        [((part, size), BF16), ((part, size), F32), ((2, part, size), BF16)],
-        flops=count * size * size,
-        scratch=[pltpu.VMEM((2 * part, size), BF16)] + [pltpu.VMEM((2 * part, size), F32)] * 2,
-    )
+    own, send, last = whole_call(
+        front_pieces_kernel, "front_pieces", [kept, other],
+        [((2 * part, size), F32), ((2 * part, size), BF16), ((2, part, size), F32)],
+    )
+    arrived = partners(send, ROW_MOVES)
+    front, kept, given = whole_call(
+        front_solve_kernel, "front_solve", [apex_rhs, own, *arrived, apex_inv, apex_lower, last],
+        [((part, width), F32), ((part, size), F32), ((part, size + width), BF16)],
+        flops=count * size * width,
+        scratch=[pltpu.VMEM((2 * part, size), F32), pltpu.VMEM((2 * part, width), F32)],
+    )
+
     (other,) = partners(given, [{"gz": 2}])
-    blocks, top_all = whole_call(
-        last_kernel, "last", [apex_rhs, last_whole, front, last, other, top_solved, other_top],
-        [((rows, 3, part, width), BF16), ((1, count, width), F32)],
-        flops=count * size * size // 4,
-    )
-    solved, send = whole_call(
-        apex_sum_kernel, "apex_sum", [exchange(blocks, "row")], [((3, part, width), F32), ((3, part, width), BF16)]
+    own, send = whole_call(
+        last_pieces_kernel, "last_pieces", [kept, other], [((part, size), F32), ((part, size), BF16)]
+    )
+    arrived = partners(send, ROW_MOVES)
+    solved, send, top_all = whole_call(
+        last_solve_kernel, "last_solve",
+        [apex_rhs, apex_inv, own, *arrived, front, other, top_solved, other_top],
+        [((3, part, width), F32), ((3, part, width), BF16), ((1, count, width), F32)],
+        flops=count * size * width // 4,
     )
     (other,) = partners(send, [{"col": 1}])
     (apex,) = whole_call(place_apex_kernel, "place_apex", [solved, other], [((3, 2 * part, width), F32)])

time: 109 us -> 86.4 us (0.79)
  blocking collectives: 16.7 us -> 0 us
  local copies, waits for them, and re-layouts: 13.4 us -> 3.17 us
  starting transfers between devices: 29.8 us -> 38 us
  Pallas kernels: 18.6 us -> 15.8 us
    ppermute x18 -> x27, starting transfers between devices: 19.9 us -> 38 us  [partners(): arrived.append(lax.ppermute(item, axes, route))]
    all_to_all x2 -> x0, blocking collectives: 16.7 us -> none  [exchange(): return lax.all_to_all(pieces, axis, split_axis=0, concat_axis=0, tiled=True)]
    all_to_all x2 -> x0, waiting for transfers between devices: 11.3 us -> none  [exchange(): return lax.all_to_all(pieces, axis, split_axis=0, concat_axis=0, tiled=True)]
    ppermute x18 -> x27, waiting for transfers between devices: 17.1 us -> 28.3 us  [partners(): arrived.append(lax.ppermute(item, axes, route))]
    unnamed x53 -> x29, local copies, waits for them, and re-layouts: 13.4 us -> 3.17 us
    all_to_all x2 -> x0, starting transfers between devices: 9.88 us -> none  [exchange(): return lax.all_to_all(pieces, axis, split_axis=0, concat_axis=0, tiled=True)]
    pallas_call x2, Pallas kernels: 11.2 us -> 8.63 us  [the longest x1 6.34 us: leaf_solve(): pl.pallas_call(functools.partial(leaf_kernel, slots), in_specs=[pl.BlockS...]
    pallas_call x13 -> x14, Pallas kernels: 7.4 us -> 7.13 us  [whole_call(): pl.pallas_call(body, in_specs=[pl.BlockSpec(memory_space=pl.ANY)] * len(a...]
  transfers between devices with their start and end apart: 20 -> 27, of which waited for: 9 -> 13; matrix products, arithmetic and copies ran while one was open for 1% -> 0% of each run, Pallas kernels for 7% -> 6%
where the time goes in v3:
time: 86.4 us; the launch traced here: 86.1 us
  starting transfers between devices  38 us (44%)
  waiting for transfers between devices  28.3 us (33%)
  Pallas kernels  15.8 us (18%)
  local copies, waits for them, and re-layouts  3.17 us (4%)
  between operations  0.87 us (1%)
    ppermute x27, starting transfers between devices, partners(): arrived.append(lax.ppermute(item, axes, route))  38 us
    ppermute x27, waiting for transfers between devices, partners(): arrived.append(lax.ppermute(item, axes, route))  28.3 us
    pallas_call x14, Pallas kernels, whole_call(): pl.pallas_call(body, in_specs=[pl.BlockSpec(memory_space=pl.ANY)] * len(a...  7.13 us
    pallas_call x1, Pallas kernels, leaf_solve(): pl.pallas_call(functools.partial(leaf_kernel, slots), in_specs=[pl.BlockS...  6.34 us
    unnamed x29, local copies, waits for them, and re-layouts  3.17 us
    pallas_call x1, Pallas kernels, leaf_coupling(): pl.pallas_call(coupling_kernel, in_specs=[pl.BlockSpec(memory_space=pltpu...  2.29 us
  transfers between devices with their start and end apart: 27, of which 13 were waited for; matrix products, arithmetic and copies ran while one was open for 0% of the time, Pallas kernels for 6%

profile of v3, /device:TPU:0, one launch (start us, length us, event | category | flops | bytes accessed | tf_op | source)
XLA Modules:
  0.0 86.1 jit_solution(9918854071321889130)
XLA Ops:
  0.7 6.3 %leaf_solve.1 = (f32[8,256,128]{2,1,0:T(8,128)}, bf16[8,256,128]{2,1,0:T(8,128)(2,1)}, bf16[256,512]{1,0:T(8,128)(2,1)}, bf16[256,512]{1,0:T(8,128)(2,1)}) custom-call(s32[8]{0:T(128)} %parent_ref.1, f32[8,256,512]{2,1,0:T(8,128)} %rhs_ref.1, bf16[8,128,512]{2,1,0:T(8,128)(2,1)} %inv_ref.1, bf16[8,512,128]{2,1,0:T(8,128)(2,1)} %mid_ref.1), custom_call_target="tpu_custom_call" | custom-call | flops 536870912 | bytes 7864320 | tf_op jit(solution)/shard_map/leaf_solve/pallas_call | solution.py:63
  7.0 3.0 %collective-permute-start.3 = (bf16[256,512]{1,0:T(8,128)(2,1)}, bf16[256,512]{1,0:T(8,128)(2,1)S(1)}, u32[]{:S(2)}, u32[]{:S(2)}) collective-permute-start(bf16[256,512]{1,0:T(8,128)(2,1)} %get-tuple-element.44), channel_id=1, source_target_pairs={{0,1},{1,0},{2,3},{3,2},{4,5},{5,4},{6,7},{7,6},{8,9},{9,8},{10,11... | collective-permute-start | bytes 786440 | tf_op jit(solution)/shard_map/ppermute | solution.py:273
  11.0 1.6 %collective-permute-start.2 = (bf16[128,256]{1,0:T(8,128)(2,1)S(1)}, bf16[128,256]{1,0:T(8,128)(2,1)S(1)}, u32[]{:S(2)}, u32[]{:S(2)}) collective-permute-start(bf16[128,256]{1,0:T(8,128)(2,1)S(1)} %get-tuple-element.42.refs_1_), channel_id=1, source_target_pairs={{0,2},{2,0},{4,6},{6,4},{1,3},{3,1},{5,7},{7,5},{8,10},{10,8},{12,... | collective-permute-start | bytes 196616 | tf_op jit(solution)/shard_map/ppermute | solution.py:273
  12.7 2.6 %collective-permute-start.1 = (bf16[128,256]{1,0:T(8,128)(2,1)S(1)}, bf16[128,256]{1,0:T(8,128)(2,1)S(1)}, u32[]{:S(2)}, u32[]{:S(2)}) collective-permute-start(bf16[128,256]{1,0:T(8,128)(2,1)S(1)} %get-tuple-element.42.refs_1_), channel_id=1, source_target_pairs={{0,4},{2,6},{4,0},{6,2},{1,5},{3,7},{5,1},{7,3},{8,12},{10,14},{12... | collective-permute-start | bytes 196616 | tf_op jit(solution)/shard_map/ppermute | solution.py:273
  15.5 4.2 %collective-permute-done.1.refs_1_.refs_3_ = bf16[128,256]{1,0:T(8,128)(2,1)S(1)} collective-permute-done((bf16[128,256]{1,0:T(8,128)(2,1)S(1)}, bf16[128,256]{1,0:T(8,128)(2,1)S(1)}, u32[]{:S(2)}, u32[]{:S(2)}) %collective-permute-start.1) | collective-permute-done | bytes 65568 | tf_op jit(solution)/shard_map/ppermute | solution.py:273
  19.6 1.7 %collective-permute-done.refs_0_.refs_2_ = bf16[128,256]{1,0:T(8,128)(2,1)S(1)} collective-permute-done((bf16[128,256]{1,0:T(8,128)(2,1)S(1)}, bf16[128,256]{1,0:T(8,128)(2,1)S(1)}, u32[]{:S(2)}, u32[]{:S(2)}) %collective-permute-start) | collective-permute-done | bytes 65568 | tf_op jit(solution)/shard_map/ppermute | solution.py:273
  24.1 2.9 %collective-permute-start.7 = (bf16[64,512]{1,0:T(8,128)(2,1)}, bf16[64,512]{1,0:T(8,128)(2,1)}, u32[]{:S(2)}, u32[]{:S(2)}) collective-permute-start(bf16[64,512]{1,0:T(8,128)(2,1)} %get-tuple-element.48), channel_id=1, source_target_pairs={{0,2},{2,0},{4,6},{6,4},{1,3},{3,1},{5,7},{7,5},{8,10},{10,8},{12,... | collective-permute-start | bytes 196616 | tf_op jit(solution)/shard_map/ppermute | solution.py:273
  27.1 1.9 %collective-permute-done.5.refs_2_ = bf16[64,512]{1,0:T(8,128)(2,1)} collective-permute-done((bf16[64,512]{1,0:T(8,128)(2,1)}, bf16[64,512]{1,0:T(8,128)(2,1)}, u32[]{:S(2)}, u32[]{:S(2)}) %collective-permute-start.5) | collective-permute-done | bytes 65568 | tf_op jit(solution)/shard_map/ppermute | solution.py:273
  34.7 2.1 %collective-permute-start.8 = (bf16[64,512]{1,0:T(8,128)(2,1)S(1)}, bf16[64,512]{1,0:T(8,128)(2,1)S(1)}, u32[]{:S(2)}, u32[]{:S(2)}) collective-permute-start(bf16[64,512]{1,0:T(8,128)(2,1)S(1)} %mid_total.1.refs_2_), channel_id=1, source_target_pairs={{0,6},{2,4},{4,2},{6,0},{1,7},{3,5},{5,3},{7,1},{8,14},{10,12},{12... | collective-permute-start | bytes 196616 | tf_op jit(solution)/shard_map/ppermute | solution.py:273
  37.9 2.3 %leaf_coupling.1.refs_8_ = f32[3,256,512]{2,1,0:T(8,128)S(1)} custom-call(s32[8,3]{1,0:T(8,128)S(1)} %copy.20.pattern_ref, bf16[8,256,128]{2,1,0:T(8,128)(2,1)S(1)} %copy-done.4, bf16[8,3,512,128]{3,2,1,0:T(8,128)(2,1)S(1)} %copy-done.1), custom_call_target="tpu_custom_call" | custom-call | flops 805306368 | bytes 5242880 | tf_op jit(solution)/shard_map/leaf_coupling/pallas_call | solution.py:112
  41.4 1.9 %mid_solve.1 = (f32[256,128]{1,0:T(8,128)}, f32[4,32,512]{2,1,0:T(8,128)S(1)}, bf16[4,32,512]{2,1,0:T(8,128)(2,1)S(1)}, f32[2,2,64,512]{3,2,1,0:T(8,128)S(1)}, bf16[2,2,64,512]{3,2,1,0:T(8,128)(2,1)S(1)}) custom-call(bf16[512,512]{1,0:T(8,128)(2,1)S(1)} %whole_top.1.refs_0_.refs_4_, s32[1,2]{1,0:T(1,128)S(1)} %copy-done.12, ...), custom_call_target="tpu_custom_call" | custom-call | flops 134217728 | bytes 3670024 | tf_op jit(solution)/shard_map/mid_solve/pallas_call | solution.py:285
  43.3 1.5 %collective-permute-start.12 = (bf16[4,32,512]{2,1,0:T(8,128)(2,1)S(1)}, bf16[4,32,512]{2,1,0:T(8,128)(2,1)S(1)}, u32[]{:S(2)}, u32[]{:S(2)}) collective-permute-start(bf16[4,32,512]{2,1,0:T(8,128)(2,1)S(1)} %get-tuple-element.55), channel_id=1, source_target_pairs={{0,1},{1,0},{2,3},{3,2},{4,5},{5,4},{6,7},{7,6},{8,9},{9,8},{10,11... | collective-permute-start | bytes 393224 | tf_op jit(solution)/shard_map/ppermute | solution.py:273
  44.9 1.6 %collective-permute-start.16 = (bf16[2,2,32,512]{3,2,1,0:T(8,128)(2,1)S(1)}, bf16[2,2,32,512]{3,2,1,0:T(8,128)(2,1)S(1)}, u32[]{:S(2)}, u32[]{:S(2)}) collective-permute-start(bf16[2,2,32,512]{3,2,1,0:T(8,128)(2,1)S(1)} %get-tuple-element.53.refs_0_), channel_id=1, source_target_pairs={{0,1},{1,0},{2,3},{3,2},{4,5},{5,4},{6,7},{7,6},{8,9},{9,8},{10,11... | collective-permute-start | bytes 393224 | tf_op jit(solution)/shard_map/ppermute | solution.py:273
  46.5 3.1 %collective-permute-done.12.refs_3_ = bf16[4,32,512]{2,1,0:T(8,128)(2,1)S(1)} collective-permute-done((bf16[4,32,512]{2,1,0:T(8,128)(2,1)S(1)}, bf16[4,32,512]{2,1,0:T(8,128)(2,1)S(1)}, u32[]{:S(2)}, u32[]{:S(2)}) %collective-permute-start.12) | collective-permute-done | bytes 131104 | tf_op jit(solution)/shard_map/ppermute | solution.py:273
  50.0 1.8 %collective-permute-start.13 = (bf16[128,128]{1,0:T(8,128)(2,1)S(1)}, bf16[128,128]{1,0:T(8,128)(2,1)S(1)}, u32[]{:S(2)}, u32[]{:S(2)}) collective-permute-start(bf16[128,128]{1,0:T(8,128)(2,1)S(1)} %get-tuple-element.57), channel_id=1, source_target_pairs={{0,6},{2,4},{4,2},{6,0},{1,7},{3,5},{5,3},{7,1},{8,14},{10,12},{12... | collective-permute-start | bytes 98312 | tf_op jit(solution)/shard_map/ppermute | solution.py:273
  51.8 2.6 %collective-permute-start.15 = (bf16[128,128]{1,0:T(8,128)(2,1)S(1)}, bf16[128,128]{1,0:T(8,128)(2,1)S(1)}, u32[]{:S(2)}, u32[]{:S(2)}) collective-permute-start(bf16[128,128]{1,0:T(8,128)(2,1)S(1)} %get-tuple-element.59), channel_id=1, source_target_pairs={{0,2},{2,0},{4,6},{6,4},{1,3},{3,1},{5,7},{7,5},{8,10},{10,8},{12,... | collective-permute-start | bytes 98312 | tf_op jit(solution)/shard_map/ppermute | solution.py:273
  54.4 1.6 %collective-permute-done.13.refs_1_ = bf16[128,128]{1,0:T(8,128)(2,1)S(1)} collective-permute-done((bf16[128,128]{1,0:T(8,128)(2,1)S(1)}, bf16[128,128]{1,0:T(8,128)(2,1)S(1)}, u32[]{:S(2)}, u32[]{:S(2)}) %collective-permute-start.13) | collective-permute-done | bytes 32800 | tf_op jit(solution)/shard_map/ppermute | solution.py:273
  58.6 1.6 %collective-permute-start.20 = (bf16[64,512]{1,0:T(8,128)(2,1)S(1)}, bf16[64,512]{1,0:T(8,128)(2,1)S(1)}, u32[]{:S(2)}, u32[]{:S(2)}) collective-permute-start(bf16[64,512]{1,0:T(8,128)(2,1)S(1)} %get-tuple-element.64), channel_id=1, source_target_pairs={{0,2},{2,0},{4,6},{6,4},{1,3},{3,1},{5,7},{7,5},{8,10},{10,8},{12,... | collective-permute-start | bytes 196616 | tf_op jit(solution)/shard_map/ppermute | solution.py:273
  61.1 2.0 %collective-permute-start.18 = (bf16[64,512]{1,0:T(8,128)(2,1)S(1)}, bf16[64,512]{1,0:T(8,128)(2,1)S(1)}, u32[]{:S(2)}, u32[]{:S(2)}) collective-permute-start(bf16[64,512]{1,0:T(8,128)(2,1)S(1)} %get-tuple-element.64), channel_id=1, source_target_pairs={{0,6},{2,4},{4,2},{6,0},{1,7},{3,5},{5,3},{7,1},{8,14},{10,12},{12... | collective-permute-start | bytes 196616 | tf_op jit(solution)/shard_map/ppermute | solution.py:273
  63.0 5.2 %collective-permute-done.19.refs_3_ = bf16[64,512]{1,0:T(8,128)(2,1)S(1)} collective-permute-done((bf16[64,512]{1,0:T(8,128)(2,1)S(1)}, bf16[64,512]{1,0:T(8,128)(2,1)S(1)}, u32[]{:S(2)}, u32[]{:S(2)}) %collective-permute-start.19) | collective-permute-done | bytes 65568 | tf_op jit(solution)/shard_map/ppermute | solution.py:273
  68.7 1.6 %collective-permute-start.21 = (bf16[32,640]{1,0:T(8,128)(2,1)S(1)}, bf16[32,640]{1,0:T(8,128)(2,1)S(1)}, u32[]{:S(2)}, u32[]{:S(2)}) collective-permute-start(bf16[32,640]{1,0:T(8,128)(2,1)S(1)} %get-tuple-element.67), channel_id=1, source_target_pairs={{0,16},{8,24},{16,0},{24,8},{1,17},{9,25},{17,1},{25,9},{2,18},{10... | collective-permute-start | bytes 122888 | tf_op jit(solution)/shard_map/ppermute | solution.py:273
  75.2 2.0 %collective-permute-start.22 = (bf16[32,512]{1,0:T(8,128)(2,1)S(1)}, bf16[32,512]{1,0:T(8,128)(2,1)S(1)}, u32[]{:S(2)}, u32[]{:S(2)}) collective-permute-start(bf16[32,512]{1,0:T(8,128)(2,1)S(1)} %get-tuple-element.69), channel_id=1, source_target_pairs={{0,6},{2,4},{4,2},{6,0},{1,7},{3,5},{5,3},{7,1},{8,14},{10,12},{12... | collective-permute-start | bytes 98312 | tf_op jit(solution)/shard_map/ppermute | solution.py:273
  77.2 2.2 %collective-permute-done.23.refs_4_ = bf16[32,512]{1,0:T(8,128)(2,1)S(1)} collective-permute-done((bf16[32,512]{1,0:T(8,128)(2,1)S(1)}, bf16[32,512]{1,0:T(8,128)(2,1)S(1)}, u32[]{:S(2)}, u32[]{:S(2)}) %collective-permute-start.23) | collective-permute-done | bytes 32800 | tf_op jit(solution)/shard_map/ppermute | solution.py:273
  83.1 2.3 %collective-permute-done.26.refs_1_ = bf16[3,32,128]{2,1,0:T(8,128)(2,1)S(1)} collective-permute-done((bf16[3,32,128]{2,1,0:T(8,128)(2,1)S(1)}, bf16[3,32,128]{2,1,0:T(8,128)(2,1)S(1)}, u32[]{:S(2)}, u32[]{:S(2)}) %collective-permute-start.26) | collective-permute-done | bytes 24608 | tf_op jit(solution)/shard_map/ppermute | solution.py:273
  (75 shorter events, 25.6 us)
Async XLA Ops:
  7.0 14.3 %collective-permute-start.3 = (bf16[256,512]{1,0:T(8,128)(2,1)}, bf16[256,512]{1,0:T(8,128)(2,1)S(1)}, u32[]{:S(2)}, u32[]{:S(2)}) collective-permute-start(bf16[256,512]{1,0:T(8,128)(2,1)} %get-tuple-element.44), channel_id=1, source_target_pairs={{0,1},{1,0},{2,3},{3,2},{4,5},{5,4},{6,7},{7,6},{8,9},{9,8},{10,11... | collective-permute-start | bytes 786440 | tf_op jit(solution)/shard_map/ppermute | solution.py:273
  11.0 4.5 %collective-permute-start.2 = (bf16[128,256]{1,0:T(8,128)(2,1)S(1)}, bf16[128,256]{1,0:T(8,128)(2,1)S(1)}, u32[]{:S(2)}, u32[]{:S(2)}) collective-permute-start(bf16[128,256]{1,0:T(8,128)(2,1)S(1)} %get-tuple-element.42.refs_1_), channel_id=1, source_target_pairs={{0,2},{2,0},{4,6},{6,4},{1,3},{3,1},{5,7},{7,5},{8,10},{10,8},{12,... | collective-permute-start | bytes 196616 | tf_op jit(solution)/shard_map/ppermute | solution.py:273
  12.7 7.0 %collective-permute-start.1 = (bf16[128,256]{1,0:T(8,128)(2,1)S(1)}, bf16[128,256]{1,0:T(8,128)(2,1)S(1)}, u32[]{:S(2)}, u32[]{:S(2)}) collective-permute-start(bf16[128,256]{1,0:T(8,128)(2,1)S(1)} %get-tuple-element.42.refs_1_), channel_id=1, source_target_pairs={{0,4},{2,6},{4,0},{6,2},{1,5},{3,7},{5,1},{7,3},{8,12},{10,14},{12... | collective-permute-start | bytes 196616 | tf_op jit(solution)/shard_map/ppermute | solution.py:273
  15.3 6.1 %collective-permute-start = (bf16[128,256]{1,0:T(8,128)(2,1)S(1)}, bf16[128,256]{1,0:T(8,128)(2,1)S(1)}, u32[]{:S(2)}, u32[]{:S(2)}) collective-permute-start(bf16[128,256]{1,0:T(8,128)(2,1)S(1)} %get-tuple-element.42.refs_1_), channel_id=1, source_target_pairs={{0,6},{2,4},{4,2},{6,0},{1,7},{3,5},{5,3},{7,1},{8,14},{10,12},{12... | collective-permute-start | bytes 196616 | tf_op jit(solution)/shard_map/ppermute | solution.py:273
  22.0 18.2 %collective-permute-start.4 = (bf16[512,256]{1,0:T(8,128)(2,1)S(1)}, bf16[512,256]{1,0:T(8,128)(2,1)}, u32[]{:S(2)}, u32[]{:S(2)}) collective-permute-start(bf16[512,256]{1,0:T(8,128)(2,1)S(1)} %half_top.1.refs_0_), channel_id=1, source_target_pairs={{0,1},{1,0},{2,3},{3,2},{4,5},{5,4},{6,7},{7,6},{8,9},{9,8},{10,11... | collective-permute-start | bytes 786440 | tf_op jit(solution)/shard_map/ppermute | solution.py:273
  22.6 6.4 %collective-permute-start.5 = (bf16[64,512]{1,0:T(8,128)(2,1)}, bf16[64,512]{1,0:T(8,128)(2,1)}, u32[]{:S(2)}, u32[]{:S(2)}) collective-permute-start(bf16[64,512]{1,0:T(8,128)(2,1)} %get-tuple-element.46), channel_id=1, source_target_pairs={{0,6},{2,4},{4,2},{6,0},{1,7},{3,5},{5,3},{7,1},{8,14},{10,12},{12... | collective-permute-start | bytes 196616 | tf_op jit(solution)/shard_map/ppermute | solution.py:273
  24.1 6.3 %collective-permute-start.6 = (bf16[64,512]{1,0:T(8,128)(2,1)}, bf16[64,512]{1,0:T(8,128)(2,1)}, u32[]{:S(2)}, u32[]{:S(2)}) collective-permute-start(bf16[64,512]{1,0:T(8,128)(2,1)} %get-tuple-element.47), channel_id=1, source_target_pairs={{0,4},{2,6},{4,0},{6,2},{1,5},{3,7},{5,1},{7,3},{8,12},{10,14},{12... | collective-permute-start | bytes 196616 | tf_op jit(solution)/shard_map/ppermute | solution.py:273
  24.1 6.3 %collective-permute-start.7 = (bf16[64,512]{1,0:T(8,128)(2,1)}, bf16[64,512]{1,0:T(8,128)(2,1)}, u32[]{:S(2)}, u32[]{:S(2)}) collective-permute-start(bf16[64,512]{1,0:T(8,128)(2,1)} %get-tuple-element.48), channel_id=1, source_target_pairs={{0,2},{2,0},{4,6},{6,4},{1,3},{3,1},{5,7},{7,5},{8,10},{10,8},{12,... | collective-permute-start | bytes 196616 | tf_op jit(solution)/shard_map/ppermute | solution.py:273
  32.4 9.0 %collective-permute-start.10 = (bf16[64,512]{1,0:T(8,128)(2,1)S(1)}, bf16[64,512]{1,0:T(8,128)(2,1)S(1)}, u32[]{:S(2)}, u32[]{:S(2)}) collective-permute-start(bf16[64,512]{1,0:T(8,128)(2,1)S(1)} %mid_total.1.refs_2_), channel_id=1, source_target_pairs={{0,2},{2,0},{4,6},{6,4},{1,3},{3,1},{5,7},{7,5},{8,10},{10,8},{12,... | collective-permute-start | bytes 196616 | tf_op jit(solution)/shard_map/ppermute | solution.py:273
  33.6 7.7 %collective-permute-start.9 = (bf16[64,512]{1,0:T(8,128)(2,1)S(1)}, bf16[64,512]{1,0:T(8,128)(2,1)S(1)}, u32[]{:S(2)}, u32[]{:S(2)}) collective-permute-start(bf16[64,512]{1,0:T(8,128)(2,1)S(1)} %mid_total.1.refs_2_), channel_id=1, source_target_pairs={{0,4},{2,6},{4,0},{6,2},{1,5},{3,7},{5,1},{7,3},{8,12},{10,14},{12... | collective-permute-start | bytes 196616 | tf_op jit(solution)/shard_map/ppermute | solution.py:273
  34.7 6.6 %collective-permute-start.8 = (bf16[64,512]{1,0:T(8,128)(2,1)S(1)}, bf16[64,512]{1,0:T(8,128)(2,1)S(1)}, u32[]{:S(2)}, u32[]{:S(2)}) collective-permute-start(bf16[64,512]{1,0:T(8,128)(2,1)S(1)} %mid_total.1.refs_2_), channel_id=1, source_target_pairs={{0,6},{2,4},{4,2},{6,0},{1,7},{3,5},{5,3},{7,1},{8,14},{10,12},{12... | collective-permute-start | bytes 196616 | tf_op jit(solution)/shard_map/ppermute | solution.py:273
  43.3 6.3 %collective-permute-start.12 = (bf16[4,32,512]{2,1,0:T(8,128)(2,1)S(1)}, bf16[4,32,512]{2,1,0:T(8,128)(2,1)S(1)}, u32[]{:S(2)}, u32[]{:S(2)}) collective-permute-start(bf16[4,32,512]{2,1,0:T(8,128)(2,1)S(1)} %get-tuple-element.55), channel_id=1, source_target_pairs={{0,1},{1,0},{2,3},{3,2},{4,5},{5,4},{6,7},{7,6},{8,9},{9,8},{10,11... | collective-permute-start | bytes 393224 | tf_op jit(solution)/shard_map/ppermute | solution.py:273
  44.9 11.9 %collective-permute-start.16 = (bf16[2,2,32,512]{3,2,1,0:T(8,128)(2,1)S(1)}, bf16[2,2,32,512]{3,2,1,0:T(8,128)(2,1)S(1)}, u32[]{:S(2)}, u32[]{:S(2)}) collective-permute-start(bf16[2,2,32,512]{3,2,1,0:T(8,128)(2,1)S(1)} %get-tuple-element.53.refs_0_), channel_id=1, source_target_pairs={{0,1},{1,0},{2,3},{3,2},{4,5},{5,4},{6,7},{7,6},{8,9},{9,8},{10,11... | collective-permute-start | bytes 393224 | tf_op jit(solution)/shard_map/ppermute | solution.py:273
  50.0 6.0 %collective-permute-start.13 = (bf16[128,128]{1,0:T(8,128)(2,1)S(1)}, bf16[128,128]{1,0:T(8,128)(2,1)S(1)}, u32[]{:S(2)}, u32[]{:S(2)}) collective-permute-start(bf16[128,128]{1,0:T(8,128)(2,1)S(1)} %get-tuple-element.57), channel_id=1, source_target_pairs={{0,6},{2,4},{4,2},{6,0},{1,7},{3,5},{5,3},{7,1},{8,14},{10,12},{12... | collective-permute-start | bytes 98312 | tf_op jit(solution)/shard_map/ppermute | solution.py:273
  51.8 5.0 %collective-permute-start.14 = (bf16[128,128]{1,0:T(8,128)(2,1)S(1)}, bf16[128,128]{1,0:T(8,128)(2,1)S(1)}, u32[]{:S(2)}, u32[]{:S(2)}) collective-permute-start(bf16[128,128]{1,0:T(8,128)(2,1)S(1)} %get-tuple-element.58), channel_id=1, source_target_pairs={{0,4},{2,6},{4,0},{6,2},{1,5},{3,7},{5,1},{7,3},{8,12},{10,14},{12... | collective-permute-start | bytes 98312 | tf_op jit(solution)/shard_map/ppermute | solution.py:273
  51.8 5.0 %collective-permute-start.15 = (bf16[128,128]{1,0:T(8,128)(2,1)S(1)}, bf16[128,128]{1,0:T(8,128)(2,1)S(1)}, u32[]{:S(2)}, u32[]{:S(2)}) collective-permute-start(bf16[128,128]{1,0:T(8,128)(2,1)S(1)} %get-tuple-element.59), channel_id=1, source_target_pairs={{0,2},{2,0},{4,6},{6,4},{1,3},{3,1},{5,7},{7,5},{8,10},{10,8},{12,... | collective-permute-start | bytes 98312 | tf_op jit(solution)/shard_map/ppermute | solution.py:273
  58.6 4.5 %collective-permute-start.20 = (bf16[64,512]{1,0:T(8,128)(2,1)S(1)}, bf16[64,512]{1,0:T(8,128)(2,1)S(1)}, u32[]{:S(2)}, u32[]{:S(2)}) collective-permute-start(bf16[64,512]{1,0:T(8,128)(2,1)S(1)} %get-tuple-element.64), channel_id=1, source_target_pairs={{0,2},{2,0},{4,6},{6,4},{1,3},{3,1},{5,7},{7,5},{8,10},{10,8},{12,... | collective-permute-start | bytes 196616 | tf_op jit(solution)/shard_map/ppermute | solution.py:273
  60.2 8.1 %collective-permute-start.19 = (bf16[64,512]{1,0:T(8,128)(2,1)S(1)}, bf16[64,512]{1,0:T(8,128)(2,1)S(1)}, u32[]{:S(2)}, u32[]{:S(2)}) collective-permute-start(bf16[64,512]{1,0:T(8,128)(2,1)S(1)} %get-tuple-element.64), channel_id=1, source_target_pairs={{0,4},{2,6},{4,0},{6,2},{1,5},{3,7},{5,1},{7,3},{8,12},{10,14},{12... | collective-permute-start | bytes 196616 | tf_op jit(solution)/shard_map/ppermute | solution.py:273
  61.1 7.2 %collective-permute-start.18 = (bf16[64,512]{1,0:T(8,128)(2,1)S(1)}, bf16[64,512]{1,0:T(8,128)(2,1)S(1)}, u32[]{:S(2)}, u32[]{:S(2)}) collective-permute-start(bf16[64,512]{1,0:T(8,128)(2,1)S(1)} %get-tuple-element.64), channel_id=1, source_target_pairs={{0,6},{2,4},{4,2},{6,0},{1,7},{3,5},{5,3},{7,1},{8,14},{10,12},{12... | collective-permute-start | bytes 196616 | tf_op jit(solution)/shard_map/ppermute | solution.py:273
  68.7 4.1 %collective-permute-start.21 = (bf16[32,640]{1,0:T(8,128)(2,1)S(1)}, bf16[32,640]{1,0:T(8,128)(2,1)S(1)}, u32[]{:S(2)}, u32[]{:S(2)}) collective-permute-start(bf16[32,640]{1,0:T(8,128)(2,1)S(1)} %get-tuple-element.67), channel_id=1, source_target_pairs={{0,16},{8,24},{16,0},{24,8},{1,17},{9,25},{17,1},{25,9},{2,18},{10... | collective-permute-start | bytes 122888 | tf_op jit(solution)/shard_map/ppermute | solution.py:273
  70.2 7.0 %collective-permute-start.25 = (bf16[4,32,128]{2,1,0:T(8,128)(2,1)S(1)}, bf16[4,32,128]{2,1,0:T(8,128)(2,1)S(1)}, u32[]{:S(2)}, u32[]{:S(2)}) collective-permute-start(bf16[4,32,128]{2,1,0:T(8,128)(2,1)S(1)} %get-tuple-element.72), channel_id=1, source_target_pairs={{0,1},{1,0},{2,3},{3,2},{4,5},{5,4},{6,7},{7,6},{8,9},{9,8},{10,11... | collective-permute-start | bytes 98312 | tf_op jit(solution)/shard_map/ppermute | solution.py:273
  72.8 4.5 %collective-permute-start.24 = (bf16[32,512]{1,0:T(8,128)(2,1)S(1)}, bf16[32,512]{1,0:T(8,128)(2,1)S(1)}, u32[]{:S(2)}, u32[]{:S(2)}) collective-permute-start(bf16[32,512]{1,0:T(8,128)(2,1)S(1)} %get-tuple-element.69), channel_id=1, source_target_pairs={{0,2},{2,0},{4,6},{6,4},{1,3},{3,1},{5,7},{7,5},{8,10},{10,8},{12,... | collective-permute-start | bytes 98312 | tf_op jit(solution)/shard_map/ppermute | solution.py:273
  74.2 5.2 %collective-permute-start.23 = (bf16[32,512]{1,0:T(8,128)(2,1)S(1)}, bf16[32,512]{1,0:T(8,128)(2,1)S(1)}, u32[]{:S(2)}, u32[]{:S(2)}) collective-permute-start(bf16[32,512]{1,0:T(8,128)(2,1)S(1)} %get-tuple-element.69), channel_id=1, source_target_pairs={{0,4},{2,6},{4,0},{6,2},{1,5},{3,7},{5,1},{7,3},{8,12},{10,14},{12... | collective-permute-start | bytes 98312 | tf_op jit(solution)/shard_map/ppermute | solution.py:273
  75.2 5.7 %collective-permute-start.22 = (bf16[32,512]{1,0:T(8,128)(2,1)S(1)}, bf16[32,512]{1,0:T(8,128)(2,1)S(1)}, u32[]{:S(2)}, u32[]{:S(2)}) collective-permute-start(bf16[32,512]{1,0:T(8,128)(2,1)S(1)} %get-tuple-element.69), channel_id=1, source_target_pairs={{0,6},{2,4},{4,2},{6,0},{1,7},{3,5},{5,3},{7,1},{8,14},{10,12},{12... | collective-permute-start | bytes 98312 | tf_op jit(solution)/shard_map/ppermute | solution.py:273
  (17 other events, 199.2 us)

commit v4 on v3

--- a/solution.py
+++ b/solution.py
@@ -10,20 +10,30 @@
 
 BF16 = jnp.bfloat16
 F32 = jnp.float32
-VMEM_BYTES = 56 * 1024 * 1024
+LEAF_VMEM_BYTES = 56 * 1024 * 1024
+OWN_VMEM_BYTES = 52 * 1024 * 1024
+LARGE_VMEM_BYTES = 50 * 1024 * 1024
 STEP_VMEM_BYTES = 16 * 1024 * 1024
 
 
 def times_transposed(left, right):
     return lax.dot_general(left, right, (((1,), (1,)), ((), ())), preferred_element_type=F32)
+
+
+def masked_terms(parent_ref, wanted, rounded, mid):
+    leaves = mid.shape[0]
+    weights = [jnp.where(parent_ref[i] == wanted, 1.0, 0.0).astype(BF16) for i in range(leaves)]
+    left = jnp.concatenate([rounded[i] * weights[i] for i in range(leaves)], axis=1)
+    right = jnp.concatenate([mid[i] for i in range(leaves)], axis=1)
+    return times_transposed(left, right)
 
 
 def leaf_kernel(
     slots, parent_ref, rhs_ref, inv_ref, mid_ref, solved_ref, round_ref, *rest
 ):
-    terms_refs, (rhs, inv, mid, solved, total, rhs_sems, inv_sems, mid_sem, out_sems) = rest[:slots], rest[slots:]
+    terms_refs = rest[: len(rest) - 11]
+    rhs, inv, mid, solved, rounded, total, rhs_sems, inv_sems, mid_sem, out_sems, round_sems = rest[len(rest) - 11 :]
     leaves = rhs.shape[0]
-    first = lax.axis_index("col") if slots == 2 else 0
     rhs_copies = [pltpu.make_async_copy(rhs_ref.at[i], rhs.at[i], rhs_sems.at[i]) for i in range(leaves)]
     inv_copies = [pltpu.make_async_copy(inv_ref.at[i], inv.at[i], inv_sems.at[i]) for i in range(leaves)]
     mid_copy = pltpu.make_async_copy(mid_ref, mid, mid_sem)
@@ -36,20 +46,18 @@
         inv_copies[i].wait()
         rhs_copies[i].wait()
         solved[i] = times_transposed(rhs[i].astype(BF16), inv[i])
+        rounded[i] = solved[i].astype(BF16)
         out_copies.append(pltpu.make_async_copy(solved.at[i], solved_ref.at[i], out_sems.at[i]))
-        out_copies[i].start()
-        round_ref[i] = solved[i].astype(BF16)
+        out_copies.append(pltpu.make_async_copy(rounded.at[i], round_ref.at[i], round_sems.at[i]))
+        for copy in out_copies[-2:]:
+            copy.start()
     mid_copy.wait()
     if slots == 2:
-        right = jnp.concatenate([mid[i] for i in range(leaves)], axis=1)
-        for s, ref in enumerate(terms_refs):
-            weights = [jnp.where(parent_ref[i] ^ first == s, 1.0, 0.0).astype(BF16) for i in range(leaves)]
-            left = jnp.concatenate([round_ref[i] * weights[i] for i in range(leaves)], axis=1)
-            ref[...] = times_transposed(left, right).astype(ref.dtype)
+        terms_refs[0][...] = masked_terms(parent_ref, 1 - lax.axis_index("col"), rounded, mid).astype(BF16)
     else:
         total[...] = jnp.zeros_like(total)
         for i in range(leaves):
-            total[parent_ref[i]] += times_transposed(round_ref[i], mid[i])
+            total[parent_ref[i]] += times_transposed(rounded[i], mid[i])
         for s, ref in enumerate(terms_refs):
             ref[...] = total[s].astype(ref.dtype)
     for copy in out_copies:
@@ -59,28 +67,31 @@
 def leaf_solve(parent, rhs, inv, lower_mid, slots):
     leaves, rows, size = rhs.shape
     width = inv.shape[1]
+    given = 1 if slots == 2 else slots
     hbm, vmem = pl.BlockSpec(memory_space=pltpu.HBM), pl.BlockSpec(memory_space=pltpu.VMEM)
     return pl.pallas_call(
         functools.partial(leaf_kernel, slots),
         in_specs=[pl.BlockSpec(memory_space=pltpu.SMEM), hbm, hbm, hbm],
-        out_specs=[hbm] + [vmem] * (1 + slots),
+        out_specs=[hbm, hbm] + [vmem] * given,
         out_shape=[
             jax.ShapeDtypeStruct((leaves, rows, width), F32),
             jax.ShapeDtypeStruct((leaves, rows, width), BF16),
         ]
-        + [jax.ShapeDtypeStruct((rows, size), BF16)] * slots,
+        + [jax.ShapeDtypeStruct((rows, size), BF16)] * given,
         scratch_shapes=[
             pltpu.VMEM(rhs.shape, F32),
             pltpu.VMEM(inv.shape, BF16),
             pltpu.VMEM(lower_mid.shape, BF16),
             pltpu.VMEM((leaves, rows, width), F32),
+            pltpu.VMEM((leaves, rows, width), BF16),
             pltpu.VMEM((8, 128) if slots == 2 else (slots, rows, size), F32),
             pltpu.SemaphoreType.DMA((leaves,)),
             pltpu.SemaphoreType.DMA((leaves,)),
             pltpu.SemaphoreType.DMA,
             pltpu.SemaphoreType.DMA((leaves,)),
+            pltpu.SemaphoreType.DMA((leaves,)),
         ],
-        compiler_params=pltpu.CompilerParams(vmem_limit_bytes=VMEM_BYTES),
+        compiler_params=pltpu.CompilerParams(vmem_limit_bytes=LEAF_VMEM_BYTES),
         cost_estimate=pl.CostEstimate(
             flops=4 * leaves * rows * size * width,
             bytes_accessed=leaves * (rows * size * 4 + 4 * width * size + rows * width * 6),
@@ -88,6 +99,46 @@
         ),
         name="leaf_solve",
     )(parent, rhs, inv, lower_mid)
+
+
+def own_terms_kernel(parent_ref, round_ref, mid_ref, rhs_ref, terms_ref, rhs_rows_ref, rounded, mid, sems):
+    length = rhs_rows_ref.shape[0]
+    copies = [
+        pltpu.make_async_copy(round_ref, rounded, sems.at[0]),
+        pltpu.make_async_copy(mid_ref, mid, sems.at[1]),
+        pltpu.make_async_copy(rhs_ref.at[0, piece(lax.axis_index("row"), length)], rhs_rows_ref, sems.at[2]),
+    ]
+    for copy in copies:
+        copy.start()
+    for copy in copies:
+        copy.wait()
+    terms_ref[...] = masked_terms(parent_ref, lax.axis_index("col"), rounded, mid).astype(BF16)
+
+
+def own_terms(parent, rounded, lower_mid, mid_rhs):
+    rows, size = mid_rhs.shape[1:]
+    hbm, vmem = pl.BlockSpec(memory_space=pltpu.HBM), pl.BlockSpec(memory_space=pltpu.VMEM)
+    return pl.pallas_call(
+        own_terms_kernel,
+        in_specs=[pl.BlockSpec(memory_space=pltpu.SMEM), hbm, hbm, hbm],
+        out_specs=[vmem, vmem],
+        out_shape=[
+            jax.ShapeDtypeStruct((rows, size), BF16),
+            jax.ShapeDtypeStruct((rows // lax.axis_size("row"), size), F32),
+        ],
+        scratch_shapes=[
+            pltpu.VMEM(rounded.shape, BF16),
+            pltpu.VMEM(lower_mid.shape, BF16),
+            pltpu.SemaphoreType.DMA((3,)),
+        ],
+        compiler_params=pltpu.CompilerParams(vmem_limit_bytes=OWN_VMEM_BYTES),
+        cost_estimate=pl.CostEstimate(
+            flops=2 * rows * size * lower_mid.shape[0] * lower_mid.shape[2],
+            bytes_accessed=2 * (math.prod(rounded.shape) + math.prod(lower_mid.shape)),
+            transcendentals=0,
+        ),
+        name="own_terms",
+    )(parent, rounded, lower_mid, mid_rhs)
 
 
 def coupling_kernel(pattern_ref, round_ref, lower_ref, up_ref, rounded, lower, round_sem, sems):
@@ -100,7 +151,7 @@
     round_copy.wait()
     for k in range(kinds):
         copies[k].wait()
-        left = [rounded[i] * pattern_ref[i, k].astype(F32).astype(BF16) for i in range(leaves)]
+        left = [rounded[i] * pattern_ref[k, i].astype(F32).astype(BF16) for i in range(leaves)]
         right = [lower[i, k] for i in range(leaves)]
         up_ref[k] = times_transposed(jnp.concatenate(left, axis=1), jnp.concatenate(right, axis=1))
 
@@ -120,7 +171,7 @@
             pltpu.SemaphoreType.DMA,
             pltpu.SemaphoreType.DMA((kinds,)),
         ],
-        compiler_params=pltpu.CompilerParams(vmem_limit_bytes=STEP_VMEM_BYTES),
+        compiler_params=pltpu.CompilerParams(vmem_limit_bytes=LARGE_VMEM_BYTES),
         cost_estimate=pl.CostEstimate(
             flops=2 * leaves * kinds * rows * size * width,
             bytes_accessed=leaves * (rows * width * 2 + kinds * size * width * 2) + kinds * rows * size * 4,
@@ -198,10 +249,11 @@
 
     leaf_solved, leaf_round, *terms = leaf_solve(leaf_parent, leaf_rhs, leaf_inv, leaf_lower_mid, cols)
     if cols == 2:
-        mid_part = terms[0].astype(F32) + swap(terms[1], "col", 0).astype(F32)
+        own, _ = own_terms(leaf_parent, leaf_round, leaf_lower_mid, mid_rhs)
+        mid_part = own.astype(F32) + swap(terms[0], "col", 0).astype(F32)
     else:
         mid_part = scatter_sum(jnp.stack(terms), "col")
-    layer_up = leaf_coupling(leaf_pattern, leaf_round, leaf_lower_coupling)
+    layer_up = leaf_coupling(leaf_pattern.T, leaf_round, leaf_lower_coupling)
     quarter = rhs_count // rows
     mid_sum = scatter_sum(mid_part.reshape(rows, quarter, size), "row")
     mid_total = lax.dynamic_slice_in_dim(mid_rhs[0], row * quarter, quarter, 0) - mid_sum
@@ -310,16 +362,16 @@
 ROW_MOVES = [{"row": d} for d in (3, 2, 1)]
 
 
-def mid_pieces_kernel(terms_ref, other_ref, kept_ref, *given_refs):
+def mid_pieces_kernel(rhs_ref, terms_ref, other_ref, kept_ref, *given_refs):
     row, length = lax.axis_index("row"), kept_ref.shape[0]
     for d, ref in zip((0, 3, 2, 1), (kept_ref,) + given_refs):
         at = piece(row ^ d, length)
-        ref[...] = (terms_ref[at].astype(F32) + other_ref[at].astype(F32)).astype(ref.dtype)
-
-
-def mid_total_kernel(rhs_ref, kept_ref, r1, r2, r3, ready_ref):
-    at = piece(lax.axis_index("row"), ready_ref.shape[0])
-    ready_ref[...] = (rhs_ref[0, at] - widened(kept_ref, r1, r2, r3)).astype(BF16)
+        total = terms_ref[at].astype(F32) + other_ref[at].astype(F32)
+        ref[...] = rhs_ref[...] - total if d == 0 else total.astype(BF16)
+
+
+def mid_total_kernel(kept_ref, r1, r2, r3, ready_ref):
+    ready_ref[...] = (kept_ref[...] - widened(r1, r2, r3)).astype(BF16)
 
 
 def mid_solve_kernel(
@@ -345,8 +397,7 @@
             late_given_ref[k - 1, half] = total[piece(half * 2 + 1 - core, length)].astype(BF16)
 
 
-def top_share_kernel(terms_ref, inv_ref, own_ref, share_ref):
-    own_ref[...] = terms_ref[...]
+def top_share_kernel(inv_ref, share_ref):
     length = share_ref.shape[1]
     share_ref[...] = inv_ref[0, :, piece(lax.axis_index("col"), length)]
 
@@ -439,19 +490,22 @@
     send_ref[...] = total.astype(BF16)
 
 
-def last_solve_kernel(
-    rhs_ref, inv_ref, own_ref, r3, r2, r1, front_ref, other_ref, top_ref, other_top_ref, solved_ref, send_ref, top_all_ref
-):
-    pair, col = lax.axis_index("gz") >> 1, lax.axis_index("col")
+def place_top_kernel(top_ref, other_ref, top_all_ref, done_ref):
+    done_ref[...] = jnp.zeros_like(done_ref)
+    col, part = lax.axis_index("col"), top_ref.shape[1]
+    for i in range(top_ref.shape[0]):
+        top_all_ref[0, piece(i * 2 + col, part)] = top_ref[i]
+        top_all_ref[0, piece(i * 2 + 1 - col, part)] = other_ref[i].astype(F32)
+
+
+def last_solve_kernel(rhs_ref, inv_ref, own_ref, r3, r2, r1, front_ref, other_ref, solved_ref, send_ref):
+    pair = lax.axis_index("gz") >> 1
     part, size = own_ref.shape
     ready = (apex_rows(rhs_ref, 2, pair, part) - widened(own_ref, r3, r2, r1)).astype(BF16)
     solved_ref[2] = times_transposed(ready, inv_ref[2])
     solved_ref[pair] = front_ref[...]
     solved_ref[1 - pair] = other_ref[:, size:].astype(F32)
     send_ref[...] = solved_ref[...].astype(BF16)
-    for i in range(top_ref.shape[0]):
-        top_all_ref[0, piece(i * 2 + col, part)] = top_ref[i]
-        top_all_ref[0, piece(i * 2 + 1 - col, part)] = other_top_ref[i].astype(F32)
 
 
 def place_apex_kernel(solved_ref, other_ref, apex_ref):
@@ -485,24 +539,25 @@
 
     rows = lax.axis_size("row")
 
-    leaf_solved, leaf_round, terms, other_terms = leaf_solve(leaf_parent, leaf_rhs, leaf_inv, leaf_lower_mid, 2)
+    leaf_solved, leaf_round, other_terms = leaf_solve(leaf_parent, leaf_rhs, leaf_inv, leaf_lower_mid, 2)
     (other_terms,) = partners(other_terms, [{"col": 1}])
-    layer_up = leaf_coupling(leaf_pattern, leaf_round, leaf_lower_coupling)
-
-    terms, share = whole_call(
-        top_share_kernel, "top_share", [terms, top_inv], [((count, size), BF16), ((width, size // 2), BF16)]
-    )
+    layer_up = leaf_coupling(leaf_pattern.T, leaf_round, leaf_lower_coupling)
+
+    (share,) = whole_call(top_share_kernel, "top_share", [top_inv], [((width, size // 2), BF16)])
     shares = partners(share, ROW_MOVES)
 
+    terms, rhs_rows = own_terms(leaf_parent, leaf_round, leaf_lower_mid, mid_rhs)
     kept, *given = whole_call(
-        mid_pieces_kernel, "mid_pieces", [terms, other_terms],
+        mid_pieces_kernel, "mid_pieces", [rhs_rows, terms, other_terms],
         [((quarter, size), F32)] + [((quarter, size), BF16)] * 3,
         after=shares,
     )
     arrived = partners(given, ROW_MOVES)
     (top_half,) = whole_call(half_top_kernel, "half_top", [share, *shares], [((size, size // 2), BF16)], after=[kept])
     (top_other,) = partners(top_half, [{"col": 1}])
-    (ready,) = whole_call(mid_total_kernel, "mid_total", [mid_rhs, kept, *arrived], [((quarter, size), BF16)])
+    (ready,) = whole_call(
+        mid_total_kernel, "mid_total", [kept, *arrived], [((quarter, size), BF16)], after=[layer_up]
+    )
     arrived = partners(ready, ROW_MOVES)
     (top_whole,) = whole_call(whole_top_kernel, "whole_top", [top_half, top_other], [((size, size), BF16)])
     mid_solved, kept, given, late_kept, late_given = whole_call(
@@ -556,11 +611,14 @@
         last_pieces_kernel, "last_pieces", [kept, other], [((part, size), F32), ((part, size), BF16)]
     )
     arrived = partners(send, ROW_MOVES)
-    solved, send, top_all = whole_call(
-        last_solve_kernel, "last_solve",
-        [apex_rhs, apex_inv, own, *arrived, front, other, top_solved, other_top],
-        [((3, part, width), F32), ((3, part, width), BF16), ((1, count, width), F32)],
+    top_all, placed = whole_call(
+        place_top_kernel, "place_top", [top_solved, other_top], [((1, count, width), F32), ((8, width), F32)], after=[own]
+    )
+    solved, send = whole_call(
+        last_solve_kernel, "last_solve", [apex_rhs, apex_inv, own, *arrived, front, other],
+        [((3, part, width), F32), ((3, part, width), BF16)],
         flops=count * size * width // 4,
+        after=[placed],
     )
     (other,) = partners(send, [{"col": 1}])
     (apex,) = whole_call(place_apex_kernel, "place_apex", [solved, other], [((3, 2 * part, width), F32)])

time: 86.4 us -> 81.5 us (0.943)
  waiting for transfers between devices: 28.3 us -> 25 us
  local copies, waits for them, and re-layouts: 3.17 us -> 1.1 us
    ppermute x27, waiting for transfers between devices: 28.3 us -> 25 us  [partners(): arrived.append(lax.ppermute(item, axes, route))]
    pallas_call x14 -> x15, Pallas kernels: 7.13 us -> 4.7 us  [whole_call(): pl.pallas_call(body, in_specs=[pl.BlockSpec(memory_space=pl.ANY)] * len(a...]
    pallas_call x0 -> x1, Pallas kernels: none -> 2.31 us  [own_terms(): pl.pallas_call(own_terms_kernel, in_specs=[pl.BlockSpec(memory_space=pltp...]
    unnamed x29 -> x26, local copies, waits for them, and re-layouts: 3.17 us -> 1.1 us
    pallas_call x1, Pallas kernels: 2.29 us -> 3.27 us  [leaf_coupling(): pl.pallas_call(coupling_kernel, in_specs=[pl.BlockSpec(memory_space=pltpu...]
  transfers between devices with their start and end apart: 27 -> 27, of which waited for: 13 -> 14; matrix products, arithmetic and copies ran while one was open for 0% -> 0% of each run, Pallas kernels for 6% -> 8%
where the time goes in v4:
time: 81.5 us; the launch traced here: 81.3 us
  starting transfers between devices  38.1 us (47%)
  waiting for transfers between devices  25 us (31%)
  Pallas kernels  16.1 us (20%)
  local copies, waits for them, and re-layouts  1.1 us (1%)
  between operations  0.88 us (1%)
    ppermute x27, starting transfers between devices, partners(): arrived.append(lax.ppermute(item, axes, route))  38.1 us
    ppermute x27, waiting for transfers between devices, partners(): arrived.append(lax.ppermute(item, axes, route))  25 us
    pallas_call x1, Pallas kernels, leaf_solve(): pl.pallas_call(functools.partial(leaf_kernel, slots), in_specs=[pl.BlockS...  5.86 us
    pallas_call x15, Pallas kernels, whole_call(): pl.pallas_call(body, in_specs=[pl.BlockSpec(memory_space=pl.ANY)] * len(a...  4.7 us
    pallas_call x1, Pallas kernels, leaf_coupling(): pl.pallas_call(coupling_kernel, in_specs=[pl.BlockSpec(memory_space=pltpu...  3.27 us
    pallas_call x1, Pallas kernels, own_terms(): pl.pallas_call(own_terms_kernel, in_specs=[pl.BlockSpec(memory_space=pltp...  2.31 us
  transfers between devices with their start and end apart: 27, of which 14 were waited for; matrix products, arithmetic and copies ran while one was open for 0% of the time, Pallas kernels for 8%

profile of v4, /device:TPU:0, one launch (start us, length us, event | category | flops | bytes accessed | tf_op | source)
XLA Modules:
  0.0 81.3 jit_solution(14433066792558266599)
XLA Ops:
  0.7 5.9 %leaf_solve.1 = (f32[8,256,128]{2,1,0:T(8,128)}, bf16[8,256,128]{2,1,0:T(8,128)(2,1)}, bf16[256,512]{1,0:T(8,128)(2,1)}) custom-call(s32[8]{0:T(128)} %parent_ref.3, f32[8,256,512]{2,1,0:T(8,128)} %rhs_ref.2, bf16[8,128,512]{2,1,0:T(8,128)(2,1)} %inv_ref.1, bf16[8,512,128]{2,1,0:T(8,128)(2,1)} %mid_ref.3), custom_call_target="tpu_custom_call" | custom-call | flops 536870912 | bytes 7864320 | tf_op jit(solution)/shard_map/leaf_solve/pallas_call | solution.py:72
  6.5 3.0 %collective-permute-start.3 = (bf16[256,512]{1,0:T(8,128)(2,1)}, bf16[256,512]{1,0:T(8,128)(2,1)S(1)}, u32[]{:S(2)}, u32[]{:S(2)}) collective-permute-start(bf16[256,512]{1,0:T(8,128)(2,1)} %get-tuple-element.44), channel_id=1, source_target_pairs={{0,1},{1,0},{2,3},{3,2},{4,5},{5,4},{6,7},{7,6},{8,9},{9,8},{10,11... | collective-permute-start | bytes 786440 | tf_op jit(solution)/shard_map/ppermute | solution.py:325
  9.6 1.6 %collective-permute-start.2 = (bf16[128,256]{1,0:T(8,128)(2,1)S(1)}, bf16[128,256]{1,0:T(8,128)(2,1)S(1)}, u32[]{:S(2)}, u32[]{:S(2)}) collective-permute-start(bf16[128,256]{1,0:T(8,128)(2,1)S(1)} %top_share.1.refs_1_), channel_id=1, source_target_pairs={{0,2},{2,0},{4,6},{6,4},{1,3},{3,1},{5,7},{7,5},{8,10},{10,8},{12,... | collective-permute-start | bytes 196616 | tf_op jit(solution)/shard_map/ppermute | solution.py:325
  11.2 2.6 %collective-permute-start.1 = (bf16[128,256]{1,0:T(8,128)(2,1)S(1)}, bf16[128,256]{1,0:T(8,128)(2,1)S(1)}, u32[]{:S(2)}, u32[]{:S(2)}) collective-permute-start(bf16[128,256]{1,0:T(8,128)(2,1)S(1)} %top_share.1.refs_1_), channel_id=1, source_target_pairs={{0,4},{2,6},{4,0},{6,2},{1,5},{3,7},{5,1},{7,3},{8,12},{10,14},{12... | collective-permute-start | bytes 196616 | tf_op jit(solution)/shard_map/ppermute | solution.py:325
  15.1 2.3 %own_terms.1 = (bf16[256,512]{1,0:T(8,128)(2,1)S(1)}, f32[64,512]{1,0:T(8,128)S(1)}) custom-call(s32[8]{0:T(128)S(1)} %copy-done.11, bf16[8,256,128]{2,1,0:T(8,128)(2,1)S(1)} %copy-done.1, bf16[8,512,128]{2,1,0:T(8,128)(2,1)} %mid_ref.3, f32[1,256,512]{2,1,0:T(8,128)S(1)} %copy-done.3), custom_call_target="tpu_custom_call" | custom-call | flops 268435456 | bytes 1572864 | tf_op jit(solution)/shard_map/own_terms/pallas_call | solution.py:121
  18.2 1.7 %collective-permute-done.refs_0_.refs_2_ = bf16[128,256]{1,0:T(8,128)(2,1)S(1)} collective-permute-done((bf16[128,256]{1,0:T(8,128)(2,1)S(1)}, bf16[128,256]{1,0:T(8,128)(2,1)S(1)}, u32[]{:S(2)}, u32[]{:S(2)}) %collective-permute-start) | collective-permute-done | bytes 65568 | tf_op jit(solution)/shard_map/ppermute | solution.py:325
  22.1 2.9 %collective-permute-start.7 = (bf16[64,512]{1,0:T(8,128)(2,1)S(1)}, bf16[64,512]{1,0:T(8,128)(2,1)S(1)}, u32[]{:S(2)}, u32[]{:S(2)}) collective-permute-start(bf16[64,512]{1,0:T(8,128)(2,1)S(1)} %get-tuple-element.48), channel_id=1, source_target_pairs={{0,2},{2,0},{4,6},{6,4},{1,3},{3,1},{5,7},{7,5},{8,10},{10,8},{12,... | collective-permute-start | bytes 196616 | tf_op jit(solution)/shard_map/ppermute | solution.py:325
  25.0 3.3 %leaf_coupling.1.refs_0_.refs_8_ = f32[3,256,512]{2,1,0:T(8,128)S(1)} custom-call(s32[3,8]{1,0:T(4,128)S(1)} %bitcast.2, bf16[8,256,128]{2,1,0:T(8,128)(2,1)S(1)} %copy-done.1, bf16[8,3,512,128]{3,2,1,0:T(8,128)(2,1)} %lower_ref.1), custom_call_target="tpu_custom_call" | custom-call | flops 805306368 | bytes 5242880 | tf_op jit(solution)/shard_map/leaf_coupling/pallas_call | solution.py:163
  28.3 1.5 %collective-permute-start.10 = (bf16[64,512]{1,0:T(8,128)(2,1)S(1)}, bf16[64,512]{1,0:T(8,128)(2,1)S(1)}, u32[]{:S(2)}, u32[]{:S(2)}) collective-permute-start(bf16[64,512]{1,0:T(8,128)(2,1)S(1)} %mid_total.1.refs_2_), channel_id=1, source_target_pairs={{0,2},{2,0},{4,6},{6,4},{1,3},{3,1},{5,7},{7,5},{8,10},{10,8},{12,... | collective-permute-start | bytes 196616 | tf_op jit(solution)/shard_map/ppermute | solution.py:325
  30.5 2.3 %collective-permute-start.8 = (bf16[64,512]{1,0:T(8,128)(2,1)S(1)}, bf16[64,512]{1,0:T(8,128)(2,1)S(1)}, u32[]{:S(2)}, u32[]{:S(2)}) collective-permute-start(bf16[64,512]{1,0:T(8,128)(2,1)S(1)} %mid_total.1.refs_2_), channel_id=1, source_target_pairs={{0,6},{2,4},{4,2},{6,0},{1,7},{3,5},{5,3},{7,1},{8,14},{10,12},{12... | collective-permute-start | bytes 196616 | tf_op jit(solution)/shard_map/ppermute | solution.py:325
  33.1 2.6 %collective-permute-done.9.refs_4_ = bf16[64,512]{1,0:T(8,128)(2,1)S(1)} collective-permute-done((bf16[64,512]{1,0:T(8,128)(2,1)S(1)}, bf16[64,512]{1,0:T(8,128)(2,1)S(1)}, u32[]{:S(2)}, u32[]{:S(2)}) %collective-permute-start.9) | collective-permute-done | bytes 65568 | tf_op jit(solution)/shard_map/ppermute | solution.py:325
  36.7 1.9 %mid_solve.1 = (f32[256,128]{1,0:T(8,128)}, f32[4,32,512]{2,1,0:T(8,128)S(1)}, bf16[4,32,512]{2,1,0:T(8,128)(2,1)S(1)}, f32[2,2,64,512]{3,2,1,0:T(8,128)S(1)}, bf16[2,2,64,512]{3,2,1,0:T(8,128)(2,1)S(1)}) custom-call(bf16[512,512]{1,0:T(8,128)(2,1)S(1)} %whole_top.1.refs_0_.refs_4_, s32[1,2]{1,0:T(1,128)S(1)} %copy-done.12, ...), custom_call_target="tpu_custom_call" | custom-call | flops 134217728 | bytes 3670024 | tf_op jit(solution)/shard_map/mid_solve/pallas_call | solution.py:337
  38.5 1.5 %collective-permute-start.12 = (bf16[4,32,512]{2,1,0:T(8,128)(2,1)S(1)}, bf16[4,32,512]{2,1,0:T(8,128)(2,1)S(1)}, u32[]{:S(2)}, u32[]{:S(2)}) collective-permute-start(bf16[4,32,512]{2,1,0:T(8,128)(2,1)S(1)} %get-tuple-element.54), channel_id=1, source_target_pairs={{0,1},{1,0},{2,3},{3,2},{4,5},{5,4},{6,7},{7,6},{8,9},{9,8},{10,11... | collective-permute-start | bytes 393224 | tf_op jit(solution)/shard_map/ppermute | solution.py:325
  40.1 1.6 %collective-permute-start.16 = (bf16[2,2,32,512]{3,2,1,0:T(8,128)(2,1)S(1)}, bf16[2,2,32,512]{3,2,1,0:T(8,128)(2,1)S(1)}, u32[]{:S(2)}, u32[]{:S(2)}) collective-permute-start(bf16[2,2,32,512]{3,2,1,0:T(8,128)(2,1)S(1)} %get-tuple-element.52.refs_0_), channel_id=1, source_target_pairs={{0,1},{1,0},{2,3},{3,2},{4,5},{5,4},{6,7},{7,6},{8,9},{9,8},{10,11... | collective-permute-start | bytes 393224 | tf_op jit(solution)/shard_map/ppermute | solution.py:325
  41.7 3.1 %collective-permute-done.12.refs_3_ = bf16[4,32,512]{2,1,0:T(8,128)(2,1)S(1)} collective-permute-done((bf16[4,32,512]{2,1,0:T(8,128)(2,1)S(1)}, bf16[4,32,512]{2,1,0:T(8,128)(2,1)S(1)}, u32[]{:S(2)}, u32[]{:S(2)}) %collective-permute-start.12) | collective-permute-done | bytes 131104 | tf_op jit(solution)/shard_map/ppermute | solution.py:325
  45.2 2.3 %collective-permute-start.13 = (bf16[128,128]{1,0:T(8,128)(2,1)S(1)}, bf16[128,128]{1,0:T(8,128)(2,1)S(1)}, u32[]{:S(2)}, u32[]{:S(2)}) collective-permute-start(bf16[128,128]{1,0:T(8,128)(2,1)S(1)} %get-tuple-element.56), channel_id=1, source_target_pairs={{0,6},{2,4},{4,2},{6,0},{1,7},{3,5},{5,3},{7,1},{8,14},{10,12},{12... | collective-permute-start | bytes 98312 | tf_op jit(solution)/shard_map/ppermute | solution.py:325
  47.8 1.9 %collective-permute-start.15 = (bf16[128,128]{1,0:T(8,128)(2,1)S(1)}, bf16[128,128]{1,0:T(8,128)(2,1)S(1)}, u32[]{:S(2)}, u32[]{:S(2)}) collective-permute-start(bf16[128,128]{1,0:T(8,128)(2,1)S(1)} %get-tuple-element.58), channel_id=1, source_target_pairs={{0,2},{2,0},{4,6},{6,4},{1,3},{3,1},{5,7},{7,5},{8,10},{10,8},{12,... | collective-permute-start | bytes 98312 | tf_op jit(solution)/shard_map/ppermute | solution.py:325
  56.6 1.9 %collective-permute-start.18 = (bf16[64,512]{1,0:T(8,128)(2,1)S(1)}, bf16[64,512]{1,0:T(8,128)(2,1)S(1)}, u32[]{:S(2)}, u32[]{:S(2)}) collective-permute-start(bf16[64,512]{1,0:T(8,128)(2,1)S(1)} %get-tuple-element.63), channel_id=1, source_target_pairs={{0,6},{2,4},{4,2},{6,0},{1,7},{3,5},{5,3},{7,1},{8,14},{10,12},{12... | collective-permute-start | bytes 196616 | tf_op jit(solution)/shard_map/ppermute | solution.py:325
  58.5 5.1 %collective-permute-done.19.refs_3_ = bf16[64,512]{1,0:T(8,128)(2,1)S(1)} collective-permute-done((bf16[64,512]{1,0:T(8,128)(2,1)S(1)}, bf16[64,512]{1,0:T(8,128)(2,1)S(1)}, u32[]{:S(2)}, u32[]{:S(2)}) %collective-permute-start.19) | collective-permute-done | bytes 65568 | tf_op jit(solution)/shard_map/ppermute | solution.py:325
  64.0 1.6 %collective-permute-start.21 = (bf16[32,640]{1,0:T(8,128)(2,1)S(1)}, bf16[32,640]{1,0:T(8,128)(2,1)S(1)}, u32[]{:S(2)}, u32[]{:S(2)}) collective-permute-start(bf16[32,640]{1,0:T(8,128)(2,1)S(1)} %get-tuple-element.66), channel_id=1, source_target_pairs={{0,16},{8,24},{16,0},{24,8},{1,17},{9,25},{17,1},{25,9},{2,18},{10... | collective-permute-start | bytes 122888 | tf_op jit(solution)/shard_map/ppermute | solution.py:325
  70.8 1.7 %collective-permute-start.23 = (bf16[32,512]{1,0:T(8,128)(2,1)S(1)}, bf16[32,512]{1,0:T(8,128)(2,1)S(1)}, u32[]{:S(2)}, u32[]{:S(2)}) collective-permute-start(bf16[32,512]{1,0:T(8,128)(2,1)S(1)} %get-tuple-element.72), channel_id=1, source_target_pairs={{0,6},{2,4},{4,2},{6,0},{1,7},{3,5},{5,3},{7,1},{8,14},{10,12},{12... | collective-permute-start | bytes 98312 | tf_op jit(solution)/shard_map/ppermute | solution.py:325
  74.7 1.9 %collective-permute-done.23.refs_4_ = bf16[32,512]{1,0:T(8,128)(2,1)S(1)} collective-permute-done((bf16[32,512]{1,0:T(8,128)(2,1)S(1)}, bf16[32,512]{1,0:T(8,128)(2,1)S(1)}, u32[]{:S(2)}, u32[]{:S(2)}) %collective-permute-start.23) | collective-permute-done | bytes 32800 | tf_op jit(solution)/shard_map/ppermute | solution.py:325
  76.7 1.6 %collective-permute-start.26 = (bf16[3,32,128]{2,1,0:T(8,128)(2,1)S(1)}, bf16[3,32,128]{2,1,0:T(8,128)(2,1)S(1)}, u32[]{:S(2)}, u32[]{:S(2)}) collective-permute-start(bf16[3,32,128]{2,1,0:T(8,128)(2,1)S(1)} %get-tuple-element.75), channel_id=1, source_target_pairs={{0,1},{1,0},{2,3},{3,2},{4,5},{5,4},{6,7},{7,6},{8,9},{9,8},{10,11... | collective-permute-start | bytes 73736 | tf_op jit(solution)/shard_map/ppermute | solution.py:325
  78.3 2.3 %collective-permute-done.26.refs_1_ = bf16[3,32,128]{2,1,0:T(8,128)(2,1)S(1)} collective-permute-done((bf16[3,32,128]{2,1,0:T(8,128)(2,1)S(1)}, bf16[3,32,128]{2,1,0:T(8,128)(2,1)S(1)}, u32[]{:S(2)}, u32[]{:S(2)}) %collective-permute-start.26) | collective-permute-done | bytes 24608 | tf_op jit(solution)/shard_map/ppermute | solution.py:325
  (74 shorter events, 22.4 us)
Async XLA Ops:
  6.5 13.3 %collective-permute-start.3 = (bf16[256,512]{1,0:T(8,128)(2,1)}, bf16[256,512]{1,0:T(8,128)(2,1)S(1)}, u32[]{:S(2)}, u32[]{:S(2)}) collective-permute-start(bf16[256,512]{1,0:T(8,128)(2,1)} %get-tuple-element.44), channel_id=1, source_target_pairs={{0,1},{1,0},{2,3},{3,2},{4,5},{5,4},{6,7},{7,6},{8,9},{9,8},{10,11... | collective-permute-start | bytes 786440 | tf_op jit(solution)/shard_map/ppermute | solution.py:325
  9.6 7.8 %collective-permute-start.2 = (bf16[128,256]{1,0:T(8,128)(2,1)S(1)}, bf16[128,256]{1,0:T(8,128)(2,1)S(1)}, u32[]{:S(2)}, u32[]{:S(2)}) collective-permute-start(bf16[128,256]{1,0:T(8,128)(2,1)S(1)} %top_share.1.refs_1_), channel_id=1, source_target_pairs={{0,2},{2,0},{4,6},{6,4},{1,3},{3,1},{5,7},{7,5},{8,10},{10,8},{12,... | collective-permute-start | bytes 196616 | tf_op jit(solution)/shard_map/ppermute | solution.py:325
  11.2 7.0 %collective-permute-start.1 = (bf16[128,256]{1,0:T(8,128)(2,1)S(1)}, bf16[128,256]{1,0:T(8,128)(2,1)S(1)}, u32[]{:S(2)}, u32[]{:S(2)}) collective-permute-start(bf16[128,256]{1,0:T(8,128)(2,1)S(1)} %top_share.1.refs_1_), channel_id=1, source_target_pairs={{0,4},{2,6},{4,0},{6,2},{1,5},{3,7},{5,1},{7,3},{8,12},{10,14},{12... | collective-permute-start | bytes 196616 | tf_op jit(solution)/shard_map/ppermute | solution.py:325
  13.8 6.1 %collective-permute-start = (bf16[128,256]{1,0:T(8,128)(2,1)S(1)}, bf16[128,256]{1,0:T(8,128)(2,1)S(1)}, u32[]{:S(2)}, u32[]{:S(2)}) collective-permute-start(bf16[128,256]{1,0:T(8,128)(2,1)S(1)} %top_share.1.refs_1_), channel_id=1, source_target_pairs={{0,6},{2,4},{4,2},{6,0},{1,7},{3,5},{5,3},{7,1},{8,14},{10,12},{12... | collective-permute-start | bytes 196616 | tf_op jit(solution)/shard_map/ppermute | solution.py:325
  20.0 12.8 %collective-permute-start.4 = (bf16[512,256]{1,0:T(8,128)(2,1)S(1)}, bf16[512,256]{1,0:T(8,128)(2,1)S(1)}, u32[]{:S(2)}, u32[]{:S(2)}) collective-permute-start(bf16[512,256]{1,0:T(8,128)(2,1)S(1)} %half_top.1.refs_0_), channel_id=1, source_target_pairs={{0,1},{1,0},{2,3},{3,2},{4,5},{5,4},{6,7},{7,6},{8,9},{9,8},{10,11... | collective-permute-start | bytes 786440 | tf_op jit(solution)/shard_map/ppermute | solution.py:325
  20.6 7.7 %collective-permute-start.5 = (bf16[64,512]{1,0:T(8,128)(2,1)S(1)}, bf16[64,512]{1,0:T(8,128)(2,1)S(1)}, u32[]{:S(2)}, u32[]{:S(2)}) collective-permute-start(bf16[64,512]{1,0:T(8,128)(2,1)S(1)} %get-tuple-element.46), channel_id=1, source_target_pairs={{0,6},{2,4},{4,2},{6,0},{1,7},{3,5},{5,3},{7,1},{8,14},{10,12},{12... | collective-permute-start | bytes 196616 | tf_op jit(solution)/shard_map/ppermute | solution.py:325
  22.1 6.2 %collective-permute-start.6 = (bf16[64,512]{1,0:T(8,128)(2,1)S(1)}, bf16[64,512]{1,0:T(8,128)(2,1)S(1)}, u32[]{:S(2)}, u32[]{:S(2)}) collective-permute-start(bf16[64,512]{1,0:T(8,128)(2,1)S(1)} %get-tuple-element.47), channel_id=1, source_target_pairs={{0,4},{2,6},{4,0},{6,2},{1,5},{3,7},{5,1},{7,3},{8,12},{10,14},{12... | collective-permute-start | bytes 196616 | tf_op jit(solution)/shard_map/ppermute | solution.py:325
  22.1 6.2 %collective-permute-start.7 = (bf16[64,512]{1,0:T(8,128)(2,1)S(1)}, bf16[64,512]{1,0:T(8,128)(2,1)S(1)}, u32[]{:S(2)}, u32[]{:S(2)}) collective-permute-start(bf16[64,512]{1,0:T(8,128)(2,1)S(1)} %get-tuple-element.48), channel_id=1, source_target_pairs={{0,2},{2,0},{4,6},{6,4},{1,3},{3,1},{5,7},{7,5},{8,10},{10,8},{12,... | collective-permute-start | bytes 196616 | tf_op jit(solution)/shard_map/ppermute | solution.py:325
  28.3 4.8 %collective-permute-start.10 = (bf16[64,512]{1,0:T(8,128)(2,1)S(1)}, bf16[64,512]{1,0:T(8,128)(2,1)S(1)}, u32[]{:S(2)}, u32[]{:S(2)}) collective-permute-start(bf16[64,512]{1,0:T(8,128)(2,1)S(1)} %mid_total.1.refs_2_), channel_id=1, source_target_pairs={{0,2},{2,0},{4,6},{6,4},{1,3},{3,1},{5,7},{7,5},{8,10},{10,8},{12,... | collective-permute-start | bytes 196616 | tf_op jit(solution)/shard_map/ppermute | solution.py:325
  29.9 5.9 %collective-permute-start.9 = (bf16[64,512]{1,0:T(8,128)(2,1)S(1)}, bf16[64,512]{1,0:T(8,128)(2,1)S(1)}, u32[]{:S(2)}, u32[]{:S(2)}) collective-permute-start(bf16[64,512]{1,0:T(8,128)(2,1)S(1)} %mid_total.1.refs_2_), channel_id=1, source_target_pairs={{0,4},{2,6},{4,0},{6,2},{1,5},{3,7},{5,1},{7,3},{8,12},{10,14},{12... | collective-permute-start | bytes 196616 | tf_op jit(solution)/shard_map/ppermute | solution.py:325
  30.5 6.2 %collective-permute-start.8 = (bf16[64,512]{1,0:T(8,128)(2,1)S(1)}, bf16[64,512]{1,0:T(8,128)(2,1)S(1)}, u32[]{:S(2)}, u32[]{:S(2)}) collective-permute-start(bf16[64,512]{1,0:T(8,128)(2,1)S(1)} %mid_total.1.refs_2_), channel_id=1, source_target_pairs={{0,6},{2,4},{4,2},{6,0},{1,7},{3,5},{5,3},{7,1},{8,14},{10,12},{12... | collective-permute-start | bytes 196616 | tf_op jit(solution)/shard_map/ppermute | solution.py:325
  38.5 6.3 %collective-permute-start.12 = (bf16[4,32,512]{2,1,0:T(8,128)(2,1)S(1)}, bf16[4,32,512]{2,1,0:T(8,128)(2,1)S(1)}, u32[]{:S(2)}, u32[]{:S(2)}) collective-permute-start(bf16[4,32,512]{2,1,0:T(8,128)(2,1)S(1)} %get-tuple-element.54), channel_id=1, source_target_pairs={{0,1},{1,0},{2,3},{3,2},{4,5},{5,4},{6,7},{7,6},{8,9},{9,8},{10,11... | collective-permute-start | bytes 393224 | tf_op jit(solution)/shard_map/ppermute | solution.py:325
  40.1 12.2 %collective-permute-start.16 = (bf16[2,2,32,512]{3,2,1,0:T(8,128)(2,1)S(1)}, bf16[2,2,32,512]{3,2,1,0:T(8,128)(2,1)S(1)}, u32[]{:S(2)}, u32[]{:S(2)}) collective-permute-start(bf16[2,2,32,512]{3,2,1,0:T(8,128)(2,1)S(1)} %get-tuple-element.52.refs_0_), channel_id=1, source_target_pairs={{0,1},{1,0},{2,3},{3,2},{4,5},{5,4},{6,7},{7,6},{8,9},{9,8},{10,11... | collective-permute-start | bytes 393224 | tf_op jit(solution)/shard_map/ppermute | solution.py:325
  45.2 5.8 %collective-permute-start.13 = (bf16[128,128]{1,0:T(8,128)(2,1)S(1)}, bf16[128,128]{1,0:T(8,128)(2,1)S(1)}, u32[]{:S(2)}, u32[]{:S(2)}) collective-permute-start(bf16[128,128]{1,0:T(8,128)(2,1)S(1)} %get-tuple-element.56), channel_id=1, source_target_pairs={{0,6},{2,4},{4,2},{6,0},{1,7},{3,5},{5,3},{7,1},{8,14},{10,12},{12... | collective-permute-start | bytes 98312 | tf_op jit(solution)/shard_map/ppermute | solution.py:325
  47.5 4.8 %collective-permute-start.14 = (bf16[128,128]{1,0:T(8,128)(2,1)S(1)}, bf16[128,128]{1,0:T(8,128)(2,1)S(1)}, u32[]{:S(2)}, u32[]{:S(2)}) collective-permute-start(bf16[128,128]{1,0:T(8,128)(2,1)S(1)} %get-tuple-element.57), channel_id=1, source_target_pairs={{0,4},{2,6},{4,0},{6,2},{1,5},{3,7},{5,1},{7,3},{8,12},{10,14},{12... | collective-permute-start | bytes 98312 | tf_op jit(solution)/shard_map/ppermute | solution.py:325
  47.8 4.5 %collective-permute-start.15 = (bf16[128,128]{1,0:T(8,128)(2,1)S(1)}, bf16[128,128]{1,0:T(8,128)(2,1)S(1)}, u32[]{:S(2)}, u32[]{:S(2)}) collective-permute-start(bf16[128,128]{1,0:T(8,128)(2,1)S(1)} %get-tuple-element.58), channel_id=1, source_target_pairs={{0,2},{2,0},{4,6},{6,4},{1,3},{3,1},{5,7},{7,5},{8,10},{10,8},{12,... | collective-permute-start | bytes 98312 | tf_op jit(solution)/shard_map/ppermute | solution.py:325
  54.1 4.5 %collective-permute-start.20 = (bf16[64,512]{1,0:T(8,128)(2,1)S(1)}, bf16[64,512]{1,0:T(8,128)(2,1)S(1)}, u32[]{:S(2)}, u32[]{:S(2)}) collective-permute-start(bf16[64,512]{1,0:T(8,128)(2,1)S(1)} %get-tuple-element.63), channel_id=1, source_target_pairs={{0,2},{2,0},{4,6},{6,4},{1,3},{3,1},{5,7},{7,5},{8,10},{10,8},{12,... | collective-permute-start | bytes 196616 | tf_op jit(solution)/shard_map/ppermute | solution.py:325
  55.4 8.2 %collective-permute-start.19 = (bf16[64,512]{1,0:T(8,128)(2,1)S(1)}, bf16[64,512]{1,0:T(8,128)(2,1)S(1)}, u32[]{:S(2)}, u32[]{:S(2)}) collective-permute-start(bf16[64,512]{1,0:T(8,128)(2,1)S(1)} %get-tuple-element.63), channel_id=1, source_target_pairs={{0,4},{2,6},{4,0},{6,2},{1,5},{3,7},{5,1},{7,3},{8,12},{10,14},{12... | collective-permute-start | bytes 196616 | tf_op jit(solution)/shard_map/ppermute | solution.py:325
  56.6 7.0 %collective-permute-start.18 = (bf16[64,512]{1,0:T(8,128)(2,1)S(1)}, bf16[64,512]{1,0:T(8,128)(2,1)S(1)}, u32[]{:S(2)}, u32[]{:S(2)}) collective-permute-start(bf16[64,512]{1,0:T(8,128)(2,1)S(1)} %get-tuple-element.63), channel_id=1, source_target_pairs={{0,6},{2,4},{4,2},{6,0},{1,7},{3,5},{5,3},{7,1},{8,14},{10,12},{12... | collective-permute-start | bytes 196616 | tf_op jit(solution)/shard_map/ppermute | solution.py:325
  64.0 4.1 %collective-permute-start.21 = (bf16[32,640]{1,0:T(8,128)(2,1)S(1)}, bf16[32,640]{1,0:T(8,128)(2,1)S(1)}, u32[]{:S(2)}, u32[]{:S(2)}) collective-permute-start(bf16[32,640]{1,0:T(8,128)(2,1)S(1)} %get-tuple-element.66), channel_id=1, source_target_pairs={{0,16},{8,24},{16,0},{24,8},{1,17},{9,25},{17,1},{25,9},{2,18},{10... | collective-permute-start | bytes 122888 | tf_op jit(solution)/shard_map/ppermute | solution.py:325
  65.6 7.0 %collective-permute-start.22 = (bf16[4,32,128]{2,1,0:T(8,128)(2,1)S(1)}, bf16[4,32,128]{2,1,0:T(8,128)(2,1)S(1)}, u32[]{:S(2)}, u32[]{:S(2)}) collective-permute-start(bf16[4,32,128]{2,1,0:T(8,128)(2,1)S(1)} %get-tuple-element.69), channel_id=1, source_target_pairs={{0,1},{1,0},{2,3},{3,2},{4,5},{5,4},{6,7},{7,6},{8,9},{9,8},{10,11... | collective-permute-start | bytes 98312 | tf_op jit(solution)/shard_map/ppermute | solution.py:325
  68.1 5.1 %collective-permute-start.25 = (bf16[32,512]{1,0:T(8,128)(2,1)S(1)}, bf16[32,512]{1,0:T(8,128)(2,1)S(1)}, u32[]{:S(2)}, u32[]{:S(2)}) collective-permute-start(bf16[32,512]{1,0:T(8,128)(2,1)S(1)} %get-tuple-element.72), channel_id=1, source_target_pairs={{0,2},{2,0},{4,6},{6,4},{1,3},{3,1},{5,7},{7,5},{8,10},{10,8},{12,... | collective-permute-start | bytes 98312 | tf_op jit(solution)/shard_map/ppermute | solution.py:325
  69.5 5.2 %collective-permute-start.24 = (bf16[32,512]{1,0:T(8,128)(2,1)S(1)}, bf16[32,512]{1,0:T(8,128)(2,1)S(1)}, u32[]{:S(2)}, u32[]{:S(2)}) collective-permute-start(bf16[32,512]{1,0:T(8,128)(2,1)S(1)} %get-tuple-element.72), channel_id=1, source_target_pairs={{0,4},{2,6},{4,0},{6,2},{1,5},{3,7},{5,1},{7,3},{8,12},{10,14},{12... | collective-permute-start | bytes 98312 | tf_op jit(solution)/shard_map/ppermute | solution.py:325
  70.8 5.7 %collective-permute-start.23 = (bf16[32,512]{1,0:T(8,128)(2,1)S(1)}, bf16[32,512]{1,0:T(8,128)(2,1)S(1)}, u32[]{:S(2)}, u32[]{:S(2)}) collective-permute-start(bf16[32,512]{1,0:T(8,128)(2,1)S(1)} %get-tuple-element.72), channel_id=1, source_target_pairs={{0,6},{2,4},{4,2},{6,0},{1,7},{3,5},{5,3},{7,1},{8,14},{10,12},{12... | collective-permute-start | bytes 98312 | tf_op jit(solution)/shard_map/ppermute | solution.py:325
  (16 other events, 230.0 us)

commit v5 on v4

--- a/solution.py
+++ b/solution.py
@@ -42,15 +42,20 @@
         rhs_copies[i].start()
     mid_copy.start()
     out_copies = []
-    for i in range(leaves):
-        inv_copies[i].wait()
-        rhs_copies[i].wait()
-        solved[i] = times_transposed(rhs[i].astype(BF16), inv[i])
-        rounded[i] = solved[i].astype(BF16)
-        out_copies.append(pltpu.make_async_copy(solved.at[i], solved_ref.at[i], out_sems.at[i]))
-        out_copies.append(pltpu.make_async_copy(rounded.at[i], round_ref.at[i], round_sems.at[i]))
-        for copy in out_copies[-2:]:
-            copy.start()
+    for start in range(0, leaves, 2):
+        group = range(start, min(start + 2, leaves))
+        for i in group:
+            inv_copies[i].wait()
+            rhs_copies[i].wait()
+        products = [times_transposed(rhs[i].astype(BF16), inv[i]) for i in group]
+        for i, product in zip(group, products):
+            solved[i] = product
+            rounded[i] = product.astype(BF16)
+        for i in group:
+            out_copies.append(pltpu.make_async_copy(solved.at[i], solved_ref.at[i], out_sems.at[i]))
+            out_copies.append(pltpu.make_async_copy(rounded.at[i], round_ref.at[i], round_sems.at[i]))
+            for copy in out_copies[-2:]:
+                copy.start()
     mid_copy.wait()
     if slots == 2:
         terms_refs[0][...] = masked_terms(parent_ref, 1 - lax.axis_index("col"), rounded, mid).astype(BF16)
@@ -326,7 +331,7 @@
     return arrived
 
 
-def whole_call(kernel, name, operands, results, flops=0, scratch=(), scalars=0, after=()):
+def whole_call(kernel, name, operands, results, flops=0, scratch=(), scalars=0, after=(), hbm_results=0):
     moved = sum(math.prod(a.shape) * a.dtype.itemsize for a in operands)
     moved += sum(math.prod(shape) * jnp.dtype(kind).itemsize for shape, kind in results)
     smem, vmem = pl.BlockSpec(memory_space=pltpu.SMEM), pl.BlockSpec(memory_space=pltpu.VMEM)
@@ -339,7 +344,7 @@
         in_specs=[pl.BlockSpec(memory_space=pl.ANY)] * len(after)
         + [smem] * scalars
         + [vmem] * (len(operands) - scalars),
-        out_specs=[vmem] * len(results),
+        out_specs=[vmem] * (len(results) - hbm_results) + [pl.BlockSpec(memory_space=pltpu.HBM)] * hbm_results,
         out_shape=[jax.ShapeDtypeStruct(shape, kind) for shape, kind in results],
         scratch_shapes=list(scratch),
         compiler_params=pltpu.CompilerParams(vmem_limit_bytes=STEP_VMEM_BYTES),
@@ -376,25 +381,28 @@
 
 def mid_solve_kernel(
     pattern_ref, p0, p3, p2, p1, inv_ref, lower_ref, up_ref,
-    solved_ref, top_ref, top_given_ref, late_ref, late_given_ref, rounded, total,
+    top_ref, top_given_ref, late_ref, late_given_ref, solved_ref, solved, rounded, total, sem,
 ):
     row, col, core = lax.axis_index("row"), lax.axis_index("col"), lax.axis_index("gz") & 1
     length, part = p0.shape[0], top_ref.shape[1]
     for d, ref in zip((0, 3, 2, 1), (p0, p3, p2, p1)):
         at = piece(row ^ d, length)
-        solved = times_transposed(ref[...], inv_ref[0])
-        solved_ref[at] = solved
-        rounded[at] = solved.astype(BF16)
-    total[...] = up_ref[0] + times_transposed(rounded[...], lower_ref[0, 0])
+        product = times_transposed(ref[...], inv_ref[0])
+        solved[at] = product
+        rounded[at] = product.astype(BF16)
+    copy = pltpu.make_async_copy(solved, solved_ref, sem)
+    copy.start()
+    total[0] = up_ref[0] + times_transposed(rounded[...], lower_ref[0, 0])
     for i in range(4):
-        top_ref[i] = total[piece(i * 2 + col, part)]
-        top_given_ref[i] = total[piece(i * 2 + 1 - col, part)].astype(BF16)
+        top_ref[i] = total[0, piece(i * 2 + col, part)]
+        top_given_ref[i] = total[0, piece(i * 2 + 1 - col, part)].astype(BF16)
     for k in (1, 2):
         weight = pattern_ref[0, k - 1].astype(F32)
-        total[...] = up_ref[k] + weight * times_transposed(rounded[...], lower_ref[0, k])
+        total[k] = up_ref[k] + weight * times_transposed(rounded[...], lower_ref[0, k])
         for half in (0, 1):
-            late_ref[k - 1, half] = total[piece(half * 2 + core, length)]
-            late_given_ref[k - 1, half] = total[piece(half * 2 + 1 - core, length)].astype(BF16)
+            late_ref[k - 1, half] = total[k, piece(half * 2 + core, length)]
+            late_given_ref[k - 1, half] = total[k, piece(half * 2 + 1 - core, length)].astype(BF16)
+    copy.wait()
 
 
 def top_share_kernel(inv_ref, share_ref):
@@ -560,14 +568,20 @@
     )
     arrived = partners(ready, ROW_MOVES)
     (top_whole,) = whole_call(whole_top_kernel, "whole_top", [top_half, top_other], [((size, size), BF16)])
-    mid_solved, kept, given, late_kept, late_given = whole_call(
+    kept, given, late_kept, late_given, mid_solved = whole_call(
         mid_solve_kernel, "mid_solve", [mid_pattern, ready, *arrived, parent_diagonal_inverse, mid_lower, layer_up],
-        [((count, width), F32), ((4, part, size), F32), ((4, part, size), BF16)]
-        + [((2, 2, quarter, size), F32), ((2, 2, quarter, size), BF16)],
+        [((4, part, size), F32), ((4, part, size), BF16), ((2, 2, quarter, size), F32), ((2, 2, quarter, size), BF16)]
+        + [((count, width), F32)],
         flops=8 * count * size * width,
-        scratch=[pltpu.VMEM((count, width), BF16), pltpu.VMEM((count, size), F32)],
+        scratch=[
+            pltpu.VMEM((count, width), F32),
+            pltpu.VMEM((count, width), BF16),
+            pltpu.VMEM((3, count, size), F32),
+            pltpu.SemaphoreType.DMA,
+        ],
         scalars=1,
         after=[top_whole],
+        hbm_results=1,
     )
 
     (other,) = partners(given, [{"col": 1}])

time: 81.5 us -> 81 us (level)
  no operation moved by 1% of the time
where the time goes in v5:
time: 81 us; the launch traced here: 80.8 us
  starting transfers between devices  38.2 us (47%)
  waiting for transfers between devices  25 us (31%)
  Pallas kernels  15.5 us (19%)
  local copies, waits for them, and re-layouts  1.1 us (1%)
  between operations  0.89 us (1%)
    ppermute x27, starting transfers between devices, partners(): arrived.append(lax.ppermute(item, axes, route))  38.2 us
    ppermute x27, waiting for transfers between devices, partners(): arrived.append(lax.ppermute(item, axes, route))  25 us
    pallas_call x1, Pallas kernels, leaf_solve(): pl.pallas_call(functools.partial(leaf_kernel, slots), in_specs=[pl.BlockS...  5.32 us
    pallas_call x15, Pallas kernels, whole_call(): pl.pallas_call(body, in_specs=[pl.BlockSpec(memory_space=pl.ANY)] * len(a...  4.63 us
    pallas_call x1, Pallas kernels, leaf_coupling(): pl.pallas_call(coupling_kernel, in_specs=[pl.BlockSpec(memory_space=pltpu...  3.27 us
    pallas_call x1, Pallas kernels, own_terms(): pl.pallas_call(own_terms_kernel, in_specs=[pl.BlockSpec(memory_space=pltp...  2.31 us
  transfers between devices with their start and end apart: 27, of which 14 were waited for; matrix products, arithmetic and copies ran while one was open for 0% of the time, Pallas kernels for 8%

profile of v5, /device:TPU:0, one launch (start us, length us, event | category | flops | bytes accessed | tf_op | source)
XLA Modules:
  0.0 80.8 jit_solution(10531249041718334960)
XLA Ops:
  0.7 5.3 %leaf_solve.1 = (f32[8,256,128]{2,1,0:T(8,128)}, bf16[8,256,128]{2,1,0:T(8,128)(2,1)}, bf16[256,512]{1,0:T(8,128)(2,1)}) custom-call(s32[8]{0:T(128)} %parent_ref.3, f32[8,256,512]{2,1,0:T(8,128)} %rhs_ref.2, bf16[8,128,512]{2,1,0:T(8,128)(2,1)} %inv_ref.1, bf16[8,512,128]{2,1,0:T(8,128)(2,1)} %mid_ref.3), custom_call_target="tpu_custom_call" | custom-call | flops 536870912 | bytes 7864320 | tf_op jit(solution)/shard_map/leaf_solve/pallas_call | solution.py:77
  6.0 3.0 %collective-permute-start.3 = (bf16[256,512]{1,0:T(8,128)(2,1)}, bf16[256,512]{1,0:T(8,128)(2,1)S(1)}, u32[]{:S(2)}, u32[]{:S(2)}) collective-permute-start(bf16[256,512]{1,0:T(8,128)(2,1)} %get-tuple-element.44), channel_id=1, source_target_pairs={{0,1},{1,0},{2,3},{3,2},{4,5},{5,4},{6,7},{7,6},{8,9},{9,8},{10,11... | collective-permute-start | bytes 786440 | tf_op jit(solution)/shard_map/ppermute | solution.py:330
  9.0 1.6 %collective-permute-start.2 = (bf16[128,256]{1,0:T(8,128)(2,1)S(1)}, bf16[128,256]{1,0:T(8,128)(2,1)S(1)}, u32[]{:S(2)}, u32[]{:S(2)}) collective-permute-start(bf16[128,256]{1,0:T(8,128)(2,1)S(1)} %top_share.1.refs_1_), channel_id=1, source_target_pairs={{0,2},{2,0},{4,6},{6,4},{1,3},{3,1},{5,7},{7,5},{8,10},{10,8},{12,... | collective-permute-start | bytes 196616 | tf_op jit(solution)/shard_map/ppermute | solution.py:330
  10.7 2.6 %collective-permute-start.1 = (bf16[128,256]{1,0:T(8,128)(2,1)S(1)}, bf16[128,256]{1,0:T(8,128)(2,1)S(1)}, u32[]{:S(2)}, u32[]{:S(2)}) collective-permute-start(bf16[128,256]{1,0:T(8,128)(2,1)S(1)} %top_share.1.refs_1_), channel_id=1, source_target_pairs={{0,4},{2,6},{4,0},{6,2},{1,5},{3,7},{5,1},{7,3},{8,12},{10,14},{12... | collective-permute-start | bytes 196616 | tf_op jit(solution)/shard_map/ppermute | solution.py:330
  14.5 2.3 %own_terms.1 = (bf16[256,512]{1,0:T(8,128)(2,1)S(1)}, f32[64,512]{1,0:T(8,128)S(1)}) custom-call(s32[8]{0:T(128)S(1)} %copy-done.11, bf16[8,256,128]{2,1,0:T(8,128)(2,1)S(1)} %copy-done.1, bf16[8,512,128]{2,1,0:T(8,128)(2,1)} %mid_ref.3, f32[1,256,512]{2,1,0:T(8,128)S(1)} %copy-done.3), custom_call_target="tpu_custom_call" | custom-call | flops 268435456 | bytes 1572864 | tf_op jit(solution)/shard_map/own_terms/pallas_call | solution.py:126
  17.7 1.7 %collective-permute-done.refs_0_.refs_2_ = bf16[128,256]{1,0:T(8,128)(2,1)S(1)} collective-permute-done((bf16[128,256]{1,0:T(8,128)(2,1)S(1)}, bf16[128,256]{1,0:T(8,128)(2,1)S(1)}, u32[]{:S(2)}, u32[]{:S(2)}) %collective-permute-start) | collective-permute-done | bytes 65568 | tf_op jit(solution)/shard_map/ppermute | solution.py:330
  21.5 2.9 %collective-permute-start.7 = (bf16[64,512]{1,0:T(8,128)(2,1)S(1)}, bf16[64,512]{1,0:T(8,128)(2,1)S(1)}, u32[]{:S(2)}, u32[]{:S(2)}) collective-permute-start(bf16[64,512]{1,0:T(8,128)(2,1)S(1)} %get-tuple-element.48), channel_id=1, source_target_pairs={{0,2},{2,0},{4,6},{6,4},{1,3},{3,1},{5,7},{7,5},{8,10},{10,8},{12,... | collective-permute-start | bytes 196616 | tf_op jit(solution)/shard_map/ppermute | solution.py:330
  24.4 3.3 %leaf_coupling.1.refs_0_.refs_8_ = f32[3,256,512]{2,1,0:T(8,128)S(1)} custom-call(s32[3,8]{1,0:T(4,128)S(1)} %bitcast.2, bf16[8,256,128]{2,1,0:T(8,128)(2,1)S(1)} %copy-done.1, bf16[8,3,512,128]{3,2,1,0:T(8,128)(2,1)} %lower_ref.1), custom_call_target="tpu_custom_call" | custom-call | flops 805306368 | bytes 5242880 | tf_op jit(solution)/shard_map/leaf_coupling/pallas_call | solution.py:168
  29.9 2.3 %collective-permute-start.8 = (bf16[64,512]{1,0:T(8,128)(2,1)S(1)}, bf16[64,512]{1,0:T(8,128)(2,1)S(1)}, u32[]{:S(2)}, u32[]{:S(2)}) collective-permute-start(bf16[64,512]{1,0:T(8,128)(2,1)S(1)} %mid_total.1.refs_2_), channel_id=1, source_target_pairs={{0,6},{2,4},{4,2},{6,0},{1,7},{3,5},{5,3},{7,1},{8,14},{10,12},{12... | collective-permute-start | bytes 196616 | tf_op jit(solution)/shard_map/ppermute | solution.py:330
  32.5 2.6 %collective-permute-done.9.refs_4_ = bf16[64,512]{1,0:T(8,128)(2,1)S(1)} collective-permute-done((bf16[64,512]{1,0:T(8,128)(2,1)S(1)}, bf16[64,512]{1,0:T(8,128)(2,1)S(1)}, u32[]{:S(2)}, u32[]{:S(2)}) %collective-permute-start.9) | collective-permute-done | bytes 65568 | tf_op jit(solution)/shard_map/ppermute | solution.py:330
  36.1 1.8 %mid_solve.1 = (f32[4,32,512]{2,1,0:T(8,128)S(1)}, bf16[4,32,512]{2,1,0:T(8,128)(2,1)S(1)}, f32[2,2,64,512]{3,2,1,0:T(8,128)S(1)}, bf16[2,2,64,512]{3,2,1,0:T(8,128)(2,1)S(1)}, f32[256,128]{1,0:T(8,128)}) custom-call(bf16[512,512]{1,0:T(8,128)(2,1)S(1)} %whole_top.1.refs_0_.refs_4_, s32[1,2]{1,0:T(1,128)S(1)} %copy-done.12, ...), custom_call_target="tpu_custom_call" | custom-call | flops 134217728 | bytes 3670024 | tf_op jit(solution)/shard_map/mid_solve/pallas_call | solution.py:342
  38.0 1.6 %collective-permute-start.12 = (bf16[4,32,512]{2,1,0:T(8,128)(2,1)S(1)}, bf16[4,32,512]{2,1,0:T(8,128)(2,1)S(1)}, u32[]{:S(2)}, u32[]{:S(2)}) collective-permute-start(bf16[4,32,512]{2,1,0:T(8,128)(2,1)S(1)} %get-tuple-element.54), channel_id=1, source_target_pairs={{0,1},{1,0},{2,3},{3,2},{4,5},{5,4},{6,7},{7,6},{8,9},{9,8},{10,11... | collective-permute-start | bytes 393224 | tf_op jit(solution)/shard_map/ppermute | solution.py:330
  39.7 1.5 %collective-permute-start.16 = (bf16[2,2,32,512]{3,2,1,0:T(8,128)(2,1)S(1)}, bf16[2,2,32,512]{3,2,1,0:T(8,128)(2,1)S(1)}, u32[]{:S(2)}, u32[]{:S(2)}) collective-permute-start(bf16[2,2,32,512]{3,2,1,0:T(8,128)(2,1)S(1)} %get-tuple-element.52.refs_0_), channel_id=1, source_target_pairs={{0,1},{1,0},{2,3},{3,2},{4,5},{5,4},{6,7},{7,6},{8,9},{9,8},{10,11... | collective-permute-start | bytes 393224 | tf_op jit(solution)/shard_map/ppermute | solution.py:330
  41.2 3.2 %collective-permute-done.12.refs_3_ = bf16[4,32,512]{2,1,0:T(8,128)(2,1)S(1)} collective-permute-done((bf16[4,32,512]{2,1,0:T(8,128)(2,1)S(1)}, bf16[4,32,512]{2,1,0:T(8,128)(2,1)S(1)}, u32[]{:S(2)}, u32[]{:S(2)}) %collective-permute-start.12) | collective-permute-done | bytes 131104 | tf_op jit(solution)/shard_map/ppermute | solution.py:330
  44.8 2.3 %collective-permute-start.13 = (bf16[128,128]{1,0:T(8,128)(2,1)S(1)}, bf16[128,128]{1,0:T(8,128)(2,1)S(1)}, u32[]{:S(2)}, u32[]{:S(2)}) collective-permute-start(bf16[128,128]{1,0:T(8,128)(2,1)S(1)} %get-tuple-element.56), channel_id=1, source_target_pairs={{0,6},{2,4},{4,2},{6,0},{1,7},{3,5},{5,3},{7,1},{8,14},{10,12},{12... | collective-permute-start | bytes 98312 | tf_op jit(solution)/shard_map/ppermute | solution.py:330
  47.3 1.9 %collective-permute-start.15 = (bf16[128,128]{1,0:T(8,128)(2,1)S(1)}, bf16[128,128]{1,0:T(8,128)(2,1)S(1)}, u32[]{:S(2)}, u32[]{:S(2)}) collective-permute-start(bf16[128,128]{1,0:T(8,128)(2,1)S(1)} %get-tuple-element.58), channel_id=1, source_target_pairs={{0,2},{2,0},{4,6},{6,4},{1,3},{3,1},{5,7},{7,5},{8,10},{10,8},{12,... | collective-permute-start | bytes 98312 | tf_op jit(solution)/shard_map/ppermute | solution.py:330
  56.1 2.0 %collective-permute-start.18 = (bf16[64,512]{1,0:T(8,128)(2,1)S(1)}, bf16[64,512]{1,0:T(8,128)(2,1)S(1)}, u32[]{:S(2)}, u32[]{:S(2)}) collective-permute-start(bf16[64,512]{1,0:T(8,128)(2,1)S(1)} %get-tuple-element.63), channel_id=1, source_target_pairs={{0,6},{2,4},{4,2},{6,0},{1,7},{3,5},{5,3},{7,1},{8,14},{10,12},{12... | collective-permute-start | bytes 196616 | tf_op jit(solution)/shard_map/ppermute | solution.py:330
  58.1 5.1 %collective-permute-done.19.refs_3_ = bf16[64,512]{1,0:T(8,128)(2,1)S(1)} collective-permute-done((bf16[64,512]{1,0:T(8,128)(2,1)S(1)}, bf16[64,512]{1,0:T(8,128)(2,1)S(1)}, u32[]{:S(2)}, u32[]{:S(2)}) %collective-permute-start.19) | collective-permute-done | bytes 65568 | tf_op jit(solution)/shard_map/ppermute | solution.py:330
  63.6 1.6 %collective-permute-start.21 = (bf16[32,640]{1,0:T(8,128)(2,1)S(1)}, bf16[32,640]{1,0:T(8,128)(2,1)S(1)}, u32[]{:S(2)}, u32[]{:S(2)}) collective-permute-start(bf16[32,640]{1,0:T(8,128)(2,1)S(1)} %get-tuple-element.66), channel_id=1, source_target_pairs={{0,16},{8,24},{16,0},{24,8},{1,17},{9,25},{17,1},{25,9},{2,18},{10... | collective-permute-start | bytes 122888 | tf_op jit(solution)/shard_map/ppermute | solution.py:330
  65.1 1.5 %collective-permute-start.22 = (bf16[4,32,128]{2,1,0:T(8,128)(2,1)S(1)}, bf16[4,32,128]{2,1,0:T(8,128)(2,1)S(1)}, u32[]{:S(2)}, u32[]{:S(2)}) collective-permute-start(bf16[4,32,128]{2,1,0:T(8,128)(2,1)S(1)} %get-tuple-element.69), channel_id=1, source_target_pairs={{0,1},{1,0},{2,3},{3,2},{4,5},{5,4},{6,7},{7,6},{8,9},{9,8},{10,11... | collective-permute-start | bytes 98312 | tf_op jit(solution)/shard_map/ppermute | solution.py:330
  70.3 1.8 %collective-permute-start.23 = (bf16[32,512]{1,0:T(8,128)(2,1)S(1)}, bf16[32,512]{1,0:T(8,128)(2,1)S(1)}, u32[]{:S(2)}, u32[]{:S(2)}) collective-permute-start(bf16[32,512]{1,0:T(8,128)(2,1)S(1)} %get-tuple-element.72), channel_id=1, source_target_pairs={{0,6},{2,4},{4,2},{6,0},{1,7},{3,5},{5,3},{7,1},{8,14},{10,12},{12... | collective-permute-start | bytes 98312 | tf_op jit(solution)/shard_map/ppermute | solution.py:330
  74.2 1.8 %collective-permute-done.23.refs_4_ = bf16[32,512]{1,0:T(8,128)(2,1)S(1)} collective-permute-done((bf16[32,512]{1,0:T(8,128)(2,1)S(1)}, bf16[32,512]{1,0:T(8,128)(2,1)S(1)}, u32[]{:S(2)}, u32[]{:S(2)}) %collective-permute-start.23) | collective-permute-done | bytes 32800 | tf_op jit(solution)/shard_map/ppermute | solution.py:330
  76.2 1.6 %collective-permute-start.26 = (bf16[3,32,128]{2,1,0:T(8,128)(2,1)S(1)}, bf16[3,32,128]{2,1,0:T(8,128)(2,1)S(1)}, u32[]{:S(2)}, u32[]{:S(2)}) collective-permute-start(bf16[3,32,128]{2,1,0:T(8,128)(2,1)S(1)} %get-tuple-element.75), channel_id=1, source_target_pairs={{0,1},{1,0},{2,3},{3,2},{4,5},{5,4},{6,7},{7,6},{8,9},{9,8},{10,11... | collective-permute-start | bytes 73736 | tf_op jit(solution)/shard_map/ppermute | solution.py:330
  77.8 2.3 %collective-permute-done.26.refs_1_ = bf16[3,32,128]{2,1,0:T(8,128)(2,1)S(1)} collective-permute-done((bf16[3,32,128]{2,1,0:T(8,128)(2,1)S(1)}, bf16[3,32,128]{2,1,0:T(8,128)(2,1)S(1)}, u32[]{:S(2)}, u32[]{:S(2)}) %collective-permute-start.26) | collective-permute-done | bytes 24608 | tf_op jit(solution)/shard_map/ppermute | solution.py:330
  (74 shorter events, 22.2 us)
Async XLA Ops:
  6.0 13.3 %collective-permute-start.3 = (bf16[256,512]{1,0:T(8,128)(2,1)}, bf16[256,512]{1,0:T(8,128)(2,1)S(1)}, u32[]{:S(2)}, u32[]{:S(2)}) collective-permute-start(bf16[256,512]{1,0:T(8,128)(2,1)} %get-tuple-element.44), channel_id=1, source_target_pairs={{0,1},{1,0},{2,3},{3,2},{4,5},{5,4},{6,7},{7,6},{8,9},{9,8},{10,11... | collective-permute-start | bytes 786440 | tf_op jit(solution)/shard_map/ppermute | solution.py:330
  9.0 7.8 %collective-permute-start.2 = (bf16[128,256]{1,0:T(8,128)(2,1)S(1)}, bf16[128,256]{1,0:T(8,128)(2,1)S(1)}, u32[]{:S(2)}, u32[]{:S(2)}) collective-permute-start(bf16[128,256]{1,0:T(8,128)(2,1)S(1)} %top_share.1.refs_1_), channel_id=1, source_target_pairs={{0,2},{2,0},{4,6},{6,4},{1,3},{3,1},{5,7},{7,5},{8,10},{10,8},{12,... | collective-permute-start | bytes 196616 | tf_op jit(solution)/shard_map/ppermute | solution.py:330
  10.7 7.0 %collective-permute-start.1 = (bf16[128,256]{1,0:T(8,128)(2,1)S(1)}, bf16[128,256]{1,0:T(8,128)(2,1)S(1)}, u32[]{:S(2)}, u32[]{:S(2)}) collective-permute-start(bf16[128,256]{1,0:T(8,128)(2,1)S(1)} %top_share.1.refs_1_), channel_id=1, source_target_pairs={{0,4},{2,6},{4,0},{6,2},{1,5},{3,7},{5,1},{7,3},{8,12},{10,14},{12... | collective-permute-start | bytes 196616 | tf_op jit(solution)/shard_map/ppermute | solution.py:330
  13.3 6.1 %collective-permute-start = (bf16[128,256]{1,0:T(8,128)(2,1)S(1)}, bf16[128,256]{1,0:T(8,128)(2,1)S(1)}, u32[]{:S(2)}, u32[]{:S(2)}) collective-permute-start(bf16[128,256]{1,0:T(8,128)(2,1)S(1)} %top_share.1.refs_1_), channel_id=1, source_target_pairs={{0,6},{2,4},{4,2},{6,0},{1,7},{3,5},{5,3},{7,1},{8,14},{10,12},{12... | collective-permute-start | bytes 196616 | tf_op jit(solution)/shard_map/ppermute | solution.py:330
  19.5 12.8 %collective-permute-start.4 = (bf16[512,256]{1,0:T(8,128)(2,1)S(1)}, bf16[512,256]{1,0:T(8,128)(2,1)S(1)}, u32[]{:S(2)}, u32[]{:S(2)}) collective-permute-start(bf16[512,256]{1,0:T(8,128)(2,1)S(1)} %half_top.1.refs_0_), channel_id=1, source_target_pairs={{0,1},{1,0},{2,3},{3,2},{4,5},{5,4},{6,7},{7,6},{8,9},{9,8},{10,11... | collective-permute-start | bytes 786440 | tf_op jit(solution)/shard_map/ppermute | solution.py:330
  20.0 7.7 %collective-permute-start.5 = (bf16[64,512]{1,0:T(8,128)(2,1)S(1)}, bf16[64,512]{1,0:T(8,128)(2,1)S(1)}, u32[]{:S(2)}, u32[]{:S(2)}) collective-permute-start(bf16[64,512]{1,0:T(8,128)(2,1)S(1)} %get-tuple-element.46), channel_id=1, source_target_pairs={{0,6},{2,4},{4,2},{6,0},{1,7},{3,5},{5,3},{7,1},{8,14},{10,12},{12... | collective-permute-start | bytes 196616 | tf_op jit(solution)/shard_map/ppermute | solution.py:330
  21.5 6.2 %collective-permute-start.6 = (bf16[64,512]{1,0:T(8,128)(2,1)S(1)}, bf16[64,512]{1,0:T(8,128)(2,1)S(1)}, u32[]{:S(2)}, u32[]{:S(2)}) collective-permute-start(bf16[64,512]{1,0:T(8,128)(2,1)S(1)} %get-tuple-element.47), channel_id=1, source_target_pairs={{0,4},{2,6},{4,0},{6,2},{1,5},{3,7},{5,1},{7,3},{8,12},{10,14},{12... | collective-permute-start | bytes 196616 | tf_op jit(solution)/shard_map/ppermute | solution.py:330
  21.5 6.2 %collective-permute-start.7 = (bf16[64,512]{1,0:T(8,128)(2,1)S(1)}, bf16[64,512]{1,0:T(8,128)(2,1)S(1)}, u32[]{:S(2)}, u32[]{:S(2)}) collective-permute-start(bf16[64,512]{1,0:T(8,128)(2,1)S(1)} %get-tuple-element.48), channel_id=1, source_target_pairs={{0,2},{2,0},{4,6},{6,4},{1,3},{3,1},{5,7},{7,5},{8,10},{10,8},{12,... | collective-permute-start | bytes 196616 | tf_op jit(solution)/shard_map/ppermute | solution.py:330
  27.8 4.7 %collective-permute-start.10 = (bf16[64,512]{1,0:T(8,128)(2,1)S(1)}, bf16[64,512]{1,0:T(8,128)(2,1)S(1)}, u32[]{:S(2)}, u32[]{:S(2)}) collective-permute-start(bf16[64,512]{1,0:T(8,128)(2,1)S(1)} %mid_total.1.refs_2_), channel_id=1, source_target_pairs={{0,2},{2,0},{4,6},{6,4},{1,3},{3,1},{5,7},{7,5},{8,10},{10,8},{12,... | collective-permute-start | bytes 196616 | tf_op jit(solution)/shard_map/ppermute | solution.py:330
  29.3 5.9 %collective-permute-start.9 = (bf16[64,512]{1,0:T(8,128)(2,1)S(1)}, bf16[64,512]{1,0:T(8,128)(2,1)S(1)}, u32[]{:S(2)}, u32[]{:S(2)}) collective-permute-start(bf16[64,512]{1,0:T(8,128)(2,1)S(1)} %mid_total.1.refs_2_), channel_id=1, source_target_pairs={{0,4},{2,6},{4,0},{6,2},{1,5},{3,7},{5,1},{7,3},{8,12},{10,14},{12... | collective-permute-start | bytes 196616 | tf_op jit(solution)/shard_map/ppermute | solution.py:330
  29.9 6.2 %collective-permute-start.8 = (bf16[64,512]{1,0:T(8,128)(2,1)S(1)}, bf16[64,512]{1,0:T(8,128)(2,1)S(1)}, u32[]{:S(2)}, u32[]{:S(2)}) collective-permute-start(bf16[64,512]{1,0:T(8,128)(2,1)S(1)} %mid_total.1.refs_2_), channel_id=1, source_target_pairs={{0,6},{2,4},{4,2},{6,0},{1,7},{3,5},{5,3},{7,1},{8,14},{10,12},{12... | collective-permute-start | bytes 196616 | tf_op jit(solution)/shard_map/ppermute | solution.py:330
  38.0 6.4 %collective-permute-start.12 = (bf16[4,32,512]{2,1,0:T(8,128)(2,1)S(1)}, bf16[4,32,512]{2,1,0:T(8,128)(2,1)S(1)}, u32[]{:S(2)}, u32[]{:S(2)}) collective-permute-start(bf16[4,32,512]{2,1,0:T(8,128)(2,1)S(1)} %get-tuple-element.54), channel_id=1, source_target_pairs={{0,1},{1,0},{2,3},{3,2},{4,5},{5,4},{6,7},{7,6},{8,9},{9,8},{10,11... | collective-permute-start | bytes 393224 | tf_op jit(solution)/shard_map/ppermute | solution.py:330
  39.7 12.2 %collective-permute-start.16 = (bf16[2,2,32,512]{3,2,1,0:T(8,128)(2,1)S(1)}, bf16[2,2,32,512]{3,2,1,0:T(8,128)(2,1)S(1)}, u32[]{:S(2)}, u32[]{:S(2)}) collective-permute-start(bf16[2,2,32,512]{3,2,1,0:T(8,128)(2,1)S(1)} %get-tuple-element.52.refs_0_), channel_id=1, source_target_pairs={{0,1},{1,0},{2,3},{3,2},{4,5},{5,4},{6,7},{7,6},{8,9},{9,8},{10,11... | collective-permute-start | bytes 393224 | tf_op jit(solution)/shard_map/ppermute | solution.py:330
  44.8 5.8 %collective-permute-start.13 = (bf16[128,128]{1,0:T(8,128)(2,1)S(1)}, bf16[128,128]{1,0:T(8,128)(2,1)S(1)}, u32[]{:S(2)}, u32[]{:S(2)}) collective-permute-start(bf16[128,128]{1,0:T(8,128)(2,1)S(1)} %get-tuple-element.56), channel_id=1, source_target_pairs={{0,6},{2,4},{4,2},{6,0},{1,7},{3,5},{5,3},{7,1},{8,14},{10,12},{12... | collective-permute-start | bytes 98312 | tf_op jit(solution)/shard_map/ppermute | solution.py:330
  47.0 4.8 %collective-permute-start.14 = (bf16[128,128]{1,0:T(8,128)(2,1)S(1)}, bf16[128,128]{1,0:T(8,128)(2,1)S(1)}, u32[]{:S(2)}, u32[]{:S(2)}) collective-permute-start(bf16[128,128]{1,0:T(8,128)(2,1)S(1)} %get-tuple-element.57), channel_id=1, source_target_pairs={{0,4},{2,6},{4,0},{6,2},{1,5},{3,7},{5,1},{7,3},{8,12},{10,14},{12... | collective-permute-start | bytes 98312 | tf_op jit(solution)/shard_map/ppermute | solution.py:330
  47.3 4.5 %collective-permute-start.15 = (bf16[128,128]{1,0:T(8,128)(2,1)S(1)}, bf16[128,128]{1,0:T(8,128)(2,1)S(1)}, u32[]{:S(2)}, u32[]{:S(2)}) collective-permute-start(bf16[128,128]{1,0:T(8,128)(2,1)S(1)} %get-tuple-element.58), channel_id=1, source_target_pairs={{0,2},{2,0},{4,6},{6,4},{1,3},{3,1},{5,7},{7,5},{8,10},{10,8},{12,... | collective-permute-start | bytes 98312 | tf_op jit(solution)/shard_map/ppermute | solution.py:330
  53.6 4.5 %collective-permute-start.20 = (bf16[64,512]{1,0:T(8,128)(2,1)S(1)}, bf16[64,512]{1,0:T(8,128)(2,1)S(1)}, u32[]{:S(2)}, u32[]{:S(2)}) collective-permute-start(bf16[64,512]{1,0:T(8,128)(2,1)S(1)} %get-tuple-element.63), channel_id=1, source_target_pairs={{0,2},{2,0},{4,6},{6,4},{1,3},{3,1},{5,7},{7,5},{8,10},{10,8},{12,... | collective-permute-start | bytes 196616 | tf_op jit(solution)/shard_map/ppermute | solution.py:330
  54.9 8.2 %collective-permute-start.19 = (bf16[64,512]{1,0:T(8,128)(2,1)S(1)}, bf16[64,512]{1,0:T(8,128)(2,1)S(1)}, u32[]{:S(2)}, u32[]{:S(2)}) collective-permute-start(bf16[64,512]{1,0:T(8,128)(2,1)S(1)} %get-tuple-element.63), channel_id=1, source_target_pairs={{0,4},{2,6},{4,0},{6,2},{1,5},{3,7},{5,1},{7,3},{8,12},{10,14},{12... | collective-permute-start | bytes 196616 | tf_op jit(solution)/shard_map/ppermute | solution.py:330
  56.1 7.1 %collective-permute-start.18 = (bf16[64,512]{1,0:T(8,128)(2,1)S(1)}, bf16[64,512]{1,0:T(8,128)(2,1)S(1)}, u32[]{:S(2)}, u32[]{:S(2)}) collective-permute-start(bf16[64,512]{1,0:T(8,128)(2,1)S(1)} %get-tuple-element.63), channel_id=1, source_target_pairs={{0,6},{2,4},{4,2},{6,0},{1,7},{3,5},{5,3},{7,1},{8,14},{10,12},{12... | collective-permute-start | bytes 196616 | tf_op jit(solution)/shard_map/ppermute | solution.py:330
  63.6 4.1 %collective-permute-start.21 = (bf16[32,640]{1,0:T(8,128)(2,1)S(1)}, bf16[32,640]{1,0:T(8,128)(2,1)S(1)}, u32[]{:S(2)}, u32[]{:S(2)}) collective-permute-start(bf16[32,640]{1,0:T(8,128)(2,1)S(1)} %get-tuple-element.66), channel_id=1, source_target_pairs={{0,16},{8,24},{16,0},{24,8},{1,17},{9,25},{17,1},{25,9},{2,18},{10... | collective-permute-start | bytes 122888 | tf_op jit(solution)/shard_map/ppermute | solution.py:330
  65.1 7.0 %collective-permute-start.22 = (bf16[4,32,128]{2,1,0:T(8,128)(2,1)S(1)}, bf16[4,32,128]{2,1,0:T(8,128)(2,1)S(1)}, u32[]{:S(2)}, u32[]{:S(2)}) collective-permute-start(bf16[4,32,128]{2,1,0:T(8,128)(2,1)S(1)} %get-tuple-element.69), channel_id=1, source_target_pairs={{0,1},{1,0},{2,3},{3,2},{4,5},{5,4},{6,7},{7,6},{8,9},{9,8},{10,11... | collective-permute-start | bytes 98312 | tf_op jit(solution)/shard_map/ppermute | solution.py:330
  67.7 5.1 %collective-permute-start.25 = (bf16[32,512]{1,0:T(8,128)(2,1)S(1)}, bf16[32,512]{1,0:T(8,128)(2,1)S(1)}, u32[]{:S(2)}, u32[]{:S(2)}) collective-permute-start(bf16[32,512]{1,0:T(8,128)(2,1)S(1)} %get-tuple-element.72), channel_id=1, source_target_pairs={{0,2},{2,0},{4,6},{6,4},{1,3},{3,1},{5,7},{7,5},{8,10},{10,8},{12,... | collective-permute-start | bytes 98312 | tf_op jit(solution)/shard_map/ppermute | solution.py:330
  69.0 5.2 %collective-permute-start.24 = (bf16[32,512]{1,0:T(8,128)(2,1)S(1)}, bf16[32,512]{1,0:T(8,128)(2,1)S(1)}, u32[]{:S(2)}, u32[]{:S(2)}) collective-permute-start(bf16[32,512]{1,0:T(8,128)(2,1)S(1)} %get-tuple-element.72), channel_id=1, source_target_pairs={{0,4},{2,6},{4,0},{6,2},{1,5},{3,7},{5,1},{7,3},{8,12},{10,14},{12... | collective-permute-start | bytes 98312 | tf_op jit(solution)/shard_map/ppermute | solution.py:330
  70.3 5.7 %collective-permute-start.23 = (bf16[32,512]{1,0:T(8,128)(2,1)S(1)}, bf16[32,512]{1,0:T(8,128)(2,1)S(1)}, u32[]{:S(2)}, u32[]{:S(2)}) collective-permute-start(bf16[32,512]{1,0:T(8,128)(2,1)S(1)} %get-tuple-element.72), channel_id=1, source_target_pairs={{0,6},{2,4},{4,2},{6,0},{1,7},{3,5},{5,3},{7,1},{8,14},{10,12},{12... | collective-permute-start | bytes 98312 | tf_op jit(solution)/shard_map/ppermute | solution.py:330
  (16 other events, 228.8 us)

commit v6 on v5

--- a/solution.py
+++ b/solution.py
@@ -422,6 +422,30 @@
     whole_ref[:, piece(1 - col, length)] = other_ref[...]
 
 
+def apex_share_kernel(inv_ref, lower_ref, share_ref):
+    gz, block = lax.axis_index("gz"), share_ref.shape[1]
+    quarter = piece((gz & 1) * 2 + lax.axis_index("col"), block)
+    share_ref[0] = inv_ref[gz >> 1, :, quarter]
+    share_ref[1] = lower_ref[gz >> 1, quarter, :]
+
+
+def rows_of_shares_kernel(p0, p3, p2, p1, share_ref):
+    row = lax.axis_index("row")
+    for d, ref in zip((0, 3, 2, 1), (p0, p3, p2, p1)):
+        share_ref[row ^ d] = ref[...]
+
+
+def whole_front_kernel(own_ref, col_ref, core_ref, both_ref, front_ref, lower_ref):
+    core, col = lax.axis_index("gz") & 1, lax.axis_index("col")
+    block = own_ref.shape[2]
+    for d, ref in enumerate((own_ref, col_ref, core_ref, both_ref)):
+        quarter = piece((core ^ d >> 1) * 2 + (col ^ d & 1), block)
+        for r in range(own_ref.shape[0]):
+            at = pl.ds(r * block, block)
+            front_ref[at, quarter] = ref[r, 0]
+            lower_ref[quarter, at] = ref[r, 1]
+
+
 def on_first_row(rhs):
     return jnp.where(lax.axis_index("row") == 0, rhs, 0.0)
 
@@ -464,38 +488,38 @@
             given_ref[k, half] = total[piece(half * 2 + 1 - core, part)].astype(BF16)
 
 
-def front_pieces_kernel(kept_ref, other_ref, own_ref, send_ref, last_ref):
-    part = kept_ref.shape[2]
-    for half in (0, 1):
-        at = pl.ds(half * part, part)
-        total = kept_ref[0, half] + other_ref[0, half].astype(F32)
-        own_ref[at] = total
-        send_ref[at] = total.astype(BF16)
-        last_ref[half] = kept_ref[1, half] + other_ref[1, half].astype(F32)
-
-
 def apex_rows(rhs_ref, which, half, part):
     core, col = lax.axis_index("gz") & 1, lax.axis_index("col")
     return rhs_ref[which, piece(half * 4 + core * 2 + col, part)]
 
 
-def front_solve_kernel(rhs_ref, own_ref, r3, r2, r1, inv_ref, lower_ref, last_ref, front_ref, kept_ref, given_ref, total, fronts):
-    pair = lax.axis_index("gz") >> 1
-    part, size = kept_ref.shape
-    rhs = jnp.concatenate([apex_rows(rhs_ref, pair, half, part) for half in (0, 1)])
-    ready = (rhs - widened(own_ref, r3, r2, r1)).astype(BF16)
-    fronts[...] = times_transposed(ready, inv_ref[pair])
-    total[...] = times_transposed(fronts[...].astype(BF16), lower_ref[pair])
-    front_ref[...] = fronts[piece(pair, part)]
-    kept_ref[...] = total[piece(pair, part)] + last_ref[pair]
-    given_ref[:, :size] = (total[piece(1 - pair, part)] + last_ref[1 - pair]).astype(BF16)
-    given_ref[:, size:] = fronts[piece(1 - pair, part)].astype(BF16)
-
-
-def last_pieces_kernel(kept_ref, other_ref, own_ref, send_ref):
-    total = kept_ref[...] + other_ref[:, : own_ref.shape[1]].astype(F32)
+def front_kernel(rhs_ref, kept_ref, other_ref, inv_ref, lower_ref, front_ref, last_ref, given_ref, ready, fronts, ups):
+    pair, part = lax.axis_index("gz") >> 1, last_ref.shape[0]
+    for half in (0, 1):
+        total = kept_ref[0, half] + other_ref[0, half].astype(F32)
+        ready[pl.ds(half * part, part)] = (on_first_row(apex_rows(rhs_ref, pair, half, part)) - total).astype(BF16)
+    fronts[...] = times_transposed(ready[...], inv_ref[...])
+    front_ref[...] = fronts[piece(pair, part)].astype(BF16)
+    given_ref[0] = fronts[piece(1 - pair, part)].astype(BF16)
+    ups[...] = times_transposed(fronts[...].astype(BF16), lower_ref[...])
+    for half in (0, 1):
+        ups[pl.ds(half * part, part)] += kept_ref[1, half] + other_ref[1, half].astype(F32)
+    last_ref[...] = ups[piece(pair, part)]
+    given_ref[1] = ups[piece(1 - pair, part)].astype(BF16)
+
+
+def last_pieces_kernel(front_ref, last_ref, other_ref, own_ref, fronts_ref, *given_refs):
+    row, pair = lax.axis_index("row"), lax.axis_index("gz") >> 1
+    size, width = last_ref.shape[1], fronts_ref.shape[2]
+    total = last_ref[...] + other_ref[1].astype(F32)
     own_ref[...] = total
-    send_ref[...] = total.astype(BF16)
+    fronts_ref[pair] = front_ref[:, piece(row, width)].astype(F32)
+    fronts_ref[1 - pair] = other_ref[0, :, piece(row, width)].astype(F32)
+    for d, ref in zip((3, 2, 1), given_refs):
+        at = piece(row ^ d, width)
+        ref[:, :size] = total.astype(BF16)
+        ref[:, pl.ds(pl.multiple_of(size + pair * width, width), width)] = front_ref[:, at]
+        ref[:, pl.ds(pl.multiple_of(size + (1 - pair) * width, width), width)] = other_ref[0, :, at]
 
 
 def place_top_kernel(top_ref, other_ref, top_all_ref, done_ref):
@@ -506,13 +530,17 @@
         top_all_ref[0, piece(i * 2 + 1 - col, part)] = other_ref[i].astype(F32)
 
 
-def last_solve_kernel(rhs_ref, inv_ref, own_ref, r3, r2, r1, front_ref, other_ref, solved_ref, send_ref):
-    pair = lax.axis_index("gz") >> 1
+def last_solve_kernel(rhs_ref, inv_ref, own_ref, fronts_ref, r3, r2, r1, solved_ref, send_ref):
     part, size = own_ref.shape
-    ready = (apex_rows(rhs_ref, 2, pair, part) - widened(own_ref, r3, r2, r1)).astype(BF16)
+    width = fronts_ref.shape[2]
+    total = own_ref[...]
+    for ref in (r3, r2, r1):
+        total = total + ref[:, :size].astype(F32)
+    ready = (apex_rows(rhs_ref, 2, lax.axis_index("gz") >> 1, part) - total).astype(BF16)
     solved_ref[2] = times_transposed(ready, inv_ref[2])
-    solved_ref[pair] = front_ref[...]
-    solved_ref[1 - pair] = other_ref[:, size:].astype(F32)
+    for j in (0, 1):
+        at = slice(size + j * width, size + (j + 1) * width)
+        solved_ref[j] = fronts_ref[j] + (r3[:, at].astype(F32) + r2[:, at].astype(F32) + r1[:, at].astype(F32))
     send_ref[...] = solved_ref[...].astype(BF16)
 
 
@@ -568,6 +596,8 @@
     )
     arrived = partners(ready, ROW_MOVES)
     (top_whole,) = whole_call(whole_top_kernel, "whole_top", [top_half, top_other], [((size, size), BF16)])
+    (share,) = whole_call(apex_share_kernel, "apex_share", [apex_inv, apex_lower], [((2, width, width), BF16)], after=[ready])
+    shares = partners(share, ROW_MOVES)
     kept, given, late_kept, late_given, mid_solved = whole_call(
         mid_solve_kernel, "mid_solve", [mid_pattern, ready, *arrived, parent_diagonal_inverse, mid_lower, layer_up],
         [((4, part, size), F32), ((4, part, size), BF16), ((2, 2, quarter, size), F32), ((2, 2, quarter, size), BF16)]
@@ -598,6 +628,11 @@
         scratch=[pltpu.VMEM((count // 2, size), BF16), pltpu.VMEM((count // 2, size), F32)],
         after=[late_given],
     )
+    held, _ = lax.optimization_barrier((share, other))
+    (front_share,) = whole_call(
+        rows_of_shares_kernel, "front_share", [held, *shares], [((4, 2, width, width), BF16)], after=[kept]
+    )
+    (col_share,) = partners(front_share, [{"col": 1}])
     arrived = partners(given, ROW_MOVES)
     top_solved, top_send, kept, given = whole_call(
         top_up_kernel, "top_up", [kept, *arrived, top_lower, late_kept, late_other],
@@ -606,30 +641,31 @@
         scratch=[pltpu.VMEM((4 * part, size), F32)],
     )
     (other,) = partners(given, [{"gz": 1}])
+    held, col_held, *_ = lax.optimization_barrier((front_share, col_share, *arrived))
+    core_share, both_share = partners([held, col_held], [{"gz": 1}] * 2)
+    front_whole, lower_whole = whole_call(
+        whole_front_kernel, "whole_front", [front_share, col_share, core_share, both_share], [((size, size), BF16)] * 2
+    )
     (other_top,) = partners(top_send, [{"col": 1}])
 
-    own, send, last = whole_call(
-        front_pieces_kernel, "front_pieces", [kept, other],
-        [((2 * part, size), F32), ((2 * part, size), BF16), ((2, part, size), F32)],
-    )
-    arrived = partners(send, ROW_MOVES)
-    front, kept, given = whole_call(
-        front_solve_kernel, "front_solve", [apex_rhs, own, *arrived, apex_inv, apex_lower, last],
-        [((part, width), F32), ((part, size), F32), ((part, size + width), BF16)],
-        flops=count * size * width,
-        scratch=[pltpu.VMEM((2 * part, size), F32), pltpu.VMEM((2 * part, width), F32)],
+    front, last, given = whole_call(
+        front_kernel, "front", [apex_rhs, kept, other, front_whole, lower_whole],
+        [((part, size), BF16), ((part, size), F32), ((2, part, size), BF16)],
+        flops=count * size * size // 2,
+        scratch=[pltpu.VMEM((2 * part, size), BF16)] + [pltpu.VMEM((2 * part, size), F32)] * 2,
     )
 
     (other,) = partners(given, [{"gz": 2}])
-    own, send = whole_call(
-        last_pieces_kernel, "last_pieces", [kept, other], [((part, size), F32), ((part, size), BF16)]
-    )
-    arrived = partners(send, ROW_MOVES)
+    own, fronts, *given = whole_call(
+        last_pieces_kernel, "last_pieces", [front, last, other],
+        [((part, size), F32), ((2, part, width), F32)] + [((part, size + 2 * width), BF16)] * 3,
+    )
+    arrived = partners(given, ROW_MOVES)
     top_all, placed = whole_call(
         place_top_kernel, "place_top", [top_solved, other_top], [((1, count, width), F32), ((8, width), F32)], after=[own]
     )
     solved, send = whole_call(
-        last_solve_kernel, "last_solve", [apex_rhs, apex_inv, own, *arrived, front, other],
+        last_solve_kernel, "last_solve", [apex_rhs, apex_inv, own, fronts, *arrived],
         [((3, part, width), F32), ((3, part, width), BF16)],
         flops=count * size * width // 4,
         after=[placed],

time: 81 us -> 79.2 us (0.978)
  waiting for transfers between devices: 25 us -> 23.7 us
    ppermute x27 -> x30, waiting for transfers between devices: 25 us -> 23.7 us  [partners(): arrived.append(lax.ppermute(item, axes, route))]
    ppermute x27 -> x30, starting transfers between devices: 38.2 us -> 37.4 us  [partners(): arrived.append(lax.ppermute(item, axes, route))]
    pallas_call x15 -> x17, Pallas kernels: 4.63 us -> 4.97 us  [whole_call(): pl.pallas_call(body, in_specs=[pl.BlockSpec(memory_space=pl.ANY)] * len(a...]
  transfers between devices with their start and end apart: 27 -> 30, of which waited for: 14 -> 16; matrix products, arithmetic and copies ran while one was open for 0% -> 0% of each run, Pallas kernels for 8% -> 9%
where the time goes in v6:
time: 79.2 us; the launch traced here: 79 us
  starting transfers between devices  37.4 us (47%)
  waiting for transfers between devices  23.7 us (30%)
  Pallas kernels  15.9 us (20%)
  local copies, waits for them, and re-layouts  1.1 us (1%)
  between operations  0.91 us (1%)
    ppermute x30, starting transfers between devices, partners(): arrived.append(lax.ppermute(item, axes, route))  37.4 us
    ppermute x30, waiting for transfers between devices, partners(): arrived.append(lax.ppermute(item, axes, route))  23.7 us
    pallas_call x1, Pallas kernels, leaf_solve(): pl.pallas_call(functools.partial(leaf_kernel, slots), in_specs=[pl.BlockS...  5.32 us
    pallas_call x17, Pallas kernels, whole_call(): pl.pallas_call(body, in_specs=[pl.BlockSpec(memory_space=pl.ANY)] * len(a...  4.97 us
    pallas_call x1, Pallas kernels, leaf_coupling(): pl.pallas_call(coupling_kernel, in_specs=[pl.BlockSpec(memory_space=pltpu...  3.28 us
    pallas_call x1, Pallas kernels, own_terms(): pl.pallas_call(own_terms_kernel, in_specs=[pl.BlockSpec(memory_space=pltp...  2.31 us
  transfers between devices with their start and end apart: 30, of which 16 were waited for; matrix products, arithmetic and copies ran while one was open for 0% of the time, Pallas kernels for 9%

profile of v6, /device:TPU:0, one launch (start us, length us, event | category | flops | bytes accessed | tf_op | source)
XLA Modules:
  0.0 79.0 jit_solution(3606518365764312509)
XLA Ops:
  0.7 5.3 %leaf_solve.1 = (f32[8,256,128]{2,1,0:T(8,128)}, bf16[8,256,128]{2,1,0:T(8,128)(2,1)}, bf16[256,512]{1,0:T(8,128)(2,1)}) custom-call(s32[8]{0:T(128)} %parent_ref.3, f32[8,256,512]{2,1,0:T(8,128)} %rhs_ref.2, bf16[8,128,512]{2,1,0:T(8,128)(2,1)} %inv_ref.1, bf16[8,512,128]{2,1,0:T(8,128)(2,1)} %mid_ref.3), custom_call_target="tpu_custom_call" | custom-call | flops 536870912 | bytes 7864320 | tf_op jit(solution)/shard_map/leaf_solve/pallas_call | solution.py:77
  6.0 3.0 %collective-permute-start.3 = (bf16[256,512]{1,0:T(8,128)(2,1)}, bf16[256,512]{1,0:T(8,128)(2,1)S(1)}, u32[]{:S(2)}, u32[]{:S(2)}) collective-permute-start(bf16[256,512]{1,0:T(8,128)(2,1)} %get-tuple-element.49), channel_id=1, source_target_pairs={{0,1},{1,0},{2,3},{3,2},{4,5},{5,4},{6,7},{7,6},{8,9},{9,8},{10,11... | collective-permute-start | bytes 786440 | tf_op jit(solution)/shard_map/ppermute | solution.py:330
  9.0 3.7 %collective-permute-start = (bf16[128,256]{1,0:T(8,128)(2,1)S(1)}, bf16[128,256]{1,0:T(8,128)(2,1)S(1)}, u32[]{:S(2)}, u32[]{:S(2)}) collective-permute-start(bf16[128,256]{1,0:T(8,128)(2,1)S(1)} %top_share.1.refs_1_), channel_id=1, source_target_pairs={{0,6},{2,4},{4,2},{6,0},{1,7},{3,5},{5,3},{7,1},{8,14},{10,12},{12... | collective-permute-start | bytes 196616 | tf_op jit(solution)/shard_map/ppermute | solution.py:330
  14.5 2.3 %own_terms.1 = (bf16[256,512]{1,0:T(8,128)(2,1)S(1)}, f32[64,512]{1,0:T(8,128)S(1)}) custom-call(s32[8]{0:T(128)S(1)} %copy-done.11, bf16[8,256,128]{2,1,0:T(8,128)(2,1)S(1)} %copy-done.1, bf16[8,512,128]{2,1,0:T(8,128)(2,1)} %mid_ref.3, f32[1,256,512]{2,1,0:T(8,128)S(1)} %copy-done.3), custom_call_target="tpu_custom_call" | custom-call | flops 268435456 | bytes 1572864 | tf_op jit(solution)/shard_map/own_terms/pallas_call | solution.py:126
  18.8 2.6 %collective-permute-start.5 = (bf16[64,512]{1,0:T(8,128)(2,1)S(1)}, bf16[64,512]{1,0:T(8,128)(2,1)S(1)}, u32[]{:S(2)}, u32[]{:S(2)}) collective-permute-start(bf16[64,512]{1,0:T(8,128)(2,1)S(1)} %get-tuple-element.51), channel_id=1, source_target_pairs={{0,6},{2,4},{4,2},{6,0},{1,7},{3,5},{5,3},{7,1},{8,14},{10,12},{12... | collective-permute-start | bytes 196616 | tf_op jit(solution)/shard_map/ppermute | solution.py:330
  21.4 1.8 %collective-permute-start.7 = (bf16[64,512]{1,0:T(8,128)(2,1)S(1)}, bf16[64,512]{1,0:T(8,128)(2,1)S(1)}, u32[]{:S(2)}, u32[]{:S(2)}) collective-permute-start(bf16[64,512]{1,0:T(8,128)(2,1)S(1)} %get-tuple-element.53), channel_id=1, source_target_pairs={{0,2},{2,0},{4,6},{6,4},{1,3},{3,1},{5,7},{7,5},{8,10},{10,8},{12,... | collective-permute-start | bytes 196616 | tf_op jit(solution)/shard_map/ppermute | solution.py:330
  23.2 3.3 %leaf_coupling.1.refs_0_.refs_8_ = f32[3,256,512]{2,1,0:T(8,128)S(1)} custom-call(s32[3,8]{1,0:T(4,128)S(1)} %bitcast.2, bf16[8,256,128]{2,1,0:T(8,128)(2,1)S(1)} %copy-done.1, bf16[8,3,512,128]{3,2,1,0:T(8,128)(2,1)} %lower_ref.1), custom_call_target="tpu_custom_call" | custom-call | flops 805306368 | bytes 5242880 | tf_op jit(solution)/shard_map/leaf_coupling/pallas_call | solution.py:168
  27.3 2.0 %collective-permute-start.8 = (bf16[64,512]{1,0:T(8,128)(2,1)S(1)}, bf16[64,512]{1,0:T(8,128)(2,1)S(1)}, u32[]{:S(2)}, u32[]{:S(2)}) collective-permute-start(bf16[64,512]{1,0:T(8,128)(2,1)S(1)} %mid_total.1.refs_2_.refs_0_), channel_id=1, source_target_pairs={{0,6},{2,4},{4,2},{6,0},{1,7},{3,5},{5,3},{7,1},{8,14},{10,12},{12... | collective-permute-start | bytes 196616 | tf_op jit(solution)/shard_map/ppermute | solution.py:330
  29.3 2.4 %collective-permute-start.10 = (bf16[64,512]{1,0:T(8,128)(2,1)S(1)}, bf16[64,512]{1,0:T(8,128)(2,1)S(1)}, u32[]{:S(2)}, u32[]{:S(2)}) collective-permute-start(bf16[64,512]{1,0:T(8,128)(2,1)S(1)} %mid_total.1.refs_2_.refs_0_), channel_id=1, source_target_pairs={{0,2},{2,0},{4,6},{6,4},{1,3},{3,1},{5,7},{7,5},{8,10},{10,8},{12,... | collective-permute-start | bytes 196616 | tf_op jit(solution)/shard_map/ppermute | solution.py:330
  31.8 2.3 %collective-permute-done.8.refs_3_ = bf16[64,512]{1,0:T(8,128)(2,1)S(1)} collective-permute-done((bf16[64,512]{1,0:T(8,128)(2,1)S(1)}, bf16[64,512]{1,0:T(8,128)(2,1)S(1)}, u32[]{:S(2)}, u32[]{:S(2)}) %collective-permute-start.8) | collective-permute-done | bytes 65568 | tf_op jit(solution)/shard_map/ppermute | solution.py:330
  35.5 1.8 %mid_solve.1 = (f32[4,32,512]{2,1,0:T(8,128)S(1)}, bf16[4,32,512]{2,1,0:T(8,128)(2,1)S(1)}, f32[2,2,64,512]{3,2,1,0:T(8,128)S(1)}, bf16[2,2,64,512]{3,2,1,0:T(8,128)(2,1)S(1)}, f32[256,128]{1,0:T(8,128)}) custom-call(bf16[512,512]{1,0:T(8,128)(2,1)S(1)} %whole_top.1.refs_0_.refs_4_, s32[1,2]{1,0:T(1,128)S(1)} %copy-done.12, ...), custom_call_target="tpu_custom_call" | custom-call | flops 134217728 | bytes 3670024 | tf_op jit(solution)/shard_map/mid_solve/pallas_call | solution.py:342
  38.7 2.1 %collective-permute-start.18 = (bf16[2,128,128]{2,1,0:T(8,128)(2,1)S(1)}, bf16[2,128,128]{2,1,0:T(8,128)(2,1)S(1)}, u32[]{:S(2)}, u32[]{:S(2)}) collective-permute-start(bf16[2,128,128]{2,1,0:T(8,128)(2,1)S(1)} %apex_share.1.refs_1_), channel_id=1, source_target_pairs={{0,6},{2,4},{4,2},{6,0},{1,7},{3,5},{5,3},{7,1},{8,14},{10,12},{12... | collective-permute-start | bytes 196616 | tf_op jit(solution)/shard_map/ppermute | solution.py:330
  41.1 2.1 %collective-permute-start.20 = (bf16[2,128,128]{2,1,0:T(8,128)(2,1)S(1)}, bf16[2,128,128]{2,1,0:T(8,128)(2,1)S(1)}, u32[]{:S(2)}, u32[]{:S(2)}) collective-permute-start(bf16[2,128,128]{2,1,0:T(8,128)(2,1)S(1)} %apex_share.1.refs_1_), channel_id=1, source_target_pairs={{0,2},{2,0},{4,6},{6,4},{1,3},{3,1},{5,7},{7,5},{8,10},{10,8},{12,... | collective-permute-start | bytes 196616 | tf_op jit(solution)/shard_map/ppermute | solution.py:330
  43.8 1.8 %collective-permute-done.18.refs_2_ = bf16[2,128,128]{2,1,0:T(8,128)(2,1)S(1)} collective-permute-done((bf16[2,128,128]{2,1,0:T(8,128)(2,1)S(1)}, bf16[2,128,128]{2,1,0:T(8,128)(2,1)S(1)}, u32[]{:S(2)}, u32[]{:S(2)}) %collective-permute-start.18) | collective-permute-done | bytes 65568 | tf_op jit(solution)/shard_map/ppermute | solution.py:330
  45.6 2.0 %collective-permute-done.19.refs_3_ = bf16[2,128,128]{2,1,0:T(8,128)(2,1)S(1)} collective-permute-done((bf16[2,128,128]{2,1,0:T(8,128)(2,1)S(1)}, bf16[2,128,128]{2,1,0:T(8,128)(2,1)S(1)}, u32[]{:S(2)}, u32[]{:S(2)}) %collective-permute-start.19) | collective-permute-done | bytes 65568 | tf_op jit(solution)/shard_map/ppermute | solution.py:330
  48.5 2.1 %collective-permute-start.13 = (bf16[128,128]{1,0:T(8,128)(2,1)S(1)}, bf16[128,128]{1,0:T(8,128)(2,1)S(1)}, u32[]{:S(2)}, u32[]{:S(2)}) collective-permute-start(bf16[128,128]{1,0:T(8,128)(2,1)S(1)} %get-tuple-element.61), channel_id=1, source_target_pairs={{0,6},{2,4},{4,2},{6,0},{1,7},{3,5},{5,3},{7,1},{8,14},{10,12},{12... | collective-permute-start | bytes 98312 | tf_op jit(solution)/shard_map/ppermute | solution.py:330
  50.6 2.3 %collective-permute-start.15 = (bf16[128,128]{1,0:T(8,128)(2,1)S(1)}, bf16[128,128]{1,0:T(8,128)(2,1)S(1)}, u32[]{:S(2)}, u32[]{:S(2)}) collective-permute-start(bf16[128,128]{1,0:T(8,128)(2,1)S(1)} %get-tuple-element.63), channel_id=1, source_target_pairs={{0,2},{2,0},{4,6},{6,4},{1,3},{3,1},{5,7},{7,5},{8,10},{10,8},{12,... | collective-permute-start | bytes 98312 | tf_op jit(solution)/shard_map/ppermute | solution.py:330
  55.4 1.5 %collective-permute-done.21.refs_1_ = bf16[4,2,128,128]{3,2,1,0:T(8,128)(2,1)S(1)} collective-permute-done((bf16[4,2,128,128]{3,2,1,0:T(8,128)(2,1)S(1)}, bf16[4,2,128,128]{3,2,1,0:T(8,128)(2,1)S(1)}, u32[]{:S(2)}, u32[]{:S(2)}) %collective-permute-start.21) | collective-permute-done | bytes 262176 | tf_op jit(solution)/shard_map/ppermute | solution.py:330
  60.9 1.6 %collective-permute-start.24 = (bf16[2,32,512]{2,1,0:T(8,128)(2,1)S(1)}, bf16[2,32,512]{2,1,0:T(8,128)(2,1)S(1)}, u32[]{:S(2)}, u32[]{:S(2)}) collective-permute-start(bf16[2,32,512]{2,1,0:T(8,128)(2,1)S(1)} %get-tuple-element.74), channel_id=1, source_target_pairs={{0,16},{8,24},{16,0},{24,8},{1,17},{9,25},{17,1},{25,9},{2,18},{10... | collective-permute-start | bytes 196616 | tf_op jit(solution)/shard_map/ppermute | solution.py:330
  62.5 2.8 %collective-permute-done.24.refs_2_ = bf16[2,32,512]{2,1,0:T(8,128)(2,1)S(1)} collective-permute-done((bf16[2,32,512]{2,1,0:T(8,128)(2,1)S(1)}, bf16[2,32,512]{2,1,0:T(8,128)(2,1)S(1)}, u32[]{:S(2)}, u32[]{:S(2)}) %collective-permute-start.24) | collective-permute-done | bytes 65568 | tf_op jit(solution)/shard_map/ppermute | solution.py:330
  65.3 2.1 %collective-permute-start.26 = (bf16[32,768]{1,0:T(8,128)(2,1)S(1)}, bf16[32,768]{1,0:T(8,128)(2,1)S(1)}, u32[]{:S(2)}, u32[]{:S(2)}) collective-permute-start(bf16[32,768]{1,0:T(8,128)(2,1)S(1)} %get-tuple-element.81), channel_id=1, source_target_pairs={{0,6},{2,4},{4,2},{6,0},{1,7},{3,5},{5,3},{7,1},{8,14},{10,12},{12... | collective-permute-start | bytes 147464 | tf_op jit(solution)/shard_map/ppermute | solution.py:330
  67.4 2.3 %collective-permute-start.28 = (bf16[32,768]{1,0:T(8,128)(2,1)S(1)}, bf16[32,768]{1,0:T(8,128)(2,1)S(1)}, u32[]{:S(2)}, u32[]{:S(2)}) collective-permute-start(bf16[32,768]{1,0:T(8,128)(2,1)S(1)} %get-tuple-element.83), channel_id=1, source_target_pairs={{0,2},{2,0},{4,6},{6,4},{1,3},{3,1},{5,7},{7,5},{8,10},{10,8},{12,... | collective-permute-start | bytes 147464 | tf_op jit(solution)/shard_map/ppermute | solution.py:330
  70.6 3.1 %collective-permute-done.25.refs_2_ = bf16[4,32,128]{2,1,0:T(8,128)(2,1)S(1)} collective-permute-done((bf16[4,32,128]{2,1,0:T(8,128)(2,1)S(1)}, bf16[4,32,128]{2,1,0:T(8,128)(2,1)S(1)}, u32[]{:S(2)}, u32[]{:S(2)}) %collective-permute-start.25) | collective-permute-done | bytes 32800 | tf_op jit(solution)/shard_map/ppermute | solution.py:330
  75.3 3.0 %collective-permute-done.29.refs_1_ = bf16[3,32,128]{2,1,0:T(8,128)(2,1)S(1)} collective-permute-done((bf16[3,32,128]{2,1,0:T(8,128)(2,1)S(1)}, bf16[3,32,128]{2,1,0:T(8,128)(2,1)S(1)}, u32[]{:S(2)}, u32[]{:S(2)}) %collective-permute-start.29) | collective-permute-done | bytes 24608 | tf_op jit(solution)/shard_map/ppermute | solution.py:330
  (82 shorter events, 18.8 us)
Async XLA Ops:
  6.0 12.1 %collective-permute-start.3 = (bf16[256,512]{1,0:T(8,128)(2,1)}, bf16[256,512]{1,0:T(8,128)(2,1)S(1)}, u32[]{:S(2)}, u32[]{:S(2)}) collective-permute-start(bf16[256,512]{1,0:T(8,128)(2,1)} %get-tuple-element.49), channel_id=1, source_target_pairs={{0,1},{1,0},{2,3},{3,2},{4,5},{5,4},{6,7},{7,6},{8,9},{9,8},{10,11... | collective-permute-start | bytes 786440 | tf_op jit(solution)/shard_map/ppermute | solution.py:330
  9.0 7.8 %collective-permute-start = (bf16[128,256]{1,0:T(8,128)(2,1)S(1)}, bf16[128,256]{1,0:T(8,128)(2,1)S(1)}, u32[]{:S(2)}, u32[]{:S(2)}) collective-permute-start(bf16[128,256]{1,0:T(8,128)(2,1)S(1)} %top_share.1.refs_1_), channel_id=1, source_target_pairs={{0,6},{2,4},{4,2},{6,0},{1,7},{3,5},{5,3},{7,1},{8,14},{10,12},{12... | collective-permute-start | bytes 196616 | tf_op jit(solution)/shard_map/ppermute | solution.py:330
  12.7 5.4 %collective-permute-start.1 = (bf16[128,256]{1,0:T(8,128)(2,1)S(1)}, bf16[128,256]{1,0:T(8,128)(2,1)S(1)}, u32[]{:S(2)}, u32[]{:S(2)}) collective-permute-start(bf16[128,256]{1,0:T(8,128)(2,1)S(1)} %top_share.1.refs_1_), channel_id=1, source_target_pairs={{0,4},{2,6},{4,0},{6,2},{1,5},{3,7},{5,1},{7,3},{8,12},{10,14},{12... | collective-permute-start | bytes 196616 | tf_op jit(solution)/shard_map/ppermute | solution.py:330
  12.7 5.4 %collective-permute-start.2 = (bf16[128,256]{1,0:T(8,128)(2,1)S(1)}, bf16[128,256]{1,0:T(8,128)(2,1)S(1)}, u32[]{:S(2)}, u32[]{:S(2)}) collective-permute-start(bf16[128,256]{1,0:T(8,128)(2,1)S(1)} %top_share.1.refs_1_), channel_id=1, source_target_pairs={{0,2},{2,0},{4,6},{6,4},{1,3},{3,1},{5,7},{7,5},{8,10},{10,8},{12,... | collective-permute-start | bytes 196616 | tf_op jit(solution)/shard_map/ppermute | solution.py:330
  18.3 13.5 %collective-permute-start.4 = (bf16[512,256]{1,0:T(8,128)(2,1)S(1)}, bf16[512,256]{1,0:T(8,128)(2,1)S(1)}, u32[]{:S(2)}, u32[]{:S(2)}) collective-permute-start(bf16[512,256]{1,0:T(8,128)(2,1)S(1)} %half_top.1.refs_0_), channel_id=1, source_target_pairs={{0,1},{1,0},{2,3},{3,2},{4,5},{5,4},{6,7},{7,6},{8,9},{9,8},{10,11... | collective-permute-start | bytes 786440 | tf_op jit(solution)/shard_map/ppermute | solution.py:330
  18.8 7.7 %collective-permute-start.5 = (bf16[64,512]{1,0:T(8,128)(2,1)S(1)}, bf16[64,512]{1,0:T(8,128)(2,1)S(1)}, u32[]{:S(2)}, u32[]{:S(2)}) collective-permute-start(bf16[64,512]{1,0:T(8,128)(2,1)S(1)} %get-tuple-element.51), channel_id=1, source_target_pairs={{0,6},{2,4},{4,2},{6,0},{1,7},{3,5},{5,3},{7,1},{8,14},{10,12},{12... | collective-permute-start | bytes 196616 | tf_op jit(solution)/shard_map/ppermute | solution.py:330
  21.4 5.8 %collective-permute-start.6 = (bf16[64,512]{1,0:T(8,128)(2,1)S(1)}, bf16[64,512]{1,0:T(8,128)(2,1)S(1)}, u32[]{:S(2)}, u32[]{:S(2)}) collective-permute-start(bf16[64,512]{1,0:T(8,128)(2,1)S(1)} %get-tuple-element.52), channel_id=1, source_target_pairs={{0,4},{2,6},{4,0},{6,2},{1,5},{3,7},{5,1},{7,3},{8,12},{10,14},{12... | collective-permute-start | bytes 196616 | tf_op jit(solution)/shard_map/ppermute | solution.py:330
  21.4 5.8 %collective-permute-start.7 = (bf16[64,512]{1,0:T(8,128)(2,1)S(1)}, bf16[64,512]{1,0:T(8,128)(2,1)S(1)}, u32[]{:S(2)}, u32[]{:S(2)}) collective-permute-start(bf16[64,512]{1,0:T(8,128)(2,1)S(1)} %get-tuple-element.53), channel_id=1, source_target_pairs={{0,2},{2,0},{4,6},{6,4},{1,3},{3,1},{5,7},{7,5},{8,10},{10,8},{12,... | collective-permute-start | bytes 196616 | tf_op jit(solution)/shard_map/ppermute | solution.py:330
  27.3 6.9 %collective-permute-start.8 = (bf16[64,512]{1,0:T(8,128)(2,1)S(1)}, bf16[64,512]{1,0:T(8,128)(2,1)S(1)}, u32[]{:S(2)}, u32[]{:S(2)}) collective-permute-start(bf16[64,512]{1,0:T(8,128)(2,1)S(1)} %mid_total.1.refs_2_.refs_0_), channel_id=1, source_target_pairs={{0,6},{2,4},{4,2},{6,0},{1,7},{3,5},{5,3},{7,1},{8,14},{10,12},{12... | collective-permute-start | bytes 196616 | tf_op jit(solution)/shard_map/ppermute | solution.py:330
  29.3 6.2 %collective-permute-start.9 = (bf16[64,512]{1,0:T(8,128)(2,1)S(1)}, bf16[64,512]{1,0:T(8,128)(2,1)S(1)}, u32[]{:S(2)}, u32[]{:S(2)}) collective-permute-start(bf16[64,512]{1,0:T(8,128)(2,1)S(1)} %mid_total.1.refs_2_.refs_0_), channel_id=1, source_target_pairs={{0,4},{2,6},{4,0},{6,2},{1,5},{3,7},{5,1},{7,3},{8,12},{10,14},{12... | collective-permute-start | bytes 196616 | tf_op jit(solution)/shard_map/ppermute | solution.py:330
  29.3 6.2 %collective-permute-start.10 = (bf16[64,512]{1,0:T(8,128)(2,1)S(1)}, bf16[64,512]{1,0:T(8,128)(2,1)S(1)}, u32[]{:S(2)}, u32[]{:S(2)}) collective-permute-start(bf16[64,512]{1,0:T(8,128)(2,1)S(1)} %mid_total.1.refs_2_.refs_0_), channel_id=1, source_target_pairs={{0,2},{2,0},{4,6},{6,4},{1,3},{3,1},{5,7},{7,5},{8,10},{10,8},{12,... | collective-permute-start | bytes 196616 | tf_op jit(solution)/shard_map/ppermute | solution.py:330
  37.4 6.0 %collective-permute-start.11 = (bf16[2,2,64,512]{3,2,1,0:T(8,128)(2,1)S(1)}, bf16[2,2,64,512]{3,2,1,0:T(8,128)(2,1)S(1)}, u32[]{:S(2)}, u32[]{:S(2)}) collective-permute-start(bf16[2,2,64,512]{3,2,1,0:T(8,128)(2,1)S(1)} %get-tuple-element.56), channel_id=1, source_target_pairs={{0,8},{8,0},{16,24},{24,16},{1,9},{9,1},{17,25},{25,17},{2,10},{10... | collective-permute-start | bytes 786440 | tf_op jit(solution)/shard_map/ppermute | solution.py:330
  37.5 5.9 %collective-permute-start.12 = (bf16[4,32,512]{2,1,0:T(8,128)(2,1)S(1)}, bf16[4,32,512]{2,1,0:T(8,128)(2,1)S(1)}, u32[]{:S(2)}, u32[]{:S(2)}) collective-permute-start(bf16[4,32,512]{2,1,0:T(8,128)(2,1)S(1)} %get-tuple-element.59), channel_id=1, source_target_pairs={{0,1},{1,0},{2,3},{3,2},{4,5},{5,4},{6,7},{7,6},{8,9},{9,8},{10,11... | collective-permute-start | bytes 393224 | tf_op jit(solution)/shard_map/ppermute | solution.py:330
  38.7 6.8 %collective-permute-start.18 = (bf16[2,128,128]{2,1,0:T(8,128)(2,1)S(1)}, bf16[2,128,128]{2,1,0:T(8,128)(2,1)S(1)}, u32[]{:S(2)}, u32[]{:S(2)}) collective-permute-start(bf16[2,128,128]{2,1,0:T(8,128)(2,1)S(1)} %apex_share.1.refs_1_), channel_id=1, source_target_pairs={{0,6},{2,4},{4,2},{6,0},{1,7},{3,5},{5,3},{7,1},{8,14},{10,12},{12... | collective-permute-start | bytes 196616 | tf_op jit(solution)/shard_map/ppermute | solution.py:330
  40.8 6.7 %collective-permute-start.19 = (bf16[2,128,128]{2,1,0:T(8,128)(2,1)S(1)}, bf16[2,128,128]{2,1,0:T(8,128)(2,1)S(1)}, u32[]{:S(2)}, u32[]{:S(2)}) collective-permute-start(bf16[2,128,128]{2,1,0:T(8,128)(2,1)S(1)} %apex_share.1.refs_1_), channel_id=1, source_target_pairs={{0,4},{2,6},{4,0},{6,2},{1,5},{3,7},{5,1},{7,3},{8,12},{10,14},{12... | collective-permute-start | bytes 196616 | tf_op jit(solution)/shard_map/ppermute | solution.py:330
  41.1 6.5 %collective-permute-start.20 = (bf16[2,128,128]{2,1,0:T(8,128)(2,1)S(1)}, bf16[2,128,128]{2,1,0:T(8,128)(2,1)S(1)}, u32[]{:S(2)}, u32[]{:S(2)}) collective-permute-start(bf16[2,128,128]{2,1,0:T(8,128)(2,1)S(1)} %apex_share.1.refs_1_), channel_id=1, source_target_pairs={{0,2},{2,0},{4,6},{6,4},{1,3},{3,1},{5,7},{7,5},{8,10},{10,8},{12,... | collective-permute-start | bytes 196616 | tf_op jit(solution)/shard_map/ppermute | solution.py:330
  47.6 9.2 %collective-permute-start.21 = (bf16[4,2,128,128]{3,2,1,0:T(8,128)(2,1)S(1)}, bf16[4,2,128,128]{3,2,1,0:T(8,128)(2,1)S(1)}, u32[]{:S(2)}, u32[]{:S(2)}) collective-permute-start(bf16[4,2,128,128]{3,2,1,0:T(8,128)(2,1)S(1)} %front_share.1.refs_0_), channel_id=1, source_target_pairs={{0,1},{1,0},{2,3},{3,2},{4,5},{5,4},{6,7},{7,6},{8,9},{9,8},{10,11... | collective-permute-start | bytes 786440 | tf_op jit(solution)/shard_map/ppermute | solution.py:330
  48.5 5.7 %collective-permute-start.13 = (bf16[128,128]{1,0:T(8,128)(2,1)S(1)}, bf16[128,128]{1,0:T(8,128)(2,1)S(1)}, u32[]{:S(2)}, u32[]{:S(2)}) collective-permute-start(bf16[128,128]{1,0:T(8,128)(2,1)S(1)} %get-tuple-element.61), channel_id=1, source_target_pairs={{0,6},{2,4},{4,2},{6,0},{1,7},{3,5},{5,3},{7,1},{8,14},{10,12},{12... | collective-permute-start | bytes 98312 | tf_op jit(solution)/shard_map/ppermute | solution.py:330
  50.6 4.8 %collective-permute-start.14 = (bf16[128,128]{1,0:T(8,128)(2,1)S(1)}, bf16[128,128]{1,0:T(8,128)(2,1)S(1)}, u32[]{:S(2)}, u32[]{:S(2)}) collective-permute-start(bf16[128,128]{1,0:T(8,128)(2,1)S(1)} %get-tuple-element.62), channel_id=1, source_target_pairs={{0,4},{2,6},{4,0},{6,2},{1,5},{3,7},{5,1},{7,3},{8,12},{10,14},{12... | collective-permute-start | bytes 98312 | tf_op jit(solution)/shard_map/ppermute | solution.py:330
  50.6 4.8 %collective-permute-start.15 = (bf16[128,128]{1,0:T(8,128)(2,1)S(1)}, bf16[128,128]{1,0:T(8,128)(2,1)S(1)}, u32[]{:S(2)}, u32[]{:S(2)}) collective-permute-start(bf16[128,128]{1,0:T(8,128)(2,1)S(1)} %get-tuple-element.63), channel_id=1, source_target_pairs={{0,2},{2,0},{4,6},{6,4},{1,3},{3,1},{5,7},{7,5},{8,10},{10,8},{12,... | collective-permute-start | bytes 98312 | tf_op jit(solution)/shard_map/ppermute | solution.py:330
  52.9 5.8 %collective-permute-start.16 = (bf16[2,2,32,512]{3,2,1,0:T(8,128)(2,1)S(1)}, bf16[2,2,32,512]{3,2,1,0:T(8,128)(2,1)S(1)}, u32[]{:S(2)}, u32[]{:S(2)}) collective-permute-start(bf16[2,2,32,512]{3,2,1,0:T(8,128)(2,1)S(1)} %get-tuple-element.57.refs_0_), channel_id=1, source_target_pairs={{0,1},{1,0},{2,3},{3,2},{4,5},{5,4},{6,7},{7,6},{8,9},{9,8},{10,11... | collective-permute-start | bytes 393224 | tf_op jit(solution)/shard_map/ppermute | solution.py:330
  65.3 9.0 %collective-permute-start.26 = (bf16[32,768]{1,0:T(8,128)(2,1)S(1)}, bf16[32,768]{1,0:T(8,128)(2,1)S(1)}, u32[]{:S(2)}, u32[]{:S(2)}) collective-permute-start(bf16[32,768]{1,0:T(8,128)(2,1)S(1)} %get-tuple-element.81), channel_id=1, source_target_pairs={{0,6},{2,4},{4,2},{6,0},{1,7},{3,5},{5,3},{7,1},{8,14},{10,12},{12... | collective-permute-start | bytes 147464 | tf_op jit(solution)/shard_map/ppermute | solution.py:330
  67.4 6.9 %collective-permute-start.27 = (bf16[32,768]{1,0:T(8,128)(2,1)S(1)}, bf16[32,768]{1,0:T(8,128)(2,1)S(1)}, u32[]{:S(2)}, u32[]{:S(2)}) collective-permute-start(bf16[32,768]{1,0:T(8,128)(2,1)S(1)} %get-tuple-element.82), channel_id=1, source_target_pairs={{0,4},{2,6},{4,0},{6,2},{1,5},{3,7},{5,1},{7,3},{8,12},{10,14},{12... | collective-permute-start | bytes 147464 | tf_op jit(solution)/shard_map/ppermute | solution.py:330
  67.4 6.9 %collective-permute-start.28 = (bf16[32,768]{1,0:T(8,128)(2,1)S(1)}, bf16[32,768]{1,0:T(8,128)(2,1)S(1)}, u32[]{:S(2)}, u32[]{:S(2)}) collective-permute-start(bf16[32,768]{1,0:T(8,128)(2,1)S(1)} %get-tuple-element.83), channel_id=1, source_target_pairs={{0,2},{2,0},{4,6},{6,4},{1,3},{3,1},{5,7},{7,5},{8,10},{10,8},{12,... | collective-permute-start | bytes 147464 | tf_op jit(solution)/shard_map/ppermute | solution.py:330
  (19 other events, 197.8 us)

commit v7 on v6

--- a/solution.py
+++ b/solution.py
@@ -659,6 +659,7 @@
     own, fronts, *given = whole_call(
         last_pieces_kernel, "last_pieces", [front, last, other],
         [((part, size), F32), ((2, part, width), F32)] + [((part, size + 2 * width), BF16)] * 3,
+        after=[other_top],
     )
     arrived = partners(given, ROW_MOVES)
     top_all, placed = whole_call(

time: 79.2 us -> 78.9 us (level)
  transfers between devices with their start and end apart: 30 -> 30, of which waited for: 16 -> 17; matrix products, arithmetic and copies ran while one was open for 0% -> 0% of each run, Pallas kernels for 9% -> 9%
where the time goes in v7:
time: 78.9 us; the launch traced here: 78.6 us
  starting transfers between devices  37.4 us (47%)
  waiting for transfers between devices  23.4 us (30%)
  Pallas kernels  15.9 us (20%)
  local copies, waits for them, and re-layouts  1.1 us (1%)
  between operations  0.91 us (1%)
    ppermute x30, starting transfers between devices, partners(): arrived.append(lax.ppermute(item, axes, route))  37.4 us
    ppermute x30, waiting for transfers between devices, partners(): arrived.append(lax.ppermute(item, axes, route))  23.4 us
    pallas_call x1, Pallas kernels, leaf_solve(): pl.pallas_call(functools.partial(leaf_kernel, slots), in_specs=[pl.BlockS...  5.32 us
    pallas_call x17, Pallas kernels, whole_call(): pl.pallas_call(body, in_specs=[pl.BlockSpec(memory_space=pl.ANY)] * len(a...  4.96 us
    pallas_call x1, Pallas kernels, leaf_coupling(): pl.pallas_call(coupling_kernel, in_specs=[pl.BlockSpec(memory_space=pltpu...  3.28 us
    pallas_call x1, Pallas kernels, own_terms(): pl.pallas_call(own_terms_kernel, in_specs=[pl.BlockSpec(memory_space=pltp...  2.31 us
  transfers between devices with their start and end apart: 30, of which 17 were waited for; matrix products, arithmetic and copies ran while one was open for 0% of the time, Pallas kernels for 9%

profile of v7, /device:TPU:0, one launch (start us, length us, event | category | flops | bytes accessed | tf_op | source)
XLA Modules:
  0.0 78.6 jit_solution(7810485639635600967)
XLA Ops:
  0.7 5.3 %leaf_solve.1 = (f32[8,256,128]{2,1,0:T(8,128)}, bf16[8,256,128]{2,1,0:T(8,128)(2,1)}, bf16[256,512]{1,0:T(8,128)(2,1)}) custom-call(s32[8]{0:T(128)} %parent_ref.3, f32[8,256,512]{2,1,0:T(8,128)} %rhs_ref.2, bf16[8,128,512]{2,1,0:T(8,128)(2,1)} %inv_ref.1, bf16[8,512,128]{2,1,0:T(8,128)(2,1)} %mid_ref.3), custom_call_target="tpu_custom_call" | custom-call | flops 536870912 | bytes 7864320 | tf_op jit(solution)/shard_map/leaf_solve/pallas_call | solution.py:77
  6.0 3.0 %collective-permute-start.3 = (bf16[256,512]{1,0:T(8,128)(2,1)}, bf16[256,512]{1,0:T(8,128)(2,1)S(1)}, u32[]{:S(2)}, u32[]{:S(2)}) collective-permute-start(bf16[256,512]{1,0:T(8,128)(2,1)} %get-tuple-element.49), channel_id=1, source_target_pairs={{0,1},{1,0},{2,3},{3,2},{4,5},{5,4},{6,7},{7,6},{8,9},{9,8},{10,11... | collective-permute-start | bytes 786440 | tf_op jit(solution)/shard_map/ppermute | solution.py:330
  9.0 3.7 %collective-permute-start = (bf16[128,256]{1,0:T(8,128)(2,1)S(1)}, bf16[128,256]{1,0:T(8,128)(2,1)S(1)}, u32[]{:S(2)}, u32[]{:S(2)}) collective-permute-start(bf16[128,256]{1,0:T(8,128)(2,1)S(1)} %top_share.1.refs_1_), channel_id=1, source_target_pairs={{0,6},{2,4},{4,2},{6,0},{1,7},{3,5},{5,3},{7,1},{8,14},{10,12},{12... | collective-permute-start | bytes 196616 | tf_op jit(solution)/shard_map/ppermute | solution.py:330
  14.5 2.3 %own_terms.1 = (bf16[256,512]{1,0:T(8,128)(2,1)S(1)}, f32[64,512]{1,0:T(8,128)S(1)}) custom-call(s32[8]{0:T(128)S(1)} %copy-done.11, bf16[8,256,128]{2,1,0:T(8,128)(2,1)S(1)} %copy-done.1, bf16[8,512,128]{2,1,0:T(8,128)(2,1)} %mid_ref.3, f32[1,256,512]{2,1,0:T(8,128)S(1)} %copy-done.3), custom_call_target="tpu_custom_call" | custom-call | flops 268435456 | bytes 1572864 | tf_op jit(solution)/shard_map/own_terms/pallas_call | solution.py:126
  18.8 2.6 %collective-permute-start.5 = (bf16[64,512]{1,0:T(8,128)(2,1)S(1)}, bf16[64,512]{1,0:T(8,128)(2,1)S(1)}, u32[]{:S(2)}, u32[]{:S(2)}) collective-permute-start(bf16[64,512]{1,0:T(8,128)(2,1)S(1)} %get-tuple-element.51), channel_id=1, source_target_pairs={{0,6},{2,4},{4,2},{6,0},{1,7},{3,5},{5,3},{7,1},{8,14},{10,12},{12... | collective-permute-start | bytes 196616 | tf_op jit(solution)/shard_map/ppermute | solution.py:330
  21.4 1.8 %collective-permute-start.7 = (bf16[64,512]{1,0:T(8,128)(2,1)S(1)}, bf16[64,512]{1,0:T(8,128)(2,1)S(1)}, u32[]{:S(2)}, u32[]{:S(2)}) collective-permute-start(bf16[64,512]{1,0:T(8,128)(2,1)S(1)} %get-tuple-element.53), channel_id=1, source_target_pairs={{0,2},{2,0},{4,6},{6,4},{1,3},{3,1},{5,7},{7,5},{8,10},{10,8},{12,... | collective-permute-start | bytes 196616 | tf_op jit(solution)/shard_map/ppermute | solution.py:330
  23.2 3.3 %leaf_coupling.1.refs_0_.refs_8_ = f32[3,256,512]{2,1,0:T(8,128)S(1)} custom-call(s32[3,8]{1,0:T(4,128)S(1)} %bitcast.2, bf16[8,256,128]{2,1,0:T(8,128)(2,1)S(1)} %copy-done.1, bf16[8,3,512,128]{3,2,1,0:T(8,128)(2,1)} %lower_ref.1), custom_call_target="tpu_custom_call" | custom-call | flops 805306368 | bytes 5242880 | tf_op jit(solution)/shard_map/leaf_coupling/pallas_call | solution.py:168
  27.3 2.0 %collective-permute-start.8 = (bf16[64,512]{1,0:T(8,128)(2,1)S(1)}, bf16[64,512]{1,0:T(8,128)(2,1)S(1)}, u32[]{:S(2)}, u32[]{:S(2)}) collective-permute-start(bf16[64,512]{1,0:T(8,128)(2,1)S(1)} %mid_total.1.refs_2_.refs_0_), channel_id=1, source_target_pairs={{0,6},{2,4},{4,2},{6,0},{1,7},{3,5},{5,3},{7,1},{8,14},{10,12},{12... | collective-permute-start | bytes 196616 | tf_op jit(solution)/shard_map/ppermute | solution.py:330
  29.3 2.4 %collective-permute-start.10 = (bf16[64,512]{1,0:T(8,128)(2,1)S(1)}, bf16[64,512]{1,0:T(8,128)(2,1)S(1)}, u32[]{:S(2)}, u32[]{:S(2)}) collective-permute-start(bf16[64,512]{1,0:T(8,128)(2,1)S(1)} %mid_total.1.refs_2_.refs_0_), channel_id=1, source_target_pairs={{0,2},{2,0},{4,6},{6,4},{1,3},{3,1},{5,7},{7,5},{8,10},{10,8},{12,... | collective-permute-start | bytes 196616 | tf_op jit(solution)/shard_map/ppermute | solution.py:330
  31.8 2.3 %collective-permute-done.8.refs_3_ = bf16[64,512]{1,0:T(8,128)(2,1)S(1)} collective-permute-done((bf16[64,512]{1,0:T(8,128)(2,1)S(1)}, bf16[64,512]{1,0:T(8,128)(2,1)S(1)}, u32[]{:S(2)}, u32[]{:S(2)}) %collective-permute-start.8) | collective-permute-done | bytes 65568 | tf_op jit(solution)/shard_map/ppermute | solution.py:330
  34.2 1.4 %collective-permute-done.9.refs_4_ = bf16[64,512]{1,0:T(8,128)(2,1)S(1)} collective-permute-done((bf16[64,512]{1,0:T(8,128)(2,1)S(1)}, bf16[64,512]{1,0:T(8,128)(2,1)S(1)}, u32[]{:S(2)}, u32[]{:S(2)}) %collective-permute-start.9) | collective-permute-done | bytes 65568 | tf_op jit(solution)/shard_map/ppermute | solution.py:330
  35.5 1.8 %mid_solve.1 = (f32[4,32,512]{2,1,0:T(8,128)S(1)}, bf16[4,32,512]{2,1,0:T(8,128)(2,1)S(1)}, f32[2,2,64,512]{3,2,1,0:T(8,128)S(1)}, bf16[2,2,64,512]{3,2,1,0:T(8,128)(2,1)S(1)}, f32[256,128]{1,0:T(8,128)}) custom-call(bf16[512,512]{1,0:T(8,128)(2,1)S(1)} %whole_top.1.refs_0_.refs_4_, s32[1,2]{1,0:T(1,128)S(1)} %copy-done.12, ...), custom_call_target="tpu_custom_call" | custom-call | flops 134217728 | bytes 3670024 | tf_op jit(solution)/shard_map/mid_solve/pallas_call | solution.py:342
  38.7 2.1 %collective-permute-start.19 = (bf16[2,128,128]{2,1,0:T(8,128)(2,1)S(1)}, bf16[2,128,128]{2,1,0:T(8,128)(2,1)S(1)}, u32[]{:S(2)}, u32[]{:S(2)}) collective-permute-start(bf16[2,128,128]{2,1,0:T(8,128)(2,1)S(1)} %apex_share.1.refs_1_), channel_id=1, source_target_pairs={{0,6},{2,4},{4,2},{6,0},{1,7},{3,5},{5,3},{7,1},{8,14},{10,12},{12... | collective-permute-start | bytes 196616 | tf_op jit(solution)/shard_map/ppermute | solution.py:330
  41.1 2.1 %collective-permute-start.21 = (bf16[2,128,128]{2,1,0:T(8,128)(2,1)S(1)}, bf16[2,128,128]{2,1,0:T(8,128)(2,1)S(1)}, u32[]{:S(2)}, u32[]{:S(2)}) collective-permute-start(bf16[2,128,128]{2,1,0:T(8,128)(2,1)S(1)} %apex_share.1.refs_1_), channel_id=1, source_target_pairs={{0,2},{2,0},{4,6},{6,4},{1,3},{3,1},{5,7},{7,5},{8,10},{10,8},{12,... | collective-permute-start | bytes 196616 | tf_op jit(solution)/shard_map/ppermute | solution.py:330
  43.8 1.8 %collective-permute-done.19.refs_2_ = bf16[2,128,128]{2,1,0:T(8,128)(2,1)S(1)} collective-permute-done((bf16[2,128,128]{2,1,0:T(8,128)(2,1)S(1)}, bf16[2,128,128]{2,1,0:T(8,128)(2,1)S(1)}, u32[]{:S(2)}, u32[]{:S(2)}) %collective-permute-start.19) | collective-permute-done | bytes 65568 | tf_op jit(solution)/shard_map/ppermute | solution.py:330
  45.6 2.0 %collective-permute-done.20.refs_3_ = bf16[2,128,128]{2,1,0:T(8,128)(2,1)S(1)} collective-permute-done((bf16[2,128,128]{2,1,0:T(8,128)(2,1)S(1)}, bf16[2,128,128]{2,1,0:T(8,128)(2,1)S(1)}, u32[]{:S(2)}, u32[]{:S(2)}) %collective-permute-start.20) | collective-permute-done | bytes 65568 | tf_op jit(solution)/shard_map/ppermute | solution.py:330
  48.5 2.1 %collective-permute-start.13 = (bf16[128,128]{1,0:T(8,128)(2,1)S(1)}, bf16[128,128]{1,0:T(8,128)(2,1)S(1)}, u32[]{:S(2)}, u32[]{:S(2)}) collective-permute-start(bf16[128,128]{1,0:T(8,128)(2,1)S(1)} %get-tuple-element.61), channel_id=1, source_target_pairs={{0,6},{2,4},{4,2},{6,0},{1,7},{3,5},{5,3},{7,1},{8,14},{10,12},{12... | collective-permute-start | bytes 98312 | tf_op jit(solution)/shard_map/ppermute | solution.py:330
  50.6 2.3 %collective-permute-start.15 = (bf16[128,128]{1,0:T(8,128)(2,1)S(1)}, bf16[128,128]{1,0:T(8,128)(2,1)S(1)}, u32[]{:S(2)}, u32[]{:S(2)}) collective-permute-start(bf16[128,128]{1,0:T(8,128)(2,1)S(1)} %get-tuple-element.63), channel_id=1, source_target_pairs={{0,2},{2,0},{4,6},{6,4},{1,3},{3,1},{5,7},{7,5},{8,10},{10,8},{12,... | collective-permute-start | bytes 98312 | tf_op jit(solution)/shard_map/ppermute | solution.py:330
  55.4 1.5 %collective-permute-done.22.refs_1_ = bf16[4,2,128,128]{3,2,1,0:T(8,128)(2,1)S(1)} collective-permute-done((bf16[4,2,128,128]{3,2,1,0:T(8,128)(2,1)S(1)}, bf16[4,2,128,128]{3,2,1,0:T(8,128)(2,1)S(1)}, u32[]{:S(2)}, u32[]{:S(2)}) %collective-permute-start.22) | collective-permute-done | bytes 262176 | tf_op jit(solution)/shard_map/ppermute | solution.py:330
  60.9 1.6 %collective-permute-start.25 = (bf16[2,32,512]{2,1,0:T(8,128)(2,1)S(1)}, bf16[2,32,512]{2,1,0:T(8,128)(2,1)S(1)}, u32[]{:S(2)}, u32[]{:S(2)}) collective-permute-start(bf16[2,32,512]{2,1,0:T(8,128)(2,1)S(1)} %get-tuple-element.75), channel_id=1, source_target_pairs={{0,16},{8,24},{16,0},{24,8},{1,17},{9,25},{17,1},{25,9},{2,18},{10... | collective-permute-start | bytes 196616 | tf_op jit(solution)/shard_map/ppermute | solution.py:330
  63.3 3.1 %collective-permute-done.17.refs_0_.refs_2_ = bf16[4,32,128]{2,1,0:T(8,128)(2,1)S(1)} collective-permute-done((bf16[4,32,128]{2,1,0:T(8,128)(2,1)S(1)}, bf16[4,32,128]{2,1,0:T(8,128)(2,1)S(1)}, u32[]{:S(2)}, u32[]{:S(2)}) %collective-permute-start.17) | collective-permute-done | bytes 32800 | tf_op jit(solution)/shard_map/ppermute | solution.py:330
  66.5 2.1 %collective-permute-start.26 = (bf16[32,768]{1,0:T(8,128)(2,1)S(1)}, bf16[32,768]{1,0:T(8,128)(2,1)S(1)}, u32[]{:S(2)}, u32[]{:S(2)}) collective-permute-start(bf16[32,768]{1,0:T(8,128)(2,1)S(1)} %get-tuple-element.81), channel_id=1, source_target_pairs={{0,6},{2,4},{4,2},{6,0},{1,7},{3,5},{5,3},{7,1},{8,14},{10,12},{12... | collective-permute-start | bytes 147464 | tf_op jit(solution)/shard_map/ppermute | solution.py:330
  68.6 2.4 %collective-permute-start.28 = (bf16[32,768]{1,0:T(8,128)(2,1)S(1)}, bf16[32,768]{1,0:T(8,128)(2,1)S(1)}, u32[]{:S(2)}, u32[]{:S(2)}) collective-permute-start(bf16[32,768]{1,0:T(8,128)(2,1)S(1)} %get-tuple-element.83), channel_id=1, source_target_pairs={{0,2},{2,0},{4,6},{6,4},{1,3},{3,1},{5,7},{7,5},{8,10},{10,8},{12,... | collective-permute-start | bytes 147464 | tf_op jit(solution)/shard_map/ppermute | solution.py:330
  75.0 3.0 %collective-permute-done.29.refs_1_ = bf16[3,32,128]{2,1,0:T(8,128)(2,1)S(1)} collective-permute-done((bf16[3,32,128]{2,1,0:T(8,128)(2,1)S(1)}, bf16[3,32,128]{2,1,0:T(8,128)(2,1)S(1)}, u32[]{:S(2)}, u32[]{:S(2)}) %collective-permute-start.29) | collective-permute-done | bytes 24608 | tf_op jit(solution)/shard_map/ppermute | solution.py:330
  (82 shorter events, 19.8 us)
Async XLA Ops:
  6.0 12.1 %collective-permute-start.3 = (bf16[256,512]{1,0:T(8,128)(2,1)}, bf16[256,512]{1,0:T(8,128)(2,1)S(1)}, u32[]{:S(2)}, u32[]{:S(2)}) collective-permute-start(bf16[256,512]{1,0:T(8,128)(2,1)} %get-tuple-element.49), channel_id=1, source_target_pairs={{0,1},{1,0},{2,3},{3,2},{4,5},{5,4},{6,7},{7,6},{8,9},{9,8},{10,11... | collective-permute-start | bytes 786440 | tf_op jit(solution)/shard_map/ppermute | solution.py:330
  9.0 7.8 %collective-permute-start = (bf16[128,256]{1,0:T(8,128)(2,1)S(1)}, bf16[128,256]{1,0:T(8,128)(2,1)S(1)}, u32[]{:S(2)}, u32[]{:S(2)}) collective-permute-start(bf16[128,256]{1,0:T(8,128)(2,1)S(1)} %top_share.1.refs_1_), channel_id=1, source_target_pairs={{0,6},{2,4},{4,2},{6,0},{1,7},{3,5},{5,3},{7,1},{8,14},{10,12},{12... | collective-permute-start | bytes 196616 | tf_op jit(solution)/shard_map/ppermute | solution.py:330
  12.7 5.4 %collective-permute-start.1 = (bf16[128,256]{1,0:T(8,128)(2,1)S(1)}, bf16[128,256]{1,0:T(8,128)(2,1)S(1)}, u32[]{:S(2)}, u32[]{:S(2)}) collective-permute-start(bf16[128,256]{1,0:T(8,128)(2,1)S(1)} %top_share.1.refs_1_), channel_id=1, source_target_pairs={{0,4},{2,6},{4,0},{6,2},{1,5},{3,7},{5,1},{7,3},{8,12},{10,14},{12... | collective-permute-start | bytes 196616 | tf_op jit(solution)/shard_map/ppermute | solution.py:330
  12.7 5.4 %collective-permute-start.2 = (bf16[128,256]{1,0:T(8,128)(2,1)S(1)}, bf16[128,256]{1,0:T(8,128)(2,1)S(1)}, u32[]{:S(2)}, u32[]{:S(2)}) collective-permute-start(bf16[128,256]{1,0:T(8,128)(2,1)S(1)} %top_share.1.refs_1_), channel_id=1, source_target_pairs={{0,2},{2,0},{4,6},{6,4},{1,3},{3,1},{5,7},{7,5},{8,10},{10,8},{12,... | collective-permute-start | bytes 196616 | tf_op jit(solution)/shard_map/ppermute | solution.py:330
  18.3 13.5 %collective-permute-start.4 = (bf16[512,256]{1,0:T(8,128)(2,1)S(1)}, bf16[512,256]{1,0:T(8,128)(2,1)S(1)}, u32[]{:S(2)}, u32[]{:S(2)}) collective-permute-start(bf16[512,256]{1,0:T(8,128)(2,1)S(1)} %half_top.1.refs_0_), channel_id=1, source_target_pairs={{0,1},{1,0},{2,3},{3,2},{4,5},{5,4},{6,7},{7,6},{8,9},{9,8},{10,11... | collective-permute-start | bytes 786440 | tf_op jit(solution)/shard_map/ppermute | solution.py:330
  18.8 7.7 %collective-permute-start.5 = (bf16[64,512]{1,0:T(8,128)(2,1)S(1)}, bf16[64,512]{1,0:T(8,128)(2,1)S(1)}, u32[]{:S(2)}, u32[]{:S(2)}) collective-permute-start(bf16[64,512]{1,0:T(8,128)(2,1)S(1)} %get-tuple-element.51), channel_id=1, source_target_pairs={{0,6},{2,4},{4,2},{6,0},{1,7},{3,5},{5,3},{7,1},{8,14},{10,12},{12... | collective-permute-start | bytes 196616 | tf_op jit(solution)/shard_map/ppermute | solution.py:330
  21.4 5.8 %collective-permute-start.6 = (bf16[64,512]{1,0:T(8,128)(2,1)S(1)}, bf16[64,512]{1,0:T(8,128)(2,1)S(1)}, u32[]{:S(2)}, u32[]{:S(2)}) collective-permute-start(bf16[64,512]{1,0:T(8,128)(2,1)S(1)} %get-tuple-element.52), channel_id=1, source_target_pairs={{0,4},{2,6},{4,0},{6,2},{1,5},{3,7},{5,1},{7,3},{8,12},{10,14},{12... | collective-permute-start | bytes 196616 | tf_op jit(solution)/shard_map/ppermute | solution.py:330
  21.4 5.8 %collective-permute-start.7 = (bf16[64,512]{1,0:T(8,128)(2,1)S(1)}, bf16[64,512]{1,0:T(8,128)(2,1)S(1)}, u32[]{:S(2)}, u32[]{:S(2)}) collective-permute-start(bf16[64,512]{1,0:T(8,128)(2,1)S(1)} %get-tuple-element.53), channel_id=1, source_target_pairs={{0,2},{2,0},{4,6},{6,4},{1,3},{3,1},{5,7},{7,5},{8,10},{10,8},{12,... | collective-permute-start | bytes 196616 | tf_op jit(solution)/shard_map/ppermute | solution.py:330
  27.3 6.9 %collective-permute-start.8 = (bf16[64,512]{1,0:T(8,128)(2,1)S(1)}, bf16[64,512]{1,0:T(8,128)(2,1)S(1)}, u32[]{:S(2)}, u32[]{:S(2)}) collective-permute-start(bf16[64,512]{1,0:T(8,128)(2,1)S(1)} %mid_total.1.refs_2_.refs_0_), channel_id=1, source_target_pairs={{0,6},{2,4},{4,2},{6,0},{1,7},{3,5},{5,3},{7,1},{8,14},{10,12},{12... | collective-permute-start | bytes 196616 | tf_op jit(solution)/shard_map/ppermute | solution.py:330
  29.3 6.2 %collective-permute-start.9 = (bf16[64,512]{1,0:T(8,128)(2,1)S(1)}, bf16[64,512]{1,0:T(8,128)(2,1)S(1)}, u32[]{:S(2)}, u32[]{:S(2)}) collective-permute-start(bf16[64,512]{1,0:T(8,128)(2,1)S(1)} %mid_total.1.refs_2_.refs_0_), channel_id=1, source_target_pairs={{0,4},{2,6},{4,0},{6,2},{1,5},{3,7},{5,1},{7,3},{8,12},{10,14},{12... | collective-permute-start | bytes 196616 | tf_op jit(solution)/shard_map/ppermute | solution.py:330
  29.3 6.2 %collective-permute-start.10 = (bf16[64,512]{1,0:T(8,128)(2,1)S(1)}, bf16[64,512]{1,0:T(8,128)(2,1)S(1)}, u32[]{:S(2)}, u32[]{:S(2)}) collective-permute-start(bf16[64,512]{1,0:T(8,128)(2,1)S(1)} %mid_total.1.refs_2_.refs_0_), channel_id=1, source_target_pairs={{0,2},{2,0},{4,6},{6,4},{1,3},{3,1},{5,7},{7,5},{8,10},{10,8},{12,... | collective-permute-start | bytes 196616 | tf_op jit(solution)/shard_map/ppermute | solution.py:330
  37.4 6.0 %collective-permute-start.11 = (bf16[2,2,64,512]{3,2,1,0:T(8,128)(2,1)S(1)}, bf16[2,2,64,512]{3,2,1,0:T(8,128)(2,1)S(1)}, u32[]{:S(2)}, u32[]{:S(2)}) collective-permute-start(bf16[2,2,64,512]{3,2,1,0:T(8,128)(2,1)S(1)} %get-tuple-element.56), channel_id=1, source_target_pairs={{0,8},{8,0},{16,24},{24,16},{1,9},{9,1},{17,25},{25,17},{2,10},{10... | collective-permute-start | bytes 786440 | tf_op jit(solution)/shard_map/ppermute | solution.py:330
  37.5 5.9 %collective-permute-start.12 = (bf16[4,32,512]{2,1,0:T(8,128)(2,1)S(1)}, bf16[4,32,512]{2,1,0:T(8,128)(2,1)S(1)}, u32[]{:S(2)}, u32[]{:S(2)}) collective-permute-start(bf16[4,32,512]{2,1,0:T(8,128)(2,1)S(1)} %get-tuple-element.59), channel_id=1, source_target_pairs={{0,1},{1,0},{2,3},{3,2},{4,5},{5,4},{6,7},{7,6},{8,9},{9,8},{10,11... | collective-permute-start | bytes 393224 | tf_op jit(solution)/shard_map/ppermute | solution.py:330
  38.7 6.8 %collective-permute-start.19 = (bf16[2,128,128]{2,1,0:T(8,128)(2,1)S(1)}, bf16[2,128,128]{2,1,0:T(8,128)(2,1)S(1)}, u32[]{:S(2)}, u32[]{:S(2)}) collective-permute-start(bf16[2,128,128]{2,1,0:T(8,128)(2,1)S(1)} %apex_share.1.refs_1_), channel_id=1, source_target_pairs={{0,6},{2,4},{4,2},{6,0},{1,7},{3,5},{5,3},{7,1},{8,14},{10,12},{12... | collective-permute-start | bytes 196616 | tf_op jit(solution)/shard_map/ppermute | solution.py:330
  40.8 6.7 %collective-permute-start.20 = (bf16[2,128,128]{2,1,0:T(8,128)(2,1)S(1)}, bf16[2,128,128]{2,1,0:T(8,128)(2,1)S(1)}, u32[]{:S(2)}, u32[]{:S(2)}) collective-permute-start(bf16[2,128,128]{2,1,0:T(8,128)(2,1)S(1)} %apex_share.1.refs_1_), channel_id=1, source_target_pairs={{0,4},{2,6},{4,0},{6,2},{1,5},{3,7},{5,1},{7,3},{8,12},{10,14},{12... | collective-permute-start | bytes 196616 | tf_op jit(solution)/shard_map/ppermute | solution.py:330
  41.1 6.5 %collective-permute-start.21 = (bf16[2,128,128]{2,1,0:T(8,128)(2,1)S(1)}, bf16[2,128,128]{2,1,0:T(8,128)(2,1)S(1)}, u32[]{:S(2)}, u32[]{:S(2)}) collective-permute-start(bf16[2,128,128]{2,1,0:T(8,128)(2,1)S(1)} %apex_share.1.refs_1_), channel_id=1, source_target_pairs={{0,2},{2,0},{4,6},{6,4},{1,3},{3,1},{5,7},{7,5},{8,10},{10,8},{12,... | collective-permute-start | bytes 196616 | tf_op jit(solution)/shard_map/ppermute | solution.py:330
  47.6 9.2 %collective-permute-start.22 = (bf16[4,2,128,128]{3,2,1,0:T(8,128)(2,1)S(1)}, bf16[4,2,128,128]{3,2,1,0:T(8,128)(2,1)S(1)}, u32[]{:S(2)}, u32[]{:S(2)}) collective-permute-start(bf16[4,2,128,128]{3,2,1,0:T(8,128)(2,1)S(1)} %front_share.1.refs_0_), channel_id=1, source_target_pairs={{0,1},{1,0},{2,3},{3,2},{4,5},{5,4},{6,7},{7,6},{8,9},{9,8},{10,11... | collective-permute-start | bytes 786440 | tf_op jit(solution)/shard_map/ppermute | solution.py:330
  48.5 5.7 %collective-permute-start.13 = (bf16[128,128]{1,0:T(8,128)(2,1)S(1)}, bf16[128,128]{1,0:T(8,128)(2,1)S(1)}, u32[]{:S(2)}, u32[]{:S(2)}) collective-permute-start(bf16[128,128]{1,0:T(8,128)(2,1)S(1)} %get-tuple-element.61), channel_id=1, source_target_pairs={{0,6},{2,4},{4,2},{6,0},{1,7},{3,5},{5,3},{7,1},{8,14},{10,12},{12... | collective-permute-start | bytes 98312 | tf_op jit(solution)/shard_map/ppermute | solution.py:330
  50.6 4.8 %collective-permute-start.14 = (bf16[128,128]{1,0:T(8,128)(2,1)S(1)}, bf16[128,128]{1,0:T(8,128)(2,1)S(1)}, u32[]{:S(2)}, u32[]{:S(2)}) collective-permute-start(bf16[128,128]{1,0:T(8,128)(2,1)S(1)} %get-tuple-element.62), channel_id=1, source_target_pairs={{0,4},{2,6},{4,0},{6,2},{1,5},{3,7},{5,1},{7,3},{8,12},{10,14},{12... | collective-permute-start | bytes 98312 | tf_op jit(solution)/shard_map/ppermute | solution.py:330
  52.9 5.8 %collective-permute-start.16 = (bf16[2,2,32,512]{3,2,1,0:T(8,128)(2,1)S(1)}, bf16[2,2,32,512]{3,2,1,0:T(8,128)(2,1)S(1)}, u32[]{:S(2)}, u32[]{:S(2)}) collective-permute-start(bf16[2,2,32,512]{3,2,1,0:T(8,128)(2,1)S(1)} %get-tuple-element.57.refs_0_), channel_id=1, source_target_pairs={{0,1},{1,0},{2,3},{3,2},{4,5},{5,4},{6,7},{7,6},{8,9},{9,8},{10,11... | collective-permute-start | bytes 393224 | tf_op jit(solution)/shard_map/ppermute | solution.py:330
  60.9 5.5 %collective-permute-start.25 = (bf16[2,32,512]{2,1,0:T(8,128)(2,1)S(1)}, bf16[2,32,512]{2,1,0:T(8,128)(2,1)S(1)}, u32[]{:S(2)}, u32[]{:S(2)}) collective-permute-start(bf16[2,32,512]{2,1,0:T(8,128)(2,1)S(1)} %get-tuple-element.75), channel_id=1, source_target_pairs={{0,16},{8,24},{16,0},{24,8},{1,17},{9,25},{17,1},{25,9},{2,18},{10... | collective-permute-start | bytes 196616 | tf_op jit(solution)/shard_map/ppermute | solution.py:330
  66.5 6.4 %collective-permute-start.26 = (bf16[32,768]{1,0:T(8,128)(2,1)S(1)}, bf16[32,768]{1,0:T(8,128)(2,1)S(1)}, u32[]{:S(2)}, u32[]{:S(2)}) collective-permute-start(bf16[32,768]{1,0:T(8,128)(2,1)S(1)} %get-tuple-element.81), channel_id=1, source_target_pairs={{0,6},{2,4},{4,2},{6,0},{1,7},{3,5},{5,3},{7,1},{8,14},{10,12},{12... | collective-permute-start | bytes 147464 | tf_op jit(solution)/shard_map/ppermute | solution.py:330
  68.6 5.4 %collective-permute-start.27 = (bf16[32,768]{1,0:T(8,128)(2,1)S(1)}, bf16[32,768]{1,0:T(8,128)(2,1)S(1)}, u32[]{:S(2)}, u32[]{:S(2)}) collective-permute-start(bf16[32,768]{1,0:T(8,128)(2,1)S(1)} %get-tuple-element.82), channel_id=1, source_target_pairs={{0,4},{2,6},{4,0},{6,2},{1,5},{3,7},{5,1},{7,3},{8,12},{10,14},{12... | collective-permute-start | bytes 147464 | tf_op jit(solution)/shard_map/ppermute | solution.py:330
  68.6 5.4 %collective-permute-start.28 = (bf16[32,768]{1,0:T(8,128)(2,1)S(1)}, bf16[32,768]{1,0:T(8,128)(2,1)S(1)}, u32[]{:S(2)}, u32[]{:S(2)}) collective-permute-start(bf16[32,768]{1,0:T(8,128)(2,1)S(1)} %get-tuple-element.83), channel_id=1, source_target_pairs={{0,2},{2,0},{4,6},{6,4},{1,3},{3,1},{5,7},{7,5},{8,10},{10,8},{12,... | collective-permute-start | bytes 147464 | tf_op jit(solution)/shard_map/ppermute | solution.py:330
  (19 other events, 198.2 us)

commit v8 on v7

--- a/solution.py
+++ b/solution.py
@@ -42,8 +42,8 @@
         rhs_copies[i].start()
     mid_copy.start()
     out_copies = []
-    for start in range(0, leaves, 2):
-        group = range(start, min(start + 2, leaves))
+    for start in range(0, leaves, 4):
+        group = range(start, min(start + 4, leaves))
         for i in group:
             inv_copies[i].wait()
             rhs_copies[i].wait()

time: 78.9 us -> 79.1 us (level)
  no operation moved by 1% of the time
where the time goes in v8:
time: 79.1 us; the launch traced here: 78.9 us
  starting transfers between devices  37.4 us (47%)
  waiting for transfers between devices  23.4 us (30%)
  Pallas kernels  16.1 us (20%)
  local copies, waits for them, and re-layouts  1.1 us (1%)
  between operations  0.91 us (1%)
    ppermute x30, starting transfers between devices, partners(): arrived.append(lax.ppermute(item, axes, route))  37.4 us
    ppermute x30, waiting for transfers between devices, partners(): arrived.append(lax.ppermute(item, axes, route))  23.4 us
    pallas_call x1, Pallas kernels, leaf_solve(): pl.pallas_call(functools.partial(leaf_kernel, slots), in_specs=[pl.BlockS...  5.59 us
    pallas_call x17, Pallas kernels, whole_call(): pl.pallas_call(body, in_specs=[pl.BlockSpec(memory_space=pl.ANY)] * len(a...  4.95 us
    pallas_call x1, Pallas kernels, leaf_coupling(): pl.pallas_call(coupling_kernel, in_specs=[pl.BlockSpec(memory_space=pltpu...  3.27 us
    pallas_call x1, Pallas kernels, own_terms(): pl.pallas_call(own_terms_kernel, in_specs=[pl.BlockSpec(memory_space=pltp...  2.31 us
  transfers between devices with their start and end apart: 30, of which 17 were waited for; matrix products, arithmetic and copies ran while one was open for 0% of the time, Pallas kernels for 9%

profile of v8, /device:TPU:0, one launch (start us, length us, event | category | flops | bytes accessed | tf_op | source)
XLA Modules:
  0.0 78.9 jit_solution(3548611797661219656)
XLA Ops:
  0.7 5.6 %leaf_solve.1 = (f32[8,256,128]{2,1,0:T(8,128)}, bf16[8,256,128]{2,1,0:T(8,128)(2,1)}, bf16[256,512]{1,0:T(8,128)(2,1)}) custom-call(s32[8]{0:T(128)} %parent_ref.3, f32[8,256,512]{2,1,0:T(8,128)} %rhs_ref.2, bf16[8,128,512]{2,1,0:T(8,128)(2,1)} %inv_ref.1, bf16[8,512,128]{2,1,0:T(8,128)(2,1)} %mid_ref.3), custom_call_target="tpu_custom_call" | custom-call | flops 536870912 | bytes 7864320 | tf_op jit(solution)/shard_map/leaf_solve/pallas_call | solution.py:77
  6.3 3.0 %collective-permute-start.3 = (bf16[256,512]{1,0:T(8,128)(2,1)}, bf16[256,512]{1,0:T(8,128)(2,1)S(1)}, u32[]{:S(2)}, u32[]{:S(2)}) collective-permute-start(bf16[256,512]{1,0:T(8,128)(2,1)} %get-tuple-element.49), channel_id=1, source_target_pairs={{0,1},{1,0},{2,3},{3,2},{4,5},{5,4},{6,7},{7,6},{8,9},{9,8},{10,11... | collective-permute-start | bytes 786440 | tf_op jit(solution)/shard_map/ppermute | solution.py:330
  9.3 3.7 %collective-permute-start = (bf16[128,256]{1,0:T(8,128)(2,1)S(1)}, bf16[128,256]{1,0:T(8,128)(2,1)S(1)}, u32[]{:S(2)}, u32[]{:S(2)}) collective-permute-start(bf16[128,256]{1,0:T(8,128)(2,1)S(1)} %top_share.1.refs_1_), channel_id=1, source_target_pairs={{0,6},{2,4},{4,2},{6,0},{1,7},{3,5},{5,3},{7,1},{8,14},{10,12},{12... | collective-permute-start | bytes 196616 | tf_op jit(solution)/shard_map/ppermute | solution.py:330
  14.8 2.3 %own_terms.1 = (bf16[256,512]{1,0:T(8,128)(2,1)S(1)}, f32[64,512]{1,0:T(8,128)S(1)}) custom-call(s32[8]{0:T(128)S(1)} %copy-done.11, bf16[8,256,128]{2,1,0:T(8,128)(2,1)S(1)} %copy-done.1, bf16[8,512,128]{2,1,0:T(8,128)(2,1)} %mid_ref.3, f32[1,256,512]{2,1,0:T(8,128)S(1)} %copy-done.3), custom_call_target="tpu_custom_call" | custom-call | flops 268435456 | bytes 1572864 | tf_op jit(solution)/shard_map/own_terms/pallas_call | solution.py:126
  19.0 2.7 %collective-permute-start.5 = (bf16[64,512]{1,0:T(8,128)(2,1)S(1)}, bf16[64,512]{1,0:T(8,128)(2,1)S(1)}, u32[]{:S(2)}, u32[]{:S(2)}) collective-permute-start(bf16[64,512]{1,0:T(8,128)(2,1)S(1)} %get-tuple-element.51), channel_id=1, source_target_pairs={{0,6},{2,4},{4,2},{6,0},{1,7},{3,5},{5,3},{7,1},{8,14},{10,12},{12... | collective-permute-start | bytes 196616 | tf_op jit(solution)/shard_map/ppermute | solution.py:330
  21.7 1.7 %collective-permute-start.7 = (bf16[64,512]{1,0:T(8,128)(2,1)S(1)}, bf16[64,512]{1,0:T(8,128)(2,1)S(1)}, u32[]{:S(2)}, u32[]{:S(2)}) collective-permute-start(bf16[64,512]{1,0:T(8,128)(2,1)S(1)} %get-tuple-element.53), channel_id=1, source_target_pairs={{0,2},{2,0},{4,6},{6,4},{1,3},{3,1},{5,7},{7,5},{8,10},{10,8},{12,... | collective-permute-start | bytes 196616 | tf_op jit(solution)/shard_map/ppermute | solution.py:330
  23.4 3.3 %leaf_coupling.1.refs_0_.refs_8_ = f32[3,256,512]{2,1,0:T(8,128)S(1)} custom-call(s32[3,8]{1,0:T(4,128)S(1)} %bitcast.2, bf16[8,256,128]{2,1,0:T(8,128)(2,1)S(1)} %copy-done.1, bf16[8,3,512,128]{3,2,1,0:T(8,128)(2,1)} %lower_ref.1), custom_call_target="tpu_custom_call" | custom-call | flops 805306368 | bytes 5242880 | tf_op jit(solution)/shard_map/leaf_coupling/pallas_call | solution.py:168
  27.6 2.0 %collective-permute-start.8 = (bf16[64,512]{1,0:T(8,128)(2,1)S(1)}, bf16[64,512]{1,0:T(8,128)(2,1)S(1)}, u32[]{:S(2)}, u32[]{:S(2)}) collective-permute-start(bf16[64,512]{1,0:T(8,128)(2,1)S(1)} %mid_total.1.refs_2_.refs_0_), channel_id=1, source_target_pairs={{0,6},{2,4},{4,2},{6,0},{1,7},{3,5},{5,3},{7,1},{8,14},{10,12},{12... | collective-permute-start | bytes 196616 | tf_op jit(solution)/shard_map/ppermute | solution.py:330
  29.6 2.5 %collective-permute-start.10 = (bf16[64,512]{1,0:T(8,128)(2,1)S(1)}, bf16[64,512]{1,0:T(8,128)(2,1)S(1)}, u32[]{:S(2)}, u32[]{:S(2)}) collective-permute-start(bf16[64,512]{1,0:T(8,128)(2,1)S(1)} %mid_total.1.refs_2_.refs_0_), channel_id=1, source_target_pairs={{0,2},{2,0},{4,6},{6,4},{1,3},{3,1},{5,7},{7,5},{8,10},{10,8},{12,... | collective-permute-start | bytes 196616 | tf_op jit(solution)/shard_map/ppermute | solution.py:330
  32.1 2.3 %collective-permute-done.8.refs_3_ = bf16[64,512]{1,0:T(8,128)(2,1)S(1)} collective-permute-done((bf16[64,512]{1,0:T(8,128)(2,1)S(1)}, bf16[64,512]{1,0:T(8,128)(2,1)S(1)}, u32[]{:S(2)}, u32[]{:S(2)}) %collective-permute-start.8) | collective-permute-done | bytes 65568 | tf_op jit(solution)/shard_map/ppermute | solution.py:330
  35.7 1.8 %mid_solve.1 = (f32[4,32,512]{2,1,0:T(8,128)S(1)}, bf16[4,32,512]{2,1,0:T(8,128)(2,1)S(1)}, f32[2,2,64,512]{3,2,1,0:T(8,128)S(1)}, bf16[2,2,64,512]{3,2,1,0:T(8,128)(2,1)S(1)}, f32[256,128]{1,0:T(8,128)}) custom-call(bf16[512,512]{1,0:T(8,128)(2,1)S(1)} %whole_top.1.refs_0_.refs_4_, s32[1,2]{1,0:T(1,128)S(1)} %copy-done.12, ...), custom_call_target="tpu_custom_call" | custom-call | flops 134217728 | bytes 3670024 | tf_op jit(solution)/shard_map/mid_solve/pallas_call | solution.py:342
  37.6 1.4 %collective-permute-start.12 = (bf16[4,32,512]{2,1,0:T(8,128)(2,1)S(1)}, bf16[4,32,512]{2,1,0:T(8,128)(2,1)S(1)}, u32[]{:S(2)}, u32[]{:S(2)}) collective-permute-start(bf16[4,32,512]{2,1,0:T(8,128)(2,1)S(1)} %get-tuple-element.59), channel_id=1, source_target_pairs={{0,1},{1,0},{2,3},{3,2},{4,5},{5,4},{6,7},{7,6},{8,9},{9,8},{10,11... | collective-permute-start | bytes 393224 | tf_op jit(solution)/shard_map/ppermute | solution.py:330
  39.0 2.1 %collective-permute-start.19 = (bf16[2,128,128]{2,1,0:T(8,128)(2,1)S(1)}, bf16[2,128,128]{2,1,0:T(8,128)(2,1)S(1)}, u32[]{:S(2)}, u32[]{:S(2)}) collective-permute-start(bf16[2,128,128]{2,1,0:T(8,128)(2,1)S(1)} %apex_share.1.refs_1_), channel_id=1, source_target_pairs={{0,6},{2,4},{4,2},{6,0},{1,7},{3,5},{5,3},{7,1},{8,14},{10,12},{12... | collective-permute-start | bytes 196616 | tf_op jit(solution)/shard_map/ppermute | solution.py:330
  41.3 2.1 %collective-permute-start.21 = (bf16[2,128,128]{2,1,0:T(8,128)(2,1)S(1)}, bf16[2,128,128]{2,1,0:T(8,128)(2,1)S(1)}, u32[]{:S(2)}, u32[]{:S(2)}) collective-permute-start(bf16[2,128,128]{2,1,0:T(8,128)(2,1)S(1)} %apex_share.1.refs_1_), channel_id=1, source_target_pairs={{0,2},{2,0},{4,6},{6,4},{1,3},{3,1},{5,7},{7,5},{8,10},{10,8},{12,... | collective-permute-start | bytes 196616 | tf_op jit(solution)/shard_map/ppermute | solution.py:330
  44.0 1.9 %collective-permute-done.19.refs_2_ = bf16[2,128,128]{2,1,0:T(8,128)(2,1)S(1)} collective-permute-done((bf16[2,128,128]{2,1,0:T(8,128)(2,1)S(1)}, bf16[2,128,128]{2,1,0:T(8,128)(2,1)S(1)}, u32[]{:S(2)}, u32[]{:S(2)}) %collective-permute-start.19) | collective-permute-done | bytes 65568 | tf_op jit(solution)/shard_map/ppermute | solution.py:330
  45.9 2.0 %collective-permute-done.20.refs_3_ = bf16[2,128,128]{2,1,0:T(8,128)(2,1)S(1)} collective-permute-done((bf16[2,128,128]{2,1,0:T(8,128)(2,1)S(1)}, bf16[2,128,128]{2,1,0:T(8,128)(2,1)S(1)}, u32[]{:S(2)}, u32[]{:S(2)}) %collective-permute-start.20) | collective-permute-done | bytes 65568 | tf_op jit(solution)/shard_map/ppermute | solution.py:330
  48.7 2.2 %collective-permute-start.13 = (bf16[128,128]{1,0:T(8,128)(2,1)S(1)}, bf16[128,128]{1,0:T(8,128)(2,1)S(1)}, u32[]{:S(2)}, u32[]{:S(2)}) collective-permute-start(bf16[128,128]{1,0:T(8,128)(2,1)S(1)} %get-tuple-element.61), channel_id=1, source_target_pairs={{0,6},{2,4},{4,2},{6,0},{1,7},{3,5},{5,3},{7,1},{8,14},{10,12},{12... | collective-permute-start | bytes 98312 | tf_op jit(solution)/shard_map/ppermute | solution.py:330
  50.8 2.2 %collective-permute-start.15 = (bf16[128,128]{1,0:T(8,128)(2,1)S(1)}, bf16[128,128]{1,0:T(8,128)(2,1)S(1)}, u32[]{:S(2)}, u32[]{:S(2)}) collective-permute-start(bf16[128,128]{1,0:T(8,128)(2,1)S(1)} %get-tuple-element.63), channel_id=1, source_target_pairs={{0,2},{2,0},{4,6},{6,4},{1,3},{3,1},{5,7},{7,5},{8,10},{10,8},{12,... | collective-permute-start | bytes 98312 | tf_op jit(solution)/shard_map/ppermute | solution.py:330
  55.6 1.5 %collective-permute-done.22.refs_1_ = bf16[4,2,128,128]{3,2,1,0:T(8,128)(2,1)S(1)} collective-permute-done((bf16[4,2,128,128]{3,2,1,0:T(8,128)(2,1)S(1)}, bf16[4,2,128,128]{3,2,1,0:T(8,128)(2,1)S(1)}, u32[]{:S(2)}, u32[]{:S(2)}) %collective-permute-start.22) | collective-permute-done | bytes 262176 | tf_op jit(solution)/shard_map/ppermute | solution.py:330
  61.2 1.6 %collective-permute-start.25 = (bf16[2,32,512]{2,1,0:T(8,128)(2,1)S(1)}, bf16[2,32,512]{2,1,0:T(8,128)(2,1)S(1)}, u32[]{:S(2)}, u32[]{:S(2)}) collective-permute-start(bf16[2,32,512]{2,1,0:T(8,128)(2,1)S(1)} %get-tuple-element.75), channel_id=1, source_target_pairs={{0,16},{8,24},{16,0},{24,8},{1,17},{9,25},{17,1},{25,9},{2,18},{10... | collective-permute-start | bytes 196616 | tf_op jit(solution)/shard_map/ppermute | solution.py:330
  63.6 3.1 %collective-permute-done.17.refs_0_.refs_2_ = bf16[4,32,128]{2,1,0:T(8,128)(2,1)S(1)} collective-permute-done((bf16[4,32,128]{2,1,0:T(8,128)(2,1)S(1)}, bf16[4,32,128]{2,1,0:T(8,128)(2,1)S(1)}, u32[]{:S(2)}, u32[]{:S(2)}) %collective-permute-start.17) | collective-permute-done | bytes 32800 | tf_op jit(solution)/shard_map/ppermute | solution.py:330
  66.7 2.1 %collective-permute-start.26 = (bf16[32,768]{1,0:T(8,128)(2,1)S(1)}, bf16[32,768]{1,0:T(8,128)(2,1)S(1)}, u32[]{:S(2)}, u32[]{:S(2)}) collective-permute-start(bf16[32,768]{1,0:T(8,128)(2,1)S(1)} %get-tuple-element.81), channel_id=1, source_target_pairs={{0,6},{2,4},{4,2},{6,0},{1,7},{3,5},{5,3},{7,1},{8,14},{10,12},{12... | collective-permute-start | bytes 147464 | tf_op jit(solution)/shard_map/ppermute | solution.py:330
  68.8 2.4 %collective-permute-start.28 = (bf16[32,768]{1,0:T(8,128)(2,1)S(1)}, bf16[32,768]{1,0:T(8,128)(2,1)S(1)}, u32[]{:S(2)}, u32[]{:S(2)}) collective-permute-start(bf16[32,768]{1,0:T(8,128)(2,1)S(1)} %get-tuple-element.83), channel_id=1, source_target_pairs={{0,2},{2,0},{4,6},{6,4},{1,3},{3,1},{5,7},{7,5},{8,10},{10,8},{12,... | collective-permute-start | bytes 147464 | tf_op jit(solution)/shard_map/ppermute | solution.py:330
  75.2 3.0 %collective-permute-done.29.refs_1_ = bf16[3,32,128]{2,1,0:T(8,128)(2,1)S(1)} collective-permute-done((bf16[3,32,128]{2,1,0:T(8,128)(2,1)S(1)}, bf16[3,32,128]{2,1,0:T(8,128)(2,1)S(1)}, u32[]{:S(2)}, u32[]{:S(2)}) %collective-permute-start.29) | collective-permute-done | bytes 24608 | tf_op jit(solution)/shard_map/ppermute | solution.py:330
  (82 shorter events, 19.7 us)
Async XLA Ops:
  6.3 12.2 %collective-permute-start.3 = (bf16[256,512]{1,0:T(8,128)(2,1)}, bf16[256,512]{1,0:T(8,128)(2,1)S(1)}, u32[]{:S(2)}, u32[]{:S(2)}) collective-permute-start(bf16[256,512]{1,0:T(8,128)(2,1)} %get-tuple-element.49), channel_id=1, source_target_pairs={{0,1},{1,0},{2,3},{3,2},{4,5},{5,4},{6,7},{7,6},{8,9},{9,8},{10,11... | collective-permute-start | bytes 786440 | tf_op jit(solution)/shard_map/ppermute | solution.py:330
  9.3 7.8 %collective-permute-start = (bf16[128,256]{1,0:T(8,128)(2,1)S(1)}, bf16[128,256]{1,0:T(8,128)(2,1)S(1)}, u32[]{:S(2)}, u32[]{:S(2)}) collective-permute-start(bf16[128,256]{1,0:T(8,128)(2,1)S(1)} %top_share.1.refs_1_), channel_id=1, source_target_pairs={{0,6},{2,4},{4,2},{6,0},{1,7},{3,5},{5,3},{7,1},{8,14},{10,12},{12... | collective-permute-start | bytes 196616 | tf_op jit(solution)/shard_map/ppermute | solution.py:330
  13.0 5.4 %collective-permute-start.1 = (bf16[128,256]{1,0:T(8,128)(2,1)S(1)}, bf16[128,256]{1,0:T(8,128)(2,1)S(1)}, u32[]{:S(2)}, u32[]{:S(2)}) collective-permute-start(bf16[128,256]{1,0:T(8,128)(2,1)S(1)} %top_share.1.refs_1_), channel_id=1, source_target_pairs={{0,4},{2,6},{4,0},{6,2},{1,5},{3,7},{5,1},{7,3},{8,12},{10,14},{12... | collective-permute-start | bytes 196616 | tf_op jit(solution)/shard_map/ppermute | solution.py:330
  13.0 5.4 %collective-permute-start.2 = (bf16[128,256]{1,0:T(8,128)(2,1)S(1)}, bf16[128,256]{1,0:T(8,128)(2,1)S(1)}, u32[]{:S(2)}, u32[]{:S(2)}) collective-permute-start(bf16[128,256]{1,0:T(8,128)(2,1)S(1)} %top_share.1.refs_1_), channel_id=1, source_target_pairs={{0,2},{2,0},{4,6},{6,4},{1,3},{3,1},{5,7},{7,5},{8,10},{10,8},{12,... | collective-permute-start | bytes 196616 | tf_op jit(solution)/shard_map/ppermute | solution.py:330
  18.5 13.5 %collective-permute-start.4 = (bf16[512,256]{1,0:T(8,128)(2,1)S(1)}, bf16[512,256]{1,0:T(8,128)(2,1)S(1)}, u32[]{:S(2)}, u32[]{:S(2)}) collective-permute-start(bf16[512,256]{1,0:T(8,128)(2,1)S(1)} %half_top.1.refs_0_), channel_id=1, source_target_pairs={{0,1},{1,0},{2,3},{3,2},{4,5},{5,4},{6,7},{7,6},{8,9},{9,8},{10,11... | collective-permute-start | bytes 786440 | tf_op jit(solution)/shard_map/ppermute | solution.py:330
  19.0 7.7 %collective-permute-start.5 = (bf16[64,512]{1,0:T(8,128)(2,1)S(1)}, bf16[64,512]{1,0:T(8,128)(2,1)S(1)}, u32[]{:S(2)}, u32[]{:S(2)}) collective-permute-start(bf16[64,512]{1,0:T(8,128)(2,1)S(1)} %get-tuple-element.51), channel_id=1, source_target_pairs={{0,6},{2,4},{4,2},{6,0},{1,7},{3,5},{5,3},{7,1},{8,14},{10,12},{12... | collective-permute-start | bytes 196616 | tf_op jit(solution)/shard_map/ppermute | solution.py:330
  21.7 5.8 %collective-permute-start.6 = (bf16[64,512]{1,0:T(8,128)(2,1)S(1)}, bf16[64,512]{1,0:T(8,128)(2,1)S(1)}, u32[]{:S(2)}, u32[]{:S(2)}) collective-permute-start(bf16[64,512]{1,0:T(8,128)(2,1)S(1)} %get-tuple-element.52), channel_id=1, source_target_pairs={{0,4},{2,6},{4,0},{6,2},{1,5},{3,7},{5,1},{7,3},{8,12},{10,14},{12... | collective-permute-start | bytes 196616 | tf_op jit(solution)/shard_map/ppermute | solution.py:330
  21.7 5.8 %collective-permute-start.7 = (bf16[64,512]{1,0:T(8,128)(2,1)S(1)}, bf16[64,512]{1,0:T(8,128)(2,1)S(1)}, u32[]{:S(2)}, u32[]{:S(2)}) collective-permute-start(bf16[64,512]{1,0:T(8,128)(2,1)S(1)} %get-tuple-element.53), channel_id=1, source_target_pairs={{0,2},{2,0},{4,6},{6,4},{1,3},{3,1},{5,7},{7,5},{8,10},{10,8},{12,... | collective-permute-start | bytes 196616 | tf_op jit(solution)/shard_map/ppermute | solution.py:330
  27.6 6.9 %collective-permute-start.8 = (bf16[64,512]{1,0:T(8,128)(2,1)S(1)}, bf16[64,512]{1,0:T(8,128)(2,1)S(1)}, u32[]{:S(2)}, u32[]{:S(2)}) collective-permute-start(bf16[64,512]{1,0:T(8,128)(2,1)S(1)} %mid_total.1.refs_2_.refs_0_), channel_id=1, source_target_pairs={{0,6},{2,4},{4,2},{6,0},{1,7},{3,5},{5,3},{7,1},{8,14},{10,12},{12... | collective-permute-start | bytes 196616 | tf_op jit(solution)/shard_map/ppermute | solution.py:330
  29.6 6.1 %collective-permute-start.9 = (bf16[64,512]{1,0:T(8,128)(2,1)S(1)}, bf16[64,512]{1,0:T(8,128)(2,1)S(1)}, u32[]{:S(2)}, u32[]{:S(2)}) collective-permute-start(bf16[64,512]{1,0:T(8,128)(2,1)S(1)} %mid_total.1.refs_2_.refs_0_), channel_id=1, source_target_pairs={{0,4},{2,6},{4,0},{6,2},{1,5},{3,7},{5,1},{7,3},{8,12},{10,14},{12... | collective-permute-start | bytes 196616 | tf_op jit(solution)/shard_map/ppermute | solution.py:330
  29.6 6.1 %collective-permute-start.10 = (bf16[64,512]{1,0:T(8,128)(2,1)S(1)}, bf16[64,512]{1,0:T(8,128)(2,1)S(1)}, u32[]{:S(2)}, u32[]{:S(2)}) collective-permute-start(bf16[64,512]{1,0:T(8,128)(2,1)S(1)} %mid_total.1.refs_2_.refs_0_), channel_id=1, source_target_pairs={{0,2},{2,0},{4,6},{6,4},{1,3},{3,1},{5,7},{7,5},{8,10},{10,8},{12,... | collective-permute-start | bytes 196616 | tf_op jit(solution)/shard_map/ppermute | solution.py:330
  37.5 6.0 %collective-permute-start.11 = (bf16[2,2,64,512]{3,2,1,0:T(8,128)(2,1)S(1)}, bf16[2,2,64,512]{3,2,1,0:T(8,128)(2,1)S(1)}, u32[]{:S(2)}, u32[]{:S(2)}) collective-permute-start(bf16[2,2,64,512]{3,2,1,0:T(8,128)(2,1)S(1)} %get-tuple-element.56), channel_id=1, source_target_pairs={{0,8},{8,0},{16,24},{24,16},{1,9},{9,1},{17,25},{25,17},{2,10},{10... | collective-permute-start | bytes 786440 | tf_op jit(solution)/shard_map/ppermute | solution.py:330
  37.6 5.9 %collective-permute-start.12 = (bf16[4,32,512]{2,1,0:T(8,128)(2,1)S(1)}, bf16[4,32,512]{2,1,0:T(8,128)(2,1)S(1)}, u32[]{:S(2)}, u32[]{:S(2)}) collective-permute-start(bf16[4,32,512]{2,1,0:T(8,128)(2,1)S(1)} %get-tuple-element.59), channel_id=1, source_target_pairs={{0,1},{1,0},{2,3},{3,2},{4,5},{5,4},{6,7},{7,6},{8,9},{9,8},{10,11... | collective-permute-start | bytes 393224 | tf_op jit(solution)/shard_map/ppermute | solution.py:330
  39.0 6.8 %collective-permute-start.19 = (bf16[2,128,128]{2,1,0:T(8,128)(2,1)S(1)}, bf16[2,128,128]{2,1,0:T(8,128)(2,1)S(1)}, u32[]{:S(2)}, u32[]{:S(2)}) collective-permute-start(bf16[2,128,128]{2,1,0:T(8,128)(2,1)S(1)} %apex_share.1.refs_1_), channel_id=1, source_target_pairs={{0,6},{2,4},{4,2},{6,0},{1,7},{3,5},{5,3},{7,1},{8,14},{10,12},{12... | collective-permute-start | bytes 196616 | tf_op jit(solution)/shard_map/ppermute | solution.py:330
  41.1 6.7 %collective-permute-start.20 = (bf16[2,128,128]{2,1,0:T(8,128)(2,1)S(1)}, bf16[2,128,128]{2,1,0:T(8,128)(2,1)S(1)}, u32[]{:S(2)}, u32[]{:S(2)}) collective-permute-start(bf16[2,128,128]{2,1,0:T(8,128)(2,1)S(1)} %apex_share.1.refs_1_), channel_id=1, source_target_pairs={{0,4},{2,6},{4,0},{6,2},{1,5},{3,7},{5,1},{7,3},{8,12},{10,14},{12... | collective-permute-start | bytes 196616 | tf_op jit(solution)/shard_map/ppermute | solution.py:330
  41.3 6.5 %collective-permute-start.21 = (bf16[2,128,128]{2,1,0:T(8,128)(2,1)S(1)}, bf16[2,128,128]{2,1,0:T(8,128)(2,1)S(1)}, u32[]{:S(2)}, u32[]{:S(2)}) collective-permute-start(bf16[2,128,128]{2,1,0:T(8,128)(2,1)S(1)} %apex_share.1.refs_1_), channel_id=1, source_target_pairs={{0,2},{2,0},{4,6},{6,4},{1,3},{3,1},{5,7},{7,5},{8,10},{10,8},{12,... | collective-permute-start | bytes 196616 | tf_op jit(solution)/shard_map/ppermute | solution.py:330
  47.9 9.2 %collective-permute-start.22 = (bf16[4,2,128,128]{3,2,1,0:T(8,128)(2,1)S(1)}, bf16[4,2,128,128]{3,2,1,0:T(8,128)(2,1)S(1)}, u32[]{:S(2)}, u32[]{:S(2)}) collective-permute-start(bf16[4,2,128,128]{3,2,1,0:T(8,128)(2,1)S(1)} %front_share.1.refs_0_), channel_id=1, source_target_pairs={{0,1},{1,0},{2,3},{3,2},{4,5},{5,4},{6,7},{7,6},{8,9},{9,8},{10,11... | collective-permute-start | bytes 786440 | tf_op jit(solution)/shard_map/ppermute | solution.py:330
  48.7 5.8 %collective-permute-start.13 = (bf16[128,128]{1,0:T(8,128)(2,1)S(1)}, bf16[128,128]{1,0:T(8,128)(2,1)S(1)}, u32[]{:S(2)}, u32[]{:S(2)}) collective-permute-start(bf16[128,128]{1,0:T(8,128)(2,1)S(1)} %get-tuple-element.61), channel_id=1, source_target_pairs={{0,6},{2,4},{4,2},{6,0},{1,7},{3,5},{5,3},{7,1},{8,14},{10,12},{12... | collective-permute-start | bytes 98312 | tf_op jit(solution)/shard_map/ppermute | solution.py:330
  50.8 4.8 %collective-permute-start.14 = (bf16[128,128]{1,0:T(8,128)(2,1)S(1)}, bf16[128,128]{1,0:T(8,128)(2,1)S(1)}, u32[]{:S(2)}, u32[]{:S(2)}) collective-permute-start(bf16[128,128]{1,0:T(8,128)(2,1)S(1)} %get-tuple-element.62), channel_id=1, source_target_pairs={{0,4},{2,6},{4,0},{6,2},{1,5},{3,7},{5,1},{7,3},{8,12},{10,14},{12... | collective-permute-start | bytes 98312 | tf_op jit(solution)/shard_map/ppermute | solution.py:330
  53.1 5.9 %collective-permute-start.16 = (bf16[2,2,32,512]{3,2,1,0:T(8,128)(2,1)S(1)}, bf16[2,2,32,512]{3,2,1,0:T(8,128)(2,1)S(1)}, u32[]{:S(2)}, u32[]{:S(2)}) collective-permute-start(bf16[2,2,32,512]{3,2,1,0:T(8,128)(2,1)S(1)} %get-tuple-element.57.refs_0_), channel_id=1, source_target_pairs={{0,1},{1,0},{2,3},{3,2},{4,5},{5,4},{6,7},{7,6},{8,9},{9,8},{10,11... | collective-permute-start | bytes 393224 | tf_op jit(solution)/shard_map/ppermute | solution.py:330
  61.2 5.5 %collective-permute-start.25 = (bf16[2,32,512]{2,1,0:T(8,128)(2,1)S(1)}, bf16[2,32,512]{2,1,0:T(8,128)(2,1)S(1)}, u32[]{:S(2)}, u32[]{:S(2)}) collective-permute-start(bf16[2,32,512]{2,1,0:T(8,128)(2,1)S(1)} %get-tuple-element.75), channel_id=1, source_target_pairs={{0,16},{8,24},{16,0},{24,8},{1,17},{9,25},{17,1},{25,9},{2,18},{10... | collective-permute-start | bytes 196616 | tf_op jit(solution)/shard_map/ppermute | solution.py:330
  66.7 6.4 %collective-permute-start.26 = (bf16[32,768]{1,0:T(8,128)(2,1)S(1)}, bf16[32,768]{1,0:T(8,128)(2,1)S(1)}, u32[]{:S(2)}, u32[]{:S(2)}) collective-permute-start(bf16[32,768]{1,0:T(8,128)(2,1)S(1)} %get-tuple-element.81), channel_id=1, source_target_pairs={{0,6},{2,4},{4,2},{6,0},{1,7},{3,5},{5,3},{7,1},{8,14},{10,12},{12... | collective-permute-start | bytes 147464 | tf_op jit(solution)/shard_map/ppermute | solution.py:330
  68.8 5.4 %collective-permute-start.27 = (bf16[32,768]{1,0:T(8,128)(2,1)S(1)}, bf16[32,768]{1,0:T(8,128)(2,1)S(1)}, u32[]{:S(2)}, u32[]{:S(2)}) collective-permute-start(bf16[32,768]{1,0:T(8,128)(2,1)S(1)} %get-tuple-element.82), channel_id=1, source_target_pairs={{0,4},{2,6},{4,0},{6,2},{1,5},{3,7},{5,1},{7,3},{8,12},{10,14},{12... | collective-permute-start | bytes 147464 | tf_op jit(solution)/shard_map/ppermute | solution.py:330
  68.8 5.4 %collective-permute-start.28 = (bf16[32,768]{1,0:T(8,128)(2,1)S(1)}, bf16[32,768]{1,0:T(8,128)(2,1)S(1)}, u32[]{:S(2)}, u32[]{:S(2)}) collective-permute-start(bf16[32,768]{1,0:T(8,128)(2,1)S(1)} %get-tuple-element.83), channel_id=1, source_target_pairs={{0,2},{2,0},{4,6},{6,4},{1,3},{3,1},{5,7},{7,5},{8,10},{10,8},{12,... | collective-permute-start | bytes 147464 | tf_op jit(solution)/shard_map/ppermute | solution.py:330
  (19 other events, 199.2 us)
